TPU v7x, 32 devices: a whole 2x2x4 slice. The times are simulated.
32 devices in a mesh: grp: 4 (over x, core), row: 8 (over z, y).
Axes of the slice: x: 2, y: 2, z: 4, core: 2. Of those that a mesh axis runs over, the one named last changes fastest.
Arguments:
- users: bfloat16 [4096, 512], P(('grp', 'row')), may hold values from -0.44921875 to 0.44921875
- items: bfloat16 [6144, 512], P('row'), may hold values from -0.8984375 to 0.8984375
- ratings: float32 [32, 16, 128, 128], P(('grp', 'row')), may hold values from 0.05 to 1
- pair_list: int32 [32, 16, 2], P(('grp', 'row')), may hold values from 0 to 15, as said below
- send_list: int32 [32, 8, 2], P(('grp', 'row')), may hold values from 0 to 5, as said below
- counts: int32 [32], P(('grp', 'row')), may hold values from 4 to 16
Outputs:
- new_users: float32 [4096, 512], P(('grp', 'row'))
- new_items: float32 [6144, 512], P('row')
Inputs may be any that keep to these rules, and one draw needn't show every extreme that they name: pair_list[d, i, 0] is below 1 and pair_list[d, i, 1] below 8 * 2; the first counts[d] pairs of a device are distinct. The 2 entries send_list[d, p, :] are distinct.
All inputs are finite; a program needn't handle non-finite values.
Results may differ from a plain program's by a relative error of at most 0.0027.
Values may be sent and summed in bfloat16 or wider, within the bound.
No kernel may reach another device: no remote copies, remote signals or barrier semaphores. Data moves between devices by JAX's collectives and lax.ppermute only.
A program may use at most 64 MiB of HBM per device.

v0:
```python
import math

import jax
import jax.numpy as jnp
from jax import lax
from jax.sharding import PartitionSpec as P

CONFIDENCE = 40.0
FULL = lax.Precision.HIGHEST


def shards(users, items, ratings, pair_list, send_list, counts):
    row_count = lax.axis_size("row")
    grp_n = lax.axis_size("grp")
    factor_width = users.shape[1]
    limit_count = send_list.shape[2]
    rating_block = ratings.shape[2]
    user_blocks = users.reshape(-1, rating_block, factor_width)
    item_blocks = items.reshape(-1, rating_block, factor_width)
    item_count = item_blocks.shape[0]
    user_count = user_blocks.shape[0]
    position_count = row_count * limit_count
    chosen = send_list[0].reshape(-1)
    outgoing = jnp.take(item_blocks, chosen, axis=0).reshape(
        row_count, limit_count, rating_block, factor_width
    )
    incoming_blocks = lax.all_to_all(outgoing, "row", split_axis=0, concat_axis=0, tiled=True)
    position_blocks = incoming_blocks.reshape(position_count, rating_block, factor_width)
    contract = (((0,), (0,)), ((), ()))
    item_part = lax.dot_general(items, items, contract, preferred_element_type=jnp.float32)
    user_part = lax.dot_general(users, users, contract, preferred_element_type=jnp.float32)
    item_gram, user_gram = (
        lax.psum(item_part.astype(jnp.bfloat16), "row").astype(jnp.float32),
        lax.psum(user_part.astype(jnp.bfloat16), "row").astype(jnp.float32),
    )
    user_idx = pair_list[0, :, 0]
    position_index = pair_list[0, :, 1]
    live_count = counts[0]
    rates = ratings[0]
    live = jnp.arange(rates.shape[0], dtype=jnp.int32) < live_count
    lefts = jnp.take(user_blocks, user_idx, axis=0)
    rights = jnp.take(position_blocks, position_index, axis=0)
    scores = jnp.einsum("obk,ock->obc", lefts, rights, preferred_element_type=jnp.float32)
    weighted = CONFIDENCE * rates
    errors = jnp.where(live[:, None, None], weighted * scores - 1.0 - weighted, 0.0).astype(
        jnp.bfloat16
    )
    user_mask = (jnp.arange(user_count, dtype=jnp.int32)[:, None] == user_idx[None, :]).astype(
        jnp.bfloat16
    )
    masked_errors = errors[None, :, :, :] * user_mask[:, :, None, None]
    user_acc = jnp.einsum(
        "uobc,ock->ubk", masked_errors, rights, preferred_element_type=jnp.float32
    )
    slot_terms = jnp.einsum("obc,obk->ock", errors, lefts, preferred_element_type=jnp.float32)
    position_onehot = (
        position_index[:, None] == jnp.arange(position_count, dtype=jnp.int32)[None, :]
    ).astype(jnp.float32)
    slot_sum = jnp.einsum("os,ock->sck", position_onehot, slot_terms, precision=FULL)
    reply_blocks = lax.all_to_all(
        slot_sum.astype(jnp.bfloat16).reshape(row_count, limit_count, rating_block, factor_width),
        "row",
        split_axis=0,
        concat_axis=0,
        tiled=True,
    )
    owner_hot = (chosen[:, None] == jnp.arange(item_count, dtype=jnp.int32)[None, :]).astype(
        jnp.bfloat16
    )
    item_resid = jnp.einsum(
        "si,sck->ick",
        owner_hot,
        reply_blocks.reshape(position_count, rating_block, factor_width),
        preferred_element_type=jnp.float32,
    )
    item_resid = item_resid.reshape(-1, factor_width)
    items_full = items.astype(jnp.float32)
    partial_grad = item_resid + jnp.dot(items_full, user_gram, precision=FULL)
    share = lax.psum_scatter(partial_grad, "grp", scatter_dimension=0, tiled=True)
    share_rows = share.shape[0]
    own_rows = lax.dynamic_slice_in_dim(
        items_full, lax.axis_index("grp") * share_rows, share_rows, 0
    )
    total_users = users.shape[0] * grp_n * row_count
    total_items = items.shape[0] * row_count
    new_share = own_rows - 8.0 / math.sqrt(total_users) * share
    new_items = lax.all_gather(new_share, "grp", axis=0, tiled=True)
    users_full = users.astype(jnp.float32)
    grad_users = jnp.dot(users_full, item_gram, precision=FULL) + user_acc.reshape(-1, factor_width)
    new_users = users_full - 4.0 / math.sqrt(total_items) * grad_users
    return (new_users, new_items)


def solution(mesh):
    in_specs = (
        P(("grp", "row"), None),
        P("row", None),
        P(("grp", "row"), None, None, None),
        P(("grp", "row"), None, None),
        P(("grp", "row"), None, None),
        P(("grp", "row")),
    )
    out_specs = (P(("grp", "row"), None), P("row", None))
    return jax.shard_map(shards, mesh=mesh, in_specs=in_specs, out_specs=out_specs, check_vma=False)
```

profile of v0, /device:TPU:0, one launch (start us, length us, event | category | flops | bytes accessed | tf_op | source)
XLA Modules:
  0.0 260.7 jit_solution(14796974979681030387)
XLA Ops:
  9.6 1.6 broadcast_select_fusion.1
  11.2 7.4 %all-to-all-start = ((bf16[8,2,128,512]{3,2,1,0:T(8,128)(2,1)}), bf16[8,2,128,512]{3,2,1,0:T(8,128)(2,1)S(1)}, u32[]{:S(2)}, u32[]{:S(2)}) async-start(bf16[8,2,128,512]{3,2,1,0:T(8,128)(2,1)} %broadcast_select_fusion.1), calls=%async_computation | async-start | bytes 4194304 | tf_op jit(solution)/shard_map/all_to_all | solution.py:27
  19.8 47.0 %all-to-all-done = bf16[8,2,128,512]{3,2,1,0:T(8,128)(2,1)S(1)} async-done(((bf16[8,2,128,512]{3,2,1,0:T(8,128)(2,1)}), bf16[8,2,128,512]{3,2,1,0:T(8,128)(2,1)S(1)}, u32[]{:S(2)}, u32[]{:S(2)}) %all-to-all-start) | async-done | bytes 2097184 | tf_op jit(solution)/shard_map/all_to_all | solution.py:27
  66.8 2.0 gather_fusion.1
  68.9 2.7 %fusion.23 = bf16[16,128,128]{2,1,0:T(8,128)(2,1)S(1)} fusion(pred[16]{0:T(512)(128)(4,1)S(1)} %get-tuple-element.12, bf16[128,512]{1,0:T(8,128)(2,1)S(1)} %copy-done.1, f32[1,16,128,128]{3,2,1,0:T(8,128)} %param.8, bf16[16,128,512]{2,1,0:T(8,128)(2,1)} %gather_fusion.1, pred[16]{0:T(512)(128)(4,1)} %get-tuple-element.11, pred[16]{0:T(512)(128)(4,1)} %get-tuple-element.13), kind=kOutput, calls=%fused_computation.20 | convolution fusion | flops 272105472 | bytes 3801136 | tf_op jit(solution)/shard_map/obk,ock->obc/dot_general | solution.py:43
  72.4 4.5 %fusion.8 = bf16[16,128,512]{2,0,1:T(8,128)(2,1)S(1)} fusion(f32[16,128,512]{2,1,0:T(8,128)S(1)} %fusion.2, s32[16]{0:T(128)S(1)} %slice_bitcast_fusion), kind=kOutput, calls=%fused_computation.12 | convolution fusion | flops 202375424 | bytes 6291520 | tf_op jit(solution)/shard_map/os,ock->sck/dot_general | solution.py:59
  76.9 2.2 reshape.157
  79.1 4.3 %copy.34 = bf16[8,2,128,512]{3,1,2,0:T(2,128)(2,1)} copy(bf16[8,2,128,512]{3,1,0,2:T(2,128)(2,1)} %reshape.157) | data formatting | bytes 4194304 | tf_op jit(solution)/shard_map/reshape | solution.py:61
  83.4 3.6 %all-to-all-start.1 = ((bf16[8,2,128,512]{3,1,2,0:T(2,128)(2,1)}), bf16[8,2,128,512]{3,1,2,0:T(2,128)(2,1)S(1)}, u32[]{:S(2)}, u32[]{:S(2)}) async-start(bf16[8,2,128,512]{3,1,2,0:T(2,128)(2,1)} %copy.34), calls=%async_computation.1 | async-start | bytes 4194304 | tf_op jit(solution)/shard_map/all_to_all | solution.py:60
  87.1 1.1 convolution_convert_fusion.1
  88.2 1.4 convolution_convert_fusion
  90.0 58.2 %all-to-all-done.1 = bf16[8,2,128,512]{3,1,2,0:T(2,128)(2,1)S(1)} async-done(((bf16[8,2,128,512]{3,1,2,0:T(2,128)(2,1)}), bf16[8,2,128,512]{3,1,2,0:T(2,128)(2,1)S(1)}, u32[]{:S(2)}, u32[]{:S(2)}) %all-to-all-start.1) | async-done | bytes 2097184 | tf_op jit(solution)/shard_map/all_to_all | solution.py:60
  148.3 3.7 %copy.35 = bf16[8,2,128,512]{3,1,0,2:T(2,128)(2,1)} copy(bf16[8,2,128,512]{3,1,2,0:T(2,128)(2,1)S(1)} %all-to-all-done.1) | data formatting | bytes 4194304 | tf_op jit(solution)/shard_map/all_to_all | solution.py:60
  152.0 2.7 %reshape.158 = bf16[16,128,512]{2,0,1:T(8,128)(2,1)S(1)} reshape(bf16[8,2,128,512]{3,1,0,2:T(2,128)(2,1)} %copy.35) | data formatting | bytes 4194304 | tf_op jit(solution)/shard_map/reshape | solution.py:73
  155.1 2.1 copy.36
  157.2 1.9 copy.37
  159.1 36.7 %all-reduce.3.cloned.1.call-done = (bf16[512,512]{1,0:T(8,128)(2,1)}, bf16[512,512]{1,0:T(8,128)(2,1)}) async-done(((bf16[512,512]{1,0:T(8,128)(2,1)}, bf16[512,512]{1,0:T(8,128)(2,1)}), (bf16[512,512]{1,0:T(8,128)(2,1)}, bf16[512,512]{1,0:T(8,128)(2,1)})) %all-reduce.3.cloned.1.call-update) | async-done | bytes 1048592 | tf_op jit(solution)/shard_map/psum | solution.py:33
  195.8 2.8 %bitcast_add_fusion = f32[768,512]{0,1:T(8,128)} fusion(f32[768,512]{0,1:T(8,128)S(1)} %copy.37, bf16[512,512]{1,0:T(8,128)(2,1)} %get-tuple-element.9, bf16[768,512]{1,0:T(8,128)(2,1)S(1)} %copy-done), kind=kOutput, calls=%fused_computation.13 | convolution fusion | flops 403046400 | bytes 4456448 | tf_op jit(solution)/shard_map/dot_general | solution.py:78
  198.6 3.0 %copy.43 = f32[768,512]{1,0:T(8,128)} copy(f32[768,512]{0,1:T(8,128)} %bitcast_add_fusion) | data formatting | bytes 3145728
  201.9 27.6 %reduce-scatter.4.cloned.1.call-done = f32[192,512]{1,0:T(8,128)} async-done(((f32[768,512]{1,0:T(8,128)}), f32[192,512]{1,0:T(8,128)}) %reduce-scatter.4.cloned.1.call-update) | async-done | bytes 393232
  229.5 1.2 copy.44
  231.9 2.7 %convolution_bitcast_fusion = f32[128,512]{0,1:T(8,128)S(1)} fusion(bf16[16,128,512]{2,1,0:T(8,128)(2,1)} %gather_fusion.1, pred[16]{0:T(512)(128)(4,1)S(1)} %copy-done.4, bf16[16,128,128]{2,1,0:T(8,128)(2,1)S(1)} %fusion.23, bf16[16]{0:T(256)(128)(2,1)S(1)} %get-tuple-element.10), kind=kOutput, calls=%fused_computation.21 | convolution fusion | flops 269746176 | bytes 2883632 | tf_op jit(solution)/shard_map/uobc,ock->ubk/dot_general | solution.py:52
  235.7 15.8 %all-gather.2.cloned.1.call-done = f32[768,512]{1,0:T(8,128)} async-done(((f32[192,512]{1,0:T(8,128)}), f32[768,512]{1,0:T(8,128)}) %all-gather.2.cloned.1.call-update) | async-done | bytes 1572880 | tf_op jit(solution)/shard_map/all_gather | solution.py:87
  251.5 2.7 %copy.54 = f32[768,512]{1,0:T(8,128)} copy(f32[768,512]{1,0:T(8,128)} %all-gather.2.cloned.1.call-done) | data formatting | bytes 3145728
  (37 shorter events, 7.1 us)
Async XLA Ops:
  7.2 1.7 copy-start
  11.2 8.1 %copy-start.3 = (s32[1,16,2]{1,2,0:T(2,128)S(1)}, s32[1,16,2]{1,2,0:T(2,128)}, u32[]{:S(2)}) copy-start(s32[1,16,2]{1,2,0:T(2,128)} %param.9) | copy-start | bytes 388
  11.2 55.7 %all-to-all-start = ((bf16[8,2,128,512]{3,2,1,0:T(8,128)(2,1)}), bf16[8,2,128,512]{3,2,1,0:T(8,128)(2,1)S(1)}, u32[]{:S(2)}, u32[]{:S(2)}) async-start(bf16[8,2,128,512]{3,2,1,0:T(8,128)(2,1)} %broadcast_select_fusion.1), calls=%async_computation | async-start | bytes 4194304 | tf_op jit(solution)/shard_map/all_to_all | solution.py:27
  66.8 2.0 copy-start.1
  83.4 64.8 %all-to-all-start.1 = ((bf16[8,2,128,512]{3,1,2,0:T(2,128)(2,1)}), bf16[8,2,128,512]{3,1,2,0:T(2,128)(2,1)S(1)}, u32[]{:S(2)}, u32[]{:S(2)}) async-start(bf16[8,2,128,512]{3,1,2,0:T(2,128)(2,1)} %copy.34), calls=%async_computation.1 | async-start | bytes 4194304 | tf_op jit(solution)/shard_map/all_to_all | solution.py:60
  87.1 108.7 %all-reduce.3.cloned.1.call-start = ((), (), s32[]{:S(2)}) async-start(), calls=%async_computation.5 | async-start | bytes 2097152 | tf_op jit(solution)/shard_map/psum | solution.py:33
  89.7 139.8 %reduce-scatter.4.cloned.1.call-start = ((), (), s32[]{:S(2)}) async-start(), calls=%async_computation.4 | async-start | bytes 1966080
  201.7 49.9 %all-gather.2.cloned.1.call-start = ((), (), s32[]{:S(2)}) async-start(), calls=%async_computation.3 | async-start | bytes 1966080 | tf_op jit(solution)/shard_map/all_gather | solution.py:87
  201.8 30.1 %copy-start.4 = (pred[16]{0:T(512)(128)(4,1)S(1)}, pred[16]{0:T(512)(128)(4,1)}, u32[]{:S(2)}) copy-start(pred[16]{0:T(512)(128)(4,1)} %get-tuple-element.11) | copy-start | bytes 52
  231.8 2.7 %copy-start.2 = (bf16[512,512]{1,0:T(8,128)(2,1)S(1)}, bf16[512,512]{1,0:T(8,128)(2,1)}, u32[]{:S(2)}) copy-start(bf16[512,512]{1,0:T(8,128)(2,1)} %get-tuple-element.8) | copy-start | bytes 1572868
Sparse Core Ops, SparseCore 0:
  91.5 104.3 all-reduce.2
  201.8 27.6 reduce-scatter.3
  231.8 19.6 all-gather.1
where the time goes:
time: 261 us
  waiting for transfers between devices  185 us (71%)
  local copies, waits for them, and re-layouts  29.7 us (11%)
  matrix products  16.8 us (6%)
  between operations  14.6 us (6%)
  starting transfers between devices  11.4 us (4%)
  other arithmetic  2.92 us (1%)
    all_to_all x1, waiting for transfers between devices, shards(): lax.all_to_all(slot_sum.astype(jnp.bfloat16).reshape(row_count, limit_cou...  58.2 us
    all_to_all x1, waiting for transfers between devices, shards(): lax.all_to_all(outgoing, 'row', split_axis=0, concat_axis=0, tiled=True)  47 us
    psum x1, waiting for transfers between devices, shards(): lax.psum(item_part.astype(jnp.bfloat16), 'row').astype(jnp.float32)  36.7 us
    unnamed x4, waiting for transfers between devices  27.6 us
    all_gather x1, waiting for transfers between devices, shards(): new_items = lax.all_gather(new_share, 'grp', axis=0, tiled=True)  15.8 us
    unnamed x17, local copies, waits for them, and re-layouts  8.84 us
    all_to_all x1, starting transfers between devices, shards(): lax.all_to_all(outgoing, 'row', split_axis=0, concat_axis=0, tiled=True)  7.41 us
    reshape x2, local copies, waits for them, and re-layouts, shards(): slot_sum.astype(jnp.bfloat16)  6.58 us
  transfers between devices with their start and end apart: 5, of which 5 were waited for; matrix products, arithmetic and copies ran while one was open for 7% of the time, Pallas kernels for 0%

commit v1 on v0

v1 whole, which is shorter than its diff:
```python
import functools
import math

import jax
import jax.numpy as jnp
from jax import lax
from jax.experimental import pallas as pl
from jax.experimental.pallas import tpu as pltpu
from jax.sharding import PartitionSpec as P

CONFIDENCE = 40.0
STEPS = 65535.0
OFFSET = 32768
BF = jnp.bfloat16
F32 = jnp.float32

VM = pl.BlockSpec(memory_space=pltpu.VMEM)
SM = pl.BlockSpec(memory_space=pltpu.SMEM)
ROWS = (((1,), (1,)), ((), ()))
COLS = (((0,), (0,)), ((), ()))


def call(body, outs, in_specs, flops, moved, scratch=(), mib=24):
    return pl.pallas_call(
        body,
        out_shape=outs,
        in_specs=in_specs,
        out_specs=jax.tree.map(lambda _: VM, outs),
        scratch_shapes=scratch,
        compiler_params=pltpu.CompilerParams(vmem_limit_bytes=mib << 20),
        cost_estimate=pl.CostEstimate(flops=flops, bytes_accessed=moved, transcendentals=0),
    )


def spread_body(n, limit, pair_ref, count_ref, rate_ref, *rest):
    outs, where = rest[:n], rest[n]
    me = lax.axis_index("row")
    width = rate_ref.shape[1]
    for s in range(n * limit):
        where[s] = -1
    for i in range(rate_ref.shape[0]):
        @pl.when(i < count_ref[0])
        def _():
            where[pair_ref[1, i]] = i
    for k in range(n):
        for c in range(limit):
            i = where[(me ^ k) * limit + c]
            rate = rate_ref[jnp.maximum(i, 0)]
            code = jnp.where(i >= 0, (rate * STEPS + 0.5).astype(jnp.int32), 0) - OFFSET
            outs[k][c * width : (c + 1) * width] = code.astype(jnp.int16)


def gram_body(item_ref, gram_ref):
    items = item_ref[...]
    gram_ref[...] = lax.dot_general(items, items, COLS, preferred_element_type=F32).astype(BF)


def score_body(n, limit, width, send_ref, item_ref, gram_ref, *rest):
    users, (score_ref, user_ref, part_ref) = rest[:n], rest[n:]
    me = lax.axis_index("row")
    gram = gram_ref[...]
    total = None
    for k in range(n):
        left = users[k][...]
        for c in range(limit):
            at = pl.multiple_of(send_ref[c, me ^ k] * width, width)
            score_ref[k * limit + c] = lax.dot_general(
                left, item_ref[pl.ds(at, width)], ROWS, preferred_element_type=F32
            )
        user_ref[k] = jnp.dot(left, gram, preferred_element_type=F32)
        term = lax.dot_general(left, left, COLS, preferred_element_type=F32)
        total = term if total is None else total + term
    part_ref[...] = jnp.dot(item_ref[...], total.astype(BF), preferred_element_type=F32)


def error_body(n, limit, width, send_ref, item_ref, score_ref, gram_user_ref, part_ref, *rest):
    users, codes, outs = rest[:n], rest[n : 2 * n], rest[2 * n : 3 * n]
    mine_ref, other_ref, sum_ref = rest[3 * n :]
    me = lax.axis_index("row")
    core = lax.axis_index("grp") % 2
    sum_ref[...] = part_ref[...]
    for k in range(n):
        left = users[k][...]
        total = gram_user_ref[k]
        for c in range(limit):
            at = pl.ds(pl.multiple_of(send_ref[c, me ^ k] * width, width), width)
            code = codes[k][c * width : (c + 1) * width].astype(jnp.int32) + OFFSET
            weighted = CONFIDENCE * (code.astype(F32) * (1.0 / STEPS))
            error = weighted * score_ref[k * limit + c] - 1.0 - weighted
            error = jnp.where(code > 0, error, 0.0).astype(BF)
            total += jnp.dot(error, item_ref[at], preferred_element_type=F32)
            term = lax.dot_general(error, left, COLS, preferred_element_type=F32)
            sum_ref[at] += term.astype(BF).astype(F32)
        outs[k][...] = total.astype(outs[k].dtype)
    half = mine_ref.shape[0]
    mine_ref[...] = sum_ref[pl.ds(pl.multiple_of(core * half, half), half)]
    other_ref[...] = sum_ref[pl.ds(pl.multiple_of((1 - core) * half, half), half)].astype(BF)


def swap(x, axis, k):
    return lax.ppermute(x, axis, [(i, i ^ k) for i in range(lax.axis_size(axis))])


def shards(users, items, ratings, pair_list, send_list, counts):
    n = lax.axis_size("row")
    grp_n = lax.axis_size("grp")
    width = ratings.shape[2]
    factors = users.shape[1]
    limit = send_list.shape[2]
    item_rows = items.shape[0]
    user_rows = users.shape[0]
    far = n // 2
    total_users = user_rows * grp_n * n
    total_items = item_rows * n
    sds = jax.ShapeDtypeStruct

    pairs = jnp.swapaxes(pair_list[0], 0, 1)
    sends = jnp.swapaxes(send_list[0], 0, 1)

    over = swap(users, "row", far)
    blocks = [users] + [swap(users, "row", k) for k in range(1, far)]
    blocks += [over] + [swap(over, "row", k) for k in range(1, far)]

    codes = call(
        functools.partial(spread_body, n, limit),
        [sds((limit * width, width), jnp.int16)] * n,
        [SM, SM, VM],
        0,
        ratings.size * 6,
        [pltpu.SMEM((n * limit,), jnp.int32)],
    )(pairs, counts, ratings[0])
    codes = [codes[0]] + [swap(codes[k], "row", k) for k in range(1, n)]

    gram = call(
        gram_body, sds((factors, factors), BF), [VM], 2 * item_rows * factors**2, items.size * 2
    )(items)
    scores, user_gram, item_part = call(
        functools.partial(score_body, n, limit, width),
        [
            sds((n * limit, user_rows, width), F32),
            sds((n, user_rows, factors), F32),
            sds((item_rows, factors), F32),
        ],
        [SM, VM, VM] + [VM] * n,
        2 * n * user_rows * factors * (limit * width + 2 * factors) + 2 * item_rows * factors**2,
        8 << 20,
    )(sends, items, gram, *blocks)
    half = item_rows // 2
    *parts, mine, other = call(
        functools.partial(error_body, n, limit, width),
        [sds((user_rows, factors), F32 if k in (0, far) else BF) for k in range(n)]
        + [sds((half, factors), F32), sds((half, factors), BF)],
        [SM, VM, VM, VM, VM] + [VM] * (2 * n),
        4 * n * limit * user_rows * factors * width,
        8 << 20,
        [pltpu.VMEM((item_rows, factors), F32)],
    )(sends, items, scores, user_gram, item_part, *blocks, *codes)

    across = parts[far]
    for k in range(1, far):
        across += swap(parts[far + k], "row", k).astype(F32)
    user_sum = parts[0]
    for k in range(1, far):
        user_sum += swap(parts[k], "row", k).astype(F32)
    user_sum += swap(across.astype(BF), "row", far).astype(F32)
    new_users = users.astype(F32) - 4.0 / math.sqrt(total_items) * user_sum

    core = lax.axis_index("grp") % 2
    pair_sum = mine + swap(other, "grp", 1).astype(F32)
    if grp_n == 4:
        here = pair_sum.astype(BF)
        there = swap(here, "grp", 2)
        first = here.astype(F32) + there.astype(F32)
        second = swap(here, "grp", 1).astype(F32) + swap(there, "grp", 1).astype(F32)
    else:
        peers = [list(range(c, grp_n, 2)) for c in range(2)]
        first = lax.psum(pair_sum, "grp", axis_index_groups=peers)
        second = swap(first, "grp", 1)
    item_sum = jnp.where(
        core == 0, jnp.concatenate([first, second]), jnp.concatenate([second, first])
    )
    new_items = items.astype(F32) - 8.0 / math.sqrt(total_users) * item_sum
    return (new_users, new_items)


def solution(mesh):
    in_specs = (
        P(("grp", "row"), None),
        P("row", None),
        P(("grp", "row"), None, None, None),
        P(("grp", "row"), None, None),
        P(("grp", "row"), None, None),
        P(("grp", "row")),
    )
    out_specs = (P(("grp", "row"), None), P("row", None))
    return jax.shard_map(shards, mesh=mesh, in_specs=in_specs, out_specs=out_specs, check_vma=False)
```

time: 261 us -> 59.7 us (0.23)
  waiting for transfers between devices: 185 us -> 7.53 us
  local copies, waits for them, and re-layouts: 29.7 us -> 3.92 us
  starting transfers between devices: 11.4 us -> 36.7 us
  matrix products: 16.8 us -> 0 us
  between operations: 14.6 us -> 1.45 us
  Pallas kernels: 0 us -> 6.92 us
    all_to_all x2 -> x0, waiting for transfers between devices: 105 us -> none  [the longest x1 58.2 us: shards(): lax.all_to_all(slot_sum.astype(jnp.bfloat16).reshape(row_count, limit_cou...]
    psum x1 -> x0, waiting for transfers between devices: 36.7 us -> none  [shards(): lax.psum(item_part.astype(jnp.bfloat16), 'row').astype(jnp.float32)]
    ppermute x0 -> x25, starting transfers between devices: none -> 36.7 us  [swap(): lax.ppermute(x, axis, [(i, i ^ k) for i in range(lax.axis_size(axis))])]
    unnamed x4 -> x0, waiting for transfers between devices: 27.6 us -> none
    dot_general x9 -> x0, matrix products: 16.8 us -> none  [the longest x1 4.49 us: shards(): jnp.einsum('os,ock->sck', position_onehot, slot_terms, precision=FULL)]
    all_gather x1 -> x0, waiting for transfers between devices: 15.8 us -> none  [shards(): new_items = lax.all_gather(new_share, 'grp', axis=0, tiled=True)]
    reshape x4 -> x0, local copies, waits for them, and re-layouts: 11.2 us -> none  [the longest x2 6.58 us: shards(): slot_sum.astype(jnp.bfloat16)]
    all_to_all x2 -> x0, starting transfers between devices: 11.1 us -> none  [the longest x1 7.41 us: shards(): lax.all_to_all(outgoing, 'row', split_axis=0, concat_axis=0, tiled=True)]
  transfers between devices with their start and end apart: 5 -> 25, of which waited for: 5 -> 4; matrix products, arithmetic and copies ran while one was open for 7% -> 2% of each run, Pallas kernels for 0% -> 8%
where the time goes in v1:
time: 59.7 us; the launch traced here: 59.2 us
  starting transfers between devices  36.7 us (61%)
  waiting for transfers between devices  7.53 us (13%)
  Pallas kernels  6.92 us (12%)
  local copies, waits for them, and re-layouts  3.92 us (7%)
  other arithmetic  2.71 us (5%)
  between operations  1.45 us (2%)
    ppermute x25, starting transfers between devices, swap(): lax.ppermute(x, axis, [(i, i ^ k) for i in range(lax.axis_size(axis))])  36.7 us
    ppermute x25, waiting for transfers between devices, swap(): lax.ppermute(x, axis, [(i, i ^ k) for i in range(lax.axis_size(axis))])  7.53 us
    unnamed x12, local copies, waits for them, and re-layouts  3.92 us
    pallas_call x1, Pallas kernels, shards(): call(functools.partial(score_body, n, limit, width), [sds((n * limit, use...  3.39 us
    pallas_call x1, Pallas kernels, shards(): call(functools.partial(error_body, n, limit, width), [sds((user_rows, fac...  2.09 us
    sub x1, other arithmetic, shards(): new_items = items.astype(F32) - 8.0 / math.sqrt(total_users) * item_sum  1.48 us
  transfers between devices with their start and end apart: 25, of which 4 were waited for; matrix products, arithmetic and copies ran while one was open for 2% of the time, Pallas kernels for 8%

profile of v1, /device:TPU:0, one launch (start us, length us, event | category | flops | bytes accessed | tf_op | source)
XLA Modules:
  0.0 59.2 jit_solution(14815618083249801466)
XLA Ops:
  0.6 4.1 %collective-permute-start.3 = (bf16[128,512]{1,0:T(8,128)(2,1)}, bf16[128,512]{1,0:T(8,128)(2,1)S(1)}, u32[]{:S(2)}, u32[]{:S(2)}) collective-permute-start(bf16[128,512]{1,0:T(8,128)(2,1)} %rest_0_.3), channel_id=1, source_target_pairs={{0,4},{1,5},{2,6},{3,7},{4,0},{5,1},{6,2},{7,3},{8,12},{9,13},{10,... | collective-permute-start | bytes 393224 | tf_op jit(solution)/shard_map/ppermute | solution.py:101
  4.7 1.5 %collective-permute-start = (bf16[128,512]{1,0:T(8,128)(2,1)}, bf16[128,512]{1,0:T(8,128)(2,1)S(1)}, u32[]{:S(2)}, u32[]{:S(2)}) collective-permute-start(bf16[128,512]{1,0:T(8,128)(2,1)} %rest_0_.3), channel_id=1, source_target_pairs={{0,1},{1,0},{2,3},{3,2},{4,5},{5,4},{6,7},{7,6},{8,9},{9,8},{10,11... | collective-permute-start | bytes 393224 | tf_op jit(solution)/shard_map/ppermute | solution.py:101
  6.9 1.2 %copy-done.2 = f32[1,16,128,128]{3,2,1,0:T(8,128)S(1)} copy-done((f32[1,16,128,128]{3,2,1,0:T(8,128)S(1)}, f32[1,16,128,128]{3,2,1,0:T(8,128)}, u32[]{:S(2)}) %copy-start.2) | copy-done | bytes 1048600
  10.1 2.5 %collective-permute-start.11 = (s16[256,128]{1,0:T(8,128)(2,1)S(1)}, s16[256,128]{1,0:T(8,128)(2,1)S(1)}, u32[]{:S(2)}, u32[]{:S(2)}) collective-permute-start(s16[256,128]{1,0:T(8,128)(2,1)S(1)} %get-tuple-element.31), channel_id=1, source_target_pairs={{0,5},{1,4},{2,7},{3,6},{4,1},{5,0},{6,3},{7,2},{8,13},{9,12},{10,... | collective-permute-start | bytes 196616 | tf_op jit(solution)/shard_map/ppermute | solution.py:101
  12.6 1.6 %collective-permute-start.1 = (bf16[128,512]{1,0:T(8,128)(2,1)}, bf16[128,512]{1,0:T(8,128)(2,1)S(1)}, u32[]{:S(2)}, u32[]{:S(2)}) collective-permute-start(bf16[128,512]{1,0:T(8,128)(2,1)} %rest_0_.3), channel_id=1, source_target_pairs={{0,2},{1,3},{2,0},{3,1},{4,6},{5,7},{6,4},{7,5},{8,10},{9,11},{10,... | collective-permute-start | bytes 393224 | tf_op jit(solution)/shard_map/ppermute | solution.py:101
  14.2 2.6 %collective-permute-done.10.rest_12_ = s16[256,128]{1,0:T(8,128)(2,1)S(1)} collective-permute-done((s16[256,128]{1,0:T(8,128)(2,1)S(1)}, s16[256,128]{1,0:T(8,128)(2,1)S(1)}, u32[]{:S(2)}, u32[]{:S(2)}) %collective-permute-start.10) | collective-permute-done | bytes 65568 | tf_op jit(solution)/shard_map/ppermute | solution.py:101
  17.1 1.6 %collective-permute-start.4 = (bf16[128,512]{1,0:T(8,128)(2,1)S(1)}, bf16[128,512]{1,0:T(8,128)(2,1)S(1)}, u32[]{:S(2)}, u32[]{:S(2)}) collective-permute-start(bf16[128,512]{1,0:T(8,128)(2,1)S(1)} %collective-permute-done.3.rest_4_), channel_id=1, source_target_pairs={{0,1},{1,0},{2,3},{3,2},{4,5},{5,4},{6,7},{7,6},{8,9},{9,8},{10,11... | collective-permute-start | bytes 393224 | tf_op jit(solution)/shard_map/ppermute | solution.py:101
  18.7 1.5 %collective-permute-start.5 = (bf16[128,512]{1,0:T(8,128)(2,1)S(1)}, bf16[128,512]{1,0:T(8,128)(2,1)S(1)}, u32[]{:S(2)}, u32[]{:S(2)}) collective-permute-start(bf16[128,512]{1,0:T(8,128)(2,1)S(1)} %collective-permute-done.3.rest_4_), channel_id=1, source_target_pairs={{0,2},{1,3},{2,0},{3,1},{4,6},{5,7},{6,4},{7,5},{8,10},{9,11},{10,... | collective-permute-start | bytes 393224 | tf_op jit(solution)/shard_map/ppermute | solution.py:101
  21.1 1.1 %copy-done = bf16[768,512]{1,0:T(8,128)(2,1)S(1)} copy-done((bf16[768,512]{1,0:T(8,128)(2,1)S(1)}, bf16[768,512]{1,0:T(8,128)(2,1)}, u32[]{:S(2)}) %copy-start) | copy-done | bytes 786456
  22.8 2.5 %collective-permute-start.12 = (s16[256,128]{1,0:T(8,128)(2,1)S(1)}, s16[256,128]{1,0:T(8,128)(2,1)S(1)}, u32[]{:S(2)}, u32[]{:S(2)}) collective-permute-start(s16[256,128]{1,0:T(8,128)(2,1)S(1)} %get-tuple-element.32), channel_id=1, source_target_pairs={{0,6},{1,7},{2,4},{3,5},{4,2},{5,3},{6,0},{7,1},{8,14},{9,15},{10,... | collective-permute-start | bytes 196616 | tf_op jit(solution)/shard_map/ppermute | solution.py:101
  25.3 2.1 %collective-permute-start.13 = (s16[256,128]{1,0:T(8,128)(2,1)S(1)}, s16[256,128]{1,0:T(8,128)(2,1)S(1)}, u32[]{:S(2)}, u32[]{:S(2)}) collective-permute-start(s16[256,128]{1,0:T(8,128)(2,1)S(1)} %get-tuple-element.33), channel_id=1, source_target_pairs={{0,7},{1,6},{2,5},{3,4},{4,3},{5,2},{6,1},{7,0},{8,15},{9,14},{10,... | collective-permute-start | bytes 196616 | tf_op jit(solution)/shard_map/ppermute | solution.py:101
  28.5 2.5 %collective-permute-start.9 = (s16[256,128]{1,0:T(8,128)(2,1)S(1)}, s16[256,128]{1,0:T(8,128)(2,1)S(1)}, u32[]{:S(2)}, u32[]{:S(2)}) collective-permute-start(s16[256,128]{1,0:T(8,128)(2,1)S(1)} %get-tuple-element.29), channel_id=1, source_target_pairs={{0,3},{1,2},{2,1},{3,0},{4,7},{5,6},{6,5},{7,4},{8,11},{9,10},{10,... | collective-permute-start | bytes 196616 | tf_op jit(solution)/shard_map/ppermute | solution.py:101
  31.0 3.4 %shard_map.78 = (f32[16,128,128]{2,1,0:T(8,128)S(1)}, f32[8,128,512]{2,1,0:T(8,128)S(1)}, f32[768,512]{1,0:T(8,128)S(1)}) custom-call(s32[2,8]{1,0:T(2,128)S(1)} %bitcast.9, bf16[768,512]{1,0:T(8,128)(2,1)S(1)} %copy-done, bf16[512,512]{1,0:T(8,128)(2,1)S(1)} %shard_map.77.gram_ref, bf16[128,512]{1,0:T(8,128)(2,1)S(1)} %copy-done.3, ...), custom_call_target="tpu_custom_call" | custom-call | flops 1744830464 | bytes 8388608 | tf_op jit(solution)/shard_map/pallas_call | solution.py:137
  34.4 2.1 %shard_map.80 = (f32[128,512]{1,0:T(8,128)S(1)}, bf16[128,512]{1,0:T(8,128)(2,1)S(1)}, bf16[128,512]{1,0:T(8,128)(2,1)S(1)}, bf16[128,512]{1,0:T(8,128)(2,1)S(1)...) custom-call(s32[2,8]{1,0:T(2,128)S(1)} %bitcast.10, ...), custom_call_target="tpu_custom_call" | custom-call | flops 536870912 | bytes 8388608 | tf_op jit(solution)/shard_map/pallas_call | solution.py:149
  37.4 1.4 %collective-permute-start.18 = (bf16[128,512]{1,0:T(8,128)(2,1)S(1)}, bf16[128,512]{1,0:T(8,128)(2,1)S(1)}, u32[]{:S(2)}, u32[]{:S(2)}) collective-permute-start(bf16[128,512]{1,0:T(8,128)(2,1)S(1)} %get-tuple-element.40), channel_id=1, source_target_pairs={{0,2},{1,3},{2,0},{3,1},{4,6},{5,7},{6,4},{7,5},{8,10},{9,11},{10,... | collective-permute-start | bytes 393224 | tf_op jit(solution)/shard_map/ppermute | solution.py:101
  38.9 1.3 %collective-permute-start.19 = (bf16[128,512]{1,0:T(8,128)(2,1)S(1)}, bf16[128,512]{1,0:T(8,128)(2,1)S(1)}, u32[]{:S(2)}, u32[]{:S(2)}) collective-permute-start(bf16[128,512]{1,0:T(8,128)(2,1)S(1)} %get-tuple-element.41), channel_id=1, source_target_pairs={{0,3},{1,2},{2,1},{3,0},{4,7},{5,6},{6,5},{7,4},{8,11},{9,10},{10,... | collective-permute-start | bytes 393224 | tf_op jit(solution)/shard_map/ppermute | solution.py:101
  40.3 1.5 %collective-permute-start.22 = (bf16[384,512]{1,0:T(8,128)(2,1)S(1)}, bf16[384,512]{1,0:T(8,128)(2,1)S(1)}, u32[]{:S(2)}, u32[]{:S(2)}) collective-permute-start(bf16[384,512]{1,0:T(8,128)(2,1)S(1)} %add_convert_fusion), channel_id=1, source_target_pairs={{0,16},{8,24},{16,0},{24,8},{1,17},{9,25},{17,1},{25,9},{2,18},{10... | collective-permute-start | bytes 1179656 | tf_op jit(solution)/shard_map/ppermute | solution.py:101
  42.6 1.5 %collective-permute-start.15 = (bf16[128,512]{1,0:T(8,128)(2,1)S(1)}, bf16[128,512]{1,0:T(8,128)(2,1)S(1)}, u32[]{:S(2)}, u32[]{:S(2)}) collective-permute-start(bf16[128,512]{1,0:T(8,128)(2,1)S(1)} %get-tuple-element.36), channel_id=1, source_target_pairs={{0,2},{1,3},{2,0},{3,1},{4,6},{5,7},{6,4},{7,5},{8,10},{9,11},{10,... | collective-permute-start | bytes 393224 | tf_op jit(solution)/shard_map/ppermute | solution.py:101
  44.1 1.3 %collective-permute-start.16 = (bf16[128,512]{1,0:T(8,128)(2,1)S(1)}, bf16[128,512]{1,0:T(8,128)(2,1)S(1)}, u32[]{:S(2)}, u32[]{:S(2)}) collective-permute-start(bf16[128,512]{1,0:T(8,128)(2,1)S(1)} %get-tuple-element.37), channel_id=1, source_target_pairs={{0,3},{1,2},{2,1},{3,0},{4,7},{5,6},{6,5},{7,4},{8,11},{9,10},{10,... | collective-permute-start | bytes 393224 | tf_op jit(solution)/shard_map/ppermute | solution.py:101
  45.4 1.9 %collective-permute-done.19 = bf16[128,512]{1,0:T(8,128)(2,1)S(1)} collective-permute-done((bf16[128,512]{1,0:T(8,128)(2,1)S(1)}, bf16[128,512]{1,0:T(8,128)(2,1)S(1)}, u32[]{:S(2)}, u32[]{:S(2)}) %collective-permute-start.19) | collective-permute-done | bytes 131104 | tf_op jit(solution)/shard_map/ppermute | solution.py:101
  47.4 5.1 %collective-permute-start.20 = (bf16[128,512]{1,0:T(8,128)(2,1)S(1)}, bf16[128,512]{1,0:T(8,128)(2,1)S(1)}, u32[]{:S(2)}, u32[]{:S(2)}) collective-permute-start(bf16[128,512]{1,0:T(8,128)(2,1)S(1)} %add_convert_fusion.1), channel_id=1, source_target_pairs={{0,4},{1,5},{2,6},{3,7},{4,0},{5,1},{6,2},{7,3},{8,12},{9,13},{10,... | collective-permute-start | bytes 393224 | tf_op jit(solution)/shard_map/ppermute | solution.py:101
  53.0 2.8 %collective-permute-done.20 = bf16[128,512]{1,0:T(8,128)(2,1)S(1)} collective-permute-done((bf16[128,512]{1,0:T(8,128)(2,1)S(1)}, bf16[128,512]{1,0:T(8,128)(2,1)S(1)}, u32[]{:S(2)}, u32[]{:S(2)}) %collective-permute-start.20) | collective-permute-done | bytes 131104 | tf_op jit(solution)/shard_map/ppermute | solution.py:101
  56.8 0.9 %copy-done.1 = bf16[768,512]{1,0:T(8,128)(2,1)S(1)} copy-done((bf16[768,512]{1,0:T(8,128)(2,1)S(1)}, bf16[768,512]{1,0:T(8,128)(2,1)}, u32[]{:S(2)}) %copy-start.1) | copy-done | bytes 786456
  57.7 1.5 %fusion.1 = f32[768,512]{1,0:T(8,128)} fusion(f32[384,512]{1,0:T(8,128)S(1)} %convert_add_fusion, f32[384,512]{1,0:T(8,128)S(1)} %convert_add_fusion.1, bf16[768,512]{1,0:T(8,128)(2,1)S(1)} %copy-done.1, pred[]{:T(512)S(6)} %eq.5), kind=kLoop, calls=%fused_computation.2 | loop fusion | flops 2359296 | bytes 3932161 | tf_op jit(solution)/shard_map/sub | solution.py:182
  (48 shorter events, 8.2 us)
Async XLA Ops:
  0.6 16.4 %collective-permute-start.3 = (bf16[128,512]{1,0:T(8,128)(2,1)}, bf16[128,512]{1,0:T(8,128)(2,1)S(1)}, u32[]{:S(2)}, u32[]{:S(2)}) collective-permute-start(bf16[128,512]{1,0:T(8,128)(2,1)} %rest_0_.3), channel_id=1, source_target_pairs={{0,4},{1,5},{2,6},{3,7},{4,0},{5,1},{6,2},{7,3},{8,12},{9,13},{10,... | collective-permute-start | bytes 393224 | tf_op jit(solution)/shard_map/ppermute | solution.py:101
  4.7 15.5 %collective-permute-start = (bf16[128,512]{1,0:T(8,128)(2,1)}, bf16[128,512]{1,0:T(8,128)(2,1)S(1)}, u32[]{:S(2)}, u32[]{:S(2)}) collective-permute-start(bf16[128,512]{1,0:T(8,128)(2,1)} %rest_0_.3), channel_id=1, source_target_pairs={{0,1},{1,0},{2,3},{3,2},{4,5},{5,4},{6,7},{7,6},{8,9},{9,8},{10,11... | collective-permute-start | bytes 393224 | tf_op jit(solution)/shard_map/ppermute | solution.py:101
  9.7 7.1 %collective-permute-start.10 = (s16[256,128]{1,0:T(8,128)(2,1)S(1)}, s16[256,128]{1,0:T(8,128)(2,1)S(1)}, u32[]{:S(2)}, u32[]{:S(2)}) collective-permute-start(s16[256,128]{1,0:T(8,128)(2,1)S(1)} %get-tuple-element.30), channel_id=1, source_target_pairs={{0,4},{1,5},{2,6},{3,7},{4,0},{5,1},{6,2},{7,3},{8,12},{9,13},{10,... | collective-permute-start | bytes 196616 | tf_op jit(solution)/shard_map/ppermute | solution.py:101
  10.1 8.6 %collective-permute-start.11 = (s16[256,128]{1,0:T(8,128)(2,1)S(1)}, s16[256,128]{1,0:T(8,128)(2,1)S(1)}, u32[]{:S(2)}, u32[]{:S(2)}) collective-permute-start(s16[256,128]{1,0:T(8,128)(2,1)S(1)} %get-tuple-element.31), channel_id=1, source_target_pairs={{0,5},{1,4},{2,7},{3,6},{4,1},{5,0},{6,3},{7,2},{8,13},{9,12},{10,... | collective-permute-start | bytes 196616 | tf_op jit(solution)/shard_map/ppermute | solution.py:101
  12.6 10.2 %collective-permute-start.1 = (bf16[128,512]{1,0:T(8,128)(2,1)}, bf16[128,512]{1,0:T(8,128)(2,1)S(1)}, u32[]{:S(2)}, u32[]{:S(2)}) collective-permute-start(bf16[128,512]{1,0:T(8,128)(2,1)} %rest_0_.3), channel_id=1, source_target_pairs={{0,2},{1,3},{2,0},{3,1},{4,6},{5,7},{6,4},{7,5},{8,10},{9,11},{10,... | collective-permute-start | bytes 393224 | tf_op jit(solution)/shard_map/ppermute | solution.py:101
  16.8 8.6 %collective-permute-start.2 = (bf16[128,512]{1,0:T(8,128)(2,1)}, bf16[128,512]{1,0:T(8,128)(2,1)S(1)}, u32[]{:S(2)}, u32[]{:S(2)}) collective-permute-start(bf16[128,512]{1,0:T(8,128)(2,1)} %rest_0_.3), channel_id=1, source_target_pairs={{0,3},{1,2},{2,1},{3,0},{4,7},{5,6},{6,5},{7,4},{8,11},{9,10},{10,... | collective-permute-start | bytes 393224 | tf_op jit(solution)/shard_map/ppermute | solution.py:101
  17.1 10.4 %collective-permute-start.4 = (bf16[128,512]{1,0:T(8,128)(2,1)S(1)}, bf16[128,512]{1,0:T(8,128)(2,1)S(1)}, u32[]{:S(2)}, u32[]{:S(2)}) collective-permute-start(bf16[128,512]{1,0:T(8,128)(2,1)S(1)} %collective-permute-done.3.rest_4_), channel_id=1, source_target_pairs={{0,1},{1,0},{2,3},{3,2},{4,5},{5,4},{6,7},{7,6},{8,9},{9,8},{10,11... | collective-permute-start | bytes 393224 | tf_op jit(solution)/shard_map/ppermute | solution.py:101
  18.7 9.5 %collective-permute-start.5 = (bf16[128,512]{1,0:T(8,128)(2,1)S(1)}, bf16[128,512]{1,0:T(8,128)(2,1)S(1)}, u32[]{:S(2)}, u32[]{:S(2)}) collective-permute-start(bf16[128,512]{1,0:T(8,128)(2,1)S(1)} %collective-permute-done.3.rest_4_), channel_id=1, source_target_pairs={{0,2},{1,3},{2,0},{3,1},{4,6},{5,7},{6,4},{7,5},{8,10},{9,11},{10,... | collective-permute-start | bytes 393224 | tf_op jit(solution)/shard_map/ppermute | solution.py:101
  20.3 8.2 %collective-permute-start.6 = (bf16[128,512]{1,0:T(8,128)(2,1)S(1)}, bf16[128,512]{1,0:T(8,128)(2,1)S(1)}, u32[]{:S(2)}, u32[]{:S(2)}) collective-permute-start(bf16[128,512]{1,0:T(8,128)(2,1)S(1)} %collective-permute-done.3.rest_4_), channel_id=1, source_target_pairs={{0,3},{1,2},{2,1},{3,0},{4,7},{5,6},{6,5},{7,4},{8,11},{9,10},{10,... | collective-permute-start | bytes 393224 | tf_op jit(solution)/shard_map/ppermute | solution.py:101
  22.8 11.5 %collective-permute-start.12 = (s16[256,128]{1,0:T(8,128)(2,1)S(1)}, s16[256,128]{1,0:T(8,128)(2,1)S(1)}, u32[]{:S(2)}, u32[]{:S(2)}) collective-permute-start(s16[256,128]{1,0:T(8,128)(2,1)S(1)} %get-tuple-element.32), channel_id=1, source_target_pairs={{0,6},{1,7},{2,4},{3,5},{4,2},{5,3},{6,0},{7,1},{8,14},{9,15},{10,... | collective-permute-start | bytes 196616 | tf_op jit(solution)/shard_map/ppermute | solution.py:101
  25.3 9.0 %collective-permute-start.13 = (s16[256,128]{1,0:T(8,128)(2,1)S(1)}, s16[256,128]{1,0:T(8,128)(2,1)S(1)}, u32[]{:S(2)}, u32[]{:S(2)}) collective-permute-start(s16[256,128]{1,0:T(8,128)(2,1)S(1)} %get-tuple-element.33), channel_id=1, source_target_pairs={{0,7},{1,6},{2,5},{3,4},{4,3},{5,2},{6,1},{7,0},{8,15},{9,14},{10,... | collective-permute-start | bytes 196616 | tf_op jit(solution)/shard_map/ppermute | solution.py:101
  27.5 6.9 %collective-permute-start.7 = (s16[256,128]{1,0:T(8,128)(2,1)S(1)}, s16[256,128]{1,0:T(8,128)(2,1)S(1)}, u32[]{:S(2)}, u32[]{:S(2)}) collective-permute-start(s16[256,128]{1,0:T(8,128)(2,1)S(1)} %get-tuple-element.27), channel_id=1, source_target_pairs={{0,1},{1,0},{2,3},{3,2},{4,5},{5,4},{6,7},{7,6},{8,9},{9,8},{10,11... | collective-permute-start | bytes 196616 | tf_op jit(solution)/shard_map/ppermute | solution.py:101
  28.2 6.2 %collective-permute-start.8 = (s16[256,128]{1,0:T(8,128)(2,1)S(1)}, s16[256,128]{1,0:T(8,128)(2,1)S(1)}, u32[]{:S(2)}, u32[]{:S(2)}) collective-permute-start(s16[256,128]{1,0:T(8,128)(2,1)S(1)} %get-tuple-element.28), channel_id=1, source_target_pairs={{0,2},{1,3},{2,0},{3,1},{4,6},{5,7},{6,4},{7,5},{8,10},{9,11},{10,... | collective-permute-start | bytes 196616 | tf_op jit(solution)/shard_map/ppermute | solution.py:101
  28.5 5.9 %collective-permute-start.9 = (s16[256,128]{1,0:T(8,128)(2,1)S(1)}, s16[256,128]{1,0:T(8,128)(2,1)S(1)}, u32[]{:S(2)}, u32[]{:S(2)}) collective-permute-start(s16[256,128]{1,0:T(8,128)(2,1)S(1)} %get-tuple-element.29), channel_id=1, source_target_pairs={{0,3},{1,2},{2,1},{3,0},{4,7},{5,6},{6,5},{7,4},{8,11},{9,10},{10,... | collective-permute-start | bytes 196616 | tf_op jit(solution)/shard_map/ppermute | solution.py:101
  36.6 6.0 %collective-permute-start.17 = (bf16[128,512]{1,0:T(8,128)(2,1)S(1)}, bf16[128,512]{1,0:T(8,128)(2,1)S(1)}, u32[]{:S(2)}, u32[]{:S(2)}) collective-permute-start(bf16[128,512]{1,0:T(8,128)(2,1)S(1)} %get-tuple-element.39), channel_id=1, source_target_pairs={{0,1},{1,0},{2,3},{3,2},{4,5},{5,4},{6,7},{7,6},{8,9},{9,8},{10,11... | collective-permute-start | bytes 393224 | tf_op jit(solution)/shard_map/ppermute | solution.py:101
  37.4 6.6 %collective-permute-start.18 = (bf16[128,512]{1,0:T(8,128)(2,1)S(1)}, bf16[128,512]{1,0:T(8,128)(2,1)S(1)}, u32[]{:S(2)}, u32[]{:S(2)}) collective-permute-start(bf16[128,512]{1,0:T(8,128)(2,1)S(1)} %get-tuple-element.40), channel_id=1, source_target_pairs={{0,2},{1,3},{2,0},{3,1},{4,6},{5,7},{6,4},{7,5},{8,10},{9,11},{10,... | collective-permute-start | bytes 393224 | tf_op jit(solution)/shard_map/ppermute | solution.py:101
  38.9 8.4 %collective-permute-start.19 = (bf16[128,512]{1,0:T(8,128)(2,1)S(1)}, bf16[128,512]{1,0:T(8,128)(2,1)S(1)}, u32[]{:S(2)}, u32[]{:S(2)}) collective-permute-start(bf16[128,512]{1,0:T(8,128)(2,1)S(1)} %get-tuple-element.41), channel_id=1, source_target_pairs={{0,3},{1,2},{2,1},{3,0},{4,7},{5,6},{6,5},{7,4},{8,11},{9,10},{10,... | collective-permute-start | bytes 393224 | tf_op jit(solution)/shard_map/ppermute | solution.py:101
  40.3 12.2 %collective-permute-start.22 = (bf16[384,512]{1,0:T(8,128)(2,1)S(1)}, bf16[384,512]{1,0:T(8,128)(2,1)S(1)}, u32[]{:S(2)}, u32[]{:S(2)}) collective-permute-start(bf16[384,512]{1,0:T(8,128)(2,1)S(1)} %add_convert_fusion), channel_id=1, source_target_pairs={{0,16},{8,24},{16,0},{24,8},{1,17},{9,25},{17,1},{25,9},{2,18},{10... | collective-permute-start | bytes 1179656 | tf_op jit(solution)/shard_map/ppermute | solution.py:101
  41.8 10.6 %collective-permute-start.14 = (bf16[128,512]{1,0:T(8,128)(2,1)S(1)}, bf16[128,512]{1,0:T(8,128)(2,1)S(1)}, u32[]{:S(2)}, u32[]{:S(2)}) collective-permute-start(bf16[128,512]{1,0:T(8,128)(2,1)S(1)} %get-tuple-element.35), channel_id=1, source_target_pairs={{0,1},{1,0},{2,3},{3,2},{4,5},{5,4},{6,7},{7,6},{8,9},{9,8},{10,11... | collective-permute-start | bytes 393224 | tf_op jit(solution)/shard_map/ppermute | solution.py:101
  42.6 10.4 %collective-permute-start.15 = (bf16[128,512]{1,0:T(8,128)(2,1)S(1)}, bf16[128,512]{1,0:T(8,128)(2,1)S(1)}, u32[]{:S(2)}, u32[]{:S(2)}) collective-permute-start(bf16[128,512]{1,0:T(8,128)(2,1)S(1)} %get-tuple-element.36), channel_id=1, source_target_pairs={{0,2},{1,3},{2,0},{3,1},{4,6},{5,7},{6,4},{7,5},{8,10},{9,11},{10,... | collective-permute-start | bytes 393224 | tf_op jit(solution)/shard_map/ppermute | solution.py:101
  44.1 8.9 %collective-permute-start.16 = (bf16[128,512]{1,0:T(8,128)(2,1)S(1)}, bf16[128,512]{1,0:T(8,128)(2,1)S(1)}, u32[]{:S(2)}, u32[]{:S(2)}) collective-permute-start(bf16[128,512]{1,0:T(8,128)(2,1)S(1)} %get-tuple-element.37), channel_id=1, source_target_pairs={{0,3},{1,2},{2,1},{3,0},{4,7},{5,6},{6,5},{7,4},{8,11},{9,10},{10,... | collective-permute-start | bytes 393224 | tf_op jit(solution)/shard_map/ppermute | solution.py:101
  47.4 8.4 %collective-permute-start.20 = (bf16[128,512]{1,0:T(8,128)(2,1)S(1)}, bf16[128,512]{1,0:T(8,128)(2,1)S(1)}, u32[]{:S(2)}, u32[]{:S(2)}) collective-permute-start(bf16[128,512]{1,0:T(8,128)(2,1)S(1)} %add_convert_fusion.1), channel_id=1, source_target_pairs={{0,4},{1,5},{2,6},{3,7},{4,0},{5,1},{6,2},{7,3},{8,12},{9,13},{10,... | collective-permute-start | bytes 393224 | tf_op jit(solution)/shard_map/ppermute | solution.py:101
  52.5 4.2 %collective-permute-start.23 = (bf16[384,512]{1,0:T(8,128)(2,1)S(1)}, bf16[384,512]{1,0:T(8,128)(2,1)S(1)}, u32[]{:S(2)}, u32[]{:S(2)}) collective-permute-start(bf16[384,512]{1,0:T(8,128)(2,1)S(1)} %add_convert_fusion), channel_id=1, source_target_pairs={{0,8},{8,0},{16,24},{24,16},{1,9},{9,1},{17,25},{25,17},{2,10},{10... | collective-permute-start | bytes 1179656 | tf_op jit(solution)/shard_map/ppermute | solution.py:101
  52.5 4.2 %collective-permute-start.24 = (bf16[384,512]{1,0:T(8,128)(2,1)S(1)}, bf16[384,512]{1,0:T(8,128)(2,1)S(1)}, u32[]{:S(2)}, u32[]{:S(2)}) collective-permute-start(bf16[384,512]{1,0:T(8,128)(2,1)S(1)} %collective-permute-done.22), channel_id=1, source_target_pairs={{0,8},{8,0},{16,24},{24,16},{1,9},{9,1},{17,25},{25,17},{2,10},{10... | collective-permute-start | bytes 1179656 | tf_op jit(solution)/shard_map/ppermute | solution.py:101
  (7 other events, 60.3 us)

commit v2 on v1

v2 whole, which is shorter than its diff:
```python
import functools
import math

import jax
import jax.numpy as jnp
from jax import lax
from jax.experimental import pallas as pl
from jax.experimental.pallas import tpu as pltpu
from jax.sharding import PartitionSpec as P

CONFIDENCE = 40.0
STEPS = 65535.0
OFFSET = 32768
BF = jnp.bfloat16
F32 = jnp.float32

VM = pl.BlockSpec(memory_space=pltpu.VMEM)
SM = pl.BlockSpec(memory_space=pltpu.SMEM)
ROWS = (((1,), (1,)), ((), ()))
COLS = (((0,), (0,)), ((), ()))


def call(body, outs, in_specs, flops, moved, scratch=(), mib=24):
    return pl.pallas_call(
        body,
        out_shape=outs,
        in_specs=in_specs,
        out_specs=jax.tree.map(lambda _: VM, outs),
        scratch_shapes=scratch,
        compiler_params=pltpu.CompilerParams(vmem_limit_bytes=mib << 20),
        cost_estimate=pl.CostEstimate(flops=flops, bytes_accessed=moved, transcendentals=0),
    )


def slots(n, limit, pair_ref, count_ref, where):
    for s in range(n * limit):
        where[s] = -1
    for i in range(pair_ref.shape[1]):
        @pl.when(i < count_ref[0])
        def _():
            where[pair_ref[1, i]] = i


def coded(limit, rate_ref, where, peer, c):
    i = where[peer * limit + c]
    rate = rate_ref[jnp.maximum(i, 0)]
    code = jnp.where(i >= 0, (rate * STEPS + 0.5).astype(jnp.int32), 0) - OFFSET
    return code.astype(jnp.int16)


def give_body(n, limit, pair_ref, count_ref, rate_ref, out_ref, where):
    slots(n, limit, pair_ref, count_ref, where)
    me, far, width = lax.axis_index("row"), n // 2, rate_ref.shape[1]
    first = far * (1 - lax.axis_index("grp") % 2)
    for j in range(far):
        for c in range(limit):
            at = (j * limit + c) * width
            out_ref[at : at + width] = coded(limit, rate_ref, where, me ^ (first + j), c)


def keep_body(n, limit, pair_ref, count_ref, rate_ref, got_ref, *rest):
    far, width = n // 2, rate_ref.shape[1]
    outs, where = rest[:far], rest[far]
    slots(n, limit, pair_ref, count_ref, where)
    me = lax.axis_index("row")
    first = far * (lax.axis_index("grp") % 2)
    rows = limit * width
    for j in range(far):
        for c in range(limit):
            outs[j][c * width : (c + 1) * width] = coded(
                limit, rate_ref, where, me ^ (first + j), c
            )
        outs[j][rows:] = got_ref[j * rows : (j + 1) * rows]


def gram_body(item_ref, gram_ref):
    items = item_ref[...]
    gram_ref[...] = lax.dot_general(items, items, COLS, preferred_element_type=F32).astype(BF)


def block_at(send_refs, t, c, peer, width):
    return pl.ds(pl.multiple_of(send_refs[t][c, peer] * width, width), width)


def peer_of(n, j):
    return lax.axis_index("row") ^ (n // 2 * (lax.axis_index("grp") % 2) + j)


def user_terms(n, limit, width, j, send_refs, item_ref, gram, user_ref, code_ref, keep):
    terms = []
    for t in range(2):
        left = user_ref[t * width : (t + 1) * width]
        total = jnp.dot(left, gram, preferred_element_type=F32)
        for c in range(limit):
            right = item_ref[block_at(send_refs, t, c, peer_of(n, j), width)]
            at = (t * limit + c) * width
            code = code_ref[at : at + width].astype(jnp.int32) + OFFSET
            weighted = CONFIDENCE * (code.astype(F32) * (1.0 / STEPS))
            score = lax.dot_general(left, right, ROWS, preferred_element_type=F32)
            error = jnp.where(code > 0, weighted * score - 1.0 - weighted, 0.0).astype(BF)
            total += jnp.dot(error, right, preferred_element_type=F32)
            keep(t, c, error)
        terms.append(total)
    return terms


def add_items(n, limit, width, j, send_refs, user_ref, t, c, error, sum_ref):
    left = user_ref[t * width : (t + 1) * width]
    term = lax.dot_general(error, left, COLS, preferred_element_type=F32)
    sum_ref[block_at(send_refs, t, c, peer_of(n, j), width)] += term.astype(BF).astype(F32)


def first_body(n, limit, width, own_ref, oth_ref, item_ref, gram_ref, user_ref, code_ref, *outs):
    out_ref, sum_ref, cross_ref = outs
    sends = (own_ref, oth_ref)
    sum_ref[...] = jnp.zeros_like(sum_ref)

    def keep(t, c, error):
        add_items(n, limit, width, 0, sends, user_ref, t, c, error, sum_ref)

    terms = user_terms(
        n, limit, width, 0, sends, item_ref, gram_ref[...], user_ref, code_ref, keep
    )
    for t in range(2):
        out_ref[t * width : (t + 1) * width] = terms[t]
    users = user_ref[...]
    cross_ref[...] = lax.dot_general(users, users, COLS, preferred_element_type=F32)


def users_body(n, limit, width, own_ref, oth_ref, item_ref, gram_ref, *rest):
    m = n // 2 - 1
    users, codes, outs, error_ref = rest[:m], rest[m : 2 * m], rest[2 * m : 3 * m], rest[3 * m]
    gram = gram_ref[...]
    for j in range(m):
        def keep(t, c, error):
            error_ref[(j * 2 + t) * limit + c] = error

        terms = user_terms(
            n, limit, width, j + 1, (own_ref, oth_ref), item_ref, gram, users[j], codes[j], keep
        )
        for t in range(2):
            outs[j][t * width : (t + 1) * width] = terms[t].astype(BF)


def items_body(n, limit, width, own_ref, oth_ref, item_ref, part_ref, cross_ref, error_ref, *rest):
    m = n // 2 - 1
    users, (mine_ref, other_ref, sum_ref) = rest[:m], rest[m:]
    cross = cross_ref[...]
    for j in range(m):
        block = users[j][...]
        cross += lax.dot_general(block, block, COLS, preferred_element_type=F32)
    sum_ref[...] = part_ref[...] + jnp.dot(
        item_ref[...], cross.astype(BF), preferred_element_type=F32
    )
    for j in range(m):
        for t in range(2):
            for c in range(limit):
                error = error_ref[(j * 2 + t) * limit + c]
                add_items(
                    n, limit, width, j + 1, (own_ref, oth_ref), users[j], t, c, error, sum_ref
                )
    core = lax.axis_index("grp") % 2
    half = mine_ref.shape[0]
    mine_ref[...] = sum_ref[pl.ds(pl.multiple_of(core * half, half), half)]
    other_ref[...] = sum_ref[pl.ds(pl.multiple_of((1 - core) * half, half), half)].astype(BF)


def swap(x, axis, k):
    return lax.ppermute(x, axis, [(i, i ^ k) for i in range(lax.axis_size(axis))])


def swap_by_core(x, j):
    n, grp_n = lax.axis_size("row"), lax.axis_size("grp")
    pairs = [(g * n + r, g * n + (r ^ (n // 2 * (g % 2) + j))) for g in range(grp_n) for r in range(n)]
    return lax.ppermute(x, ("grp", "row"), pairs)


def shards(users, items, ratings, pair_list, send_list, counts):
    n = lax.axis_size("row")
    grp_n = lax.axis_size("grp")
    width = ratings.shape[2]
    factors = users.shape[1]
    limit = send_list.shape[2]
    item_rows = items.shape[0]
    user_rows = users.shape[0]
    far = n // 2
    total_users = user_rows * grp_n * n
    total_items = item_rows * n
    sds = jax.ShapeDtypeStruct
    table = pltpu.SMEM((n * limit,), jnp.int32)

    pairs = jnp.swapaxes(pair_list[0], 0, 1)
    sends = jnp.swapaxes(send_list[0], 0, 1)
    sends = (sends, swap(sends, "grp", 1))

    both = jnp.concatenate([users, swap(users, "grp", 1)])
    blocks = [swap_by_core(both, 0)]
    blocks += [swap(blocks[0], "row", j) for j in range(1, far)]

    given = call(
        functools.partial(give_body, n, limit),
        sds((far * limit * width, width), jnp.int16),
        [SM, SM, VM],
        0,
        ratings.size * 3,
        [table],
    )(pairs, counts, ratings[0])
    codes = call(
        functools.partial(keep_body, n, limit),
        [sds((2 * limit * width, width), jnp.int16)] * far,
        [SM, SM, VM, VM],
        0,
        ratings.size * 3,
        [table],
    )(pairs, counts, ratings[0], swap(given, "grp", 1))
    codes = [swap_by_core(codes[j], j) for j in range(far)]

    pair_flops = 2 * 2 * limit * user_rows * factors * width
    cross_flops = 2 * 2 * user_rows * factors**2
    gram = call(
        gram_body, sds((factors, factors), BF), [VM], 2 * item_rows * factors**2, items.size * 2
    )(items)
    first, part, cross = call(
        functools.partial(first_body, n, limit, width),
        [
            sds((2 * user_rows, factors), F32),
            sds((item_rows, factors), F32),
            sds((factors, factors), F32),
        ],
        [SM, SM, VM, VM, VM, VM],
        3 * pair_flops + 2 * cross_flops,
        4 << 20,
    )(*sends, items, gram, blocks[0], codes[0])
    *terms, errors = call(
        functools.partial(users_body, n, limit, width),
        [sds((2 * user_rows, factors), BF)] * (far - 1)
        + [sds(((far - 1) * 2 * limit, user_rows, width), BF)],
        [SM, SM, VM, VM] + [VM] * (2 * far - 2),
        (far - 1) * (2 * pair_flops + cross_flops),
        4 << 20,
    )(*sends, items, gram, *blocks[1:], *codes[1:])
    half = item_rows // 2
    mine, other = call(
        functools.partial(items_body, n, limit, width),
        [sds((half, factors), F32), sds((half, factors), BF)],
        [SM, SM, VM, VM, VM, VM] + [VM] * (far - 1),
        (far - 1) * (pair_flops + cross_flops) + 2 * item_rows * factors**2,
        8 << 20,
        [pltpu.VMEM((item_rows, factors), F32)],
    )(*sends, items, part, cross, errors, *blocks[1:])

    user_sum = first
    for j in range(1, far):
        user_sum += swap(terms[j - 1], "row", j).astype(F32)
    user_sum = swap_by_core(user_sum.astype(BF), 0)
    user_sum = user_sum[:user_rows].astype(F32) + swap(user_sum[user_rows:], "grp", 1).astype(F32)
    new_users = users.astype(F32) - 4.0 / math.sqrt(total_items) * user_sum

    core = lax.axis_index("grp") % 2
    pair_sum = mine + swap(other, "grp", 1).astype(F32)
    if grp_n == 4:
        here = pair_sum.astype(BF)
        there = swap(here, "grp", 2)
        one = here.astype(F32) + there.astype(F32)
        two = swap(here, "grp", 1).astype(F32) + swap(there, "grp", 1).astype(F32)
    else:
        peers = [list(range(c, grp_n, 2)) for c in range(2)]
        one = lax.psum(pair_sum, "grp", axis_index_groups=peers)
        two = swap(one, "grp", 1)
    item_sum = jnp.where(core == 0, jnp.concatenate([one, two]), jnp.concatenate([two, one]))
    new_items = items.astype(F32) - 8.0 / math.sqrt(total_users) * item_sum
    return (new_users, new_items)


def solution(mesh):
    in_specs = (
        P(("grp", "row"), None),
        P("row", None),
        P(("grp", "row"), None, None, None),
        P(("grp", "row"), None, None),
        P(("grp", "row"), None, None),
        P(("grp", "row")),
    )
    out_specs = (P(("grp", "row"), None), P("row", None))
    return jax.shard_map(shards, mesh=mesh, in_specs=in_specs, out_specs=out_specs, check_vma=False)
```

time: 59.7 us -> 68.2 us (1.14)
  starting transfers between devices: 36.7 us -> 42.7 us
  local copies, waits for them, and re-layouts: 3.92 us -> 1.92 us
  Pallas kernels: 6.92 us -> 8.66 us
  waiting for transfers between devices: 7.53 us -> 9.13 us
  other arithmetic: 2.71 us -> 3.67 us
    ppermute x0 -> x6, starting transfers between devices: none -> 8.25 us  [swap_by_core(): return lax.ppermute(x, ('grp', 'row'), pairs)]
    ppermute x0 -> x6, waiting for transfers between devices: none -> 5.27 us  [swap_by_core(): return lax.ppermute(x, ('grp', 'row'), pairs)]
    ppermute x25 -> x14, waiting for transfers between devices: 7.53 us -> 3.86 us  [swap(): lax.ppermute(x, axis, [(i, i ^ k) for i in range(lax.axis_size(axis))])]
    ppermute x25 -> x14, starting transfers between devices: 36.7 us -> 34.4 us  [swap(): lax.ppermute(x, axis, [(i, i ^ k) for i in range(lax.axis_size(axis))])]
    unnamed x12 -> x10, local copies, waits for them, and re-layouts: 3.92 us -> 1.91 us
    pallas_call x3 -> x5, Pallas kernels: 6.32 us -> 8.05 us  [the longest x1 2.42 us: shards(): call(functools.partial(users_body, n, limit, width), [sds((2 * user_rows,...]
    concatenate x0 -> x1, other arithmetic: none -> 0.92 us  [shards(): both = jnp.concatenate([users, swap(users, 'grp', 1)])]
  transfers between devices with their start and end apart: 25 -> 20, of which waited for: 4 -> 7; matrix products, arithmetic and copies ran while one was open for 2% -> 3% of each run, Pallas kernels for 8% -> 13%
where the time goes in v2:
time: 68.2 us; the launch traced here: 67.5 us
  starting transfers between devices  42.7 us (63%)
  waiting for transfers between devices  9.13 us (13%)
  Pallas kernels  8.66 us (13%)
  other arithmetic  3.67 us (5%)
  local copies, waits for them, and re-layouts  1.92 us (3%)
  between operations  1.44 us (2%)
    ppermute x14, starting transfers between devices, swap(): lax.ppermute(x, axis, [(i, i ^ k) for i in range(lax.axis_size(axis))])  34.4 us
    ppermute x6, starting transfers between devices, swap_by_core(): return lax.ppermute(x, ('grp', 'row'), pairs)  8.25 us
    ppermute x6, waiting for transfers between devices, swap_by_core(): return lax.ppermute(x, ('grp', 'row'), pairs)  5.27 us
    ppermute x14, waiting for transfers between devices, swap(): lax.ppermute(x, axis, [(i, i ^ k) for i in range(lax.axis_size(axis))])  3.86 us
    pallas_call x1, Pallas kernels, shards(): call(functools.partial(users_body, n, limit, width), [sds((2 * user_rows,...  2.42 us
    pallas_call x1, Pallas kernels, shards(): call(functools.partial(items_body, n, limit, width), [sds((half, factors)...  2.16 us
    pallas_call x1, Pallas kernels, shards(): call(functools.partial(first_body, n, limit, width), [sds((2 * user_rows,...  2.02 us
    unnamed x10, local copies, waits for them, and re-layouts  1.91 us
  transfers between devices with their start and end apart: 20, of which 7 were waited for; matrix products, arithmetic and copies ran while one was open for 3% of the time, Pallas kernels for 13%

profile of v2, /device:TPU:0, one launch (start us, length us, event | category | flops | bytes accessed | tf_op | source)
XLA Modules:
  0.0 67.5 jit_solution(14667011939037439745)
XLA Ops:
  1.8 1.2 %copy-done = f32[1,16,128,128]{3,2,1,0:T(8,128)S(1)} copy-done((f32[1,16,128,128]{3,2,1,0:T(8,128)S(1)}, f32[1,16,128,128]{3,2,1,0:T(8,128)}, u32[]{:S(2)}) %copy-start) | copy-done | bytes 1048600
  3.7 0.7 %shard_map.78 = s16[1024,128]{1,0:T(8,128)(2,1)S(1)} custom-call(s32[2,16]{1,0:T(2,128)S(1)} %bitcast.9, s32[1]{0:T(128)S(6)} %copy.8.count_ref, f32[16,128,128]{2,1,0:T(8,128)S(1)} %bitcast.7), custom_call_target="tpu_custom_call" | custom-call | bytes 786432 | tf_op jit(solution)/shard_map/pallas_call | solution.py:200
  4.6 0.9 %pad_maximum_fusion = bf16[256,512]{1,0:T(8,128)(2,1)S(1)} fusion(bf16[128,512]{1,0:T(8,128)(2,1)S(1)} %collective-permute-done.1, bf16[128,512]{1,0:T(8,128)(2,1)} %param.6), kind=kLoop, calls=%fused_computation.7 | loop fusion | flops 524288 | bytes 524288 | tf_op jit(solution)/shard_map/concatenate | solution.py:196
  6.2 0.7 %shard_map.79 = (s16[512,128]{1,0:T(8,128)(2,1)S(1)}, s16[512,128]{1,0:T(8,128)(2,1)S(1)}, s16[512,128]{1,0:T(8,128)(2,1)S(1)}, s16[512,128]{1,0:T(8,128)(2,1)S(1)}) custom-call(s32[2,16]{1,0:T(2,128)S(1)} %bitcast.10, s32[1]{0:T(128)S(6)} %copy.8.count_ref, f32[16,128,128]{2,1,0:T(8,128)S(1)} %bitcast.8, s16[1024,128]{1,0:T(8,128)(2,1)S(1)} %collective-permute-done.3.got_ref), custom_call_target="tpu_custom_call" | custom-call | bytes 786432 | tf_op jit(solution)/shard_map/pallas_call | solution.py:208
  6.9 3.0 %collective-permute-start.8 = (s16[512,128]{1,0:T(8,128)(2,1)S(1)}, s16[512,128]{1,0:T(8,128)(2,1)S(1)}, u32[]{:S(2)}, u32[]{:S(2)}) collective-permute-start(s16[512,128]{1,0:T(8,128)(2,1)S(1)} %get-tuple-element.17), channel_id=1, source_target_pairs={{0,1},{1,0},{2,3},{3,2},{4,5},{5,4},{6,7},{7,6},{8,13},{9,12},{10,... | collective-permute-start | bytes 393224 | tf_op jit(solution)/shard_map/ppermute | solution.py:175
  10.0 2.0 %collective-permute-start.6 = (bf16[256,512]{1,0:T(8,128)(2,1)S(1)}, bf16[256,512]{1,0:T(8,128)(2,1)S(1)}, u32[]{:S(2)}, u32[]{:S(2)}) collective-permute-start(bf16[256,512]{1,0:T(8,128)(2,1)S(1)} %collective-permute-done.2.user_ref), channel_id=1, source_target_pairs={{0,2},{1,3},{2,0},{3,1},{4,6},{5,7},{6,4},{7,5},{8,10},{9,11},{10,... | collective-permute-start | bytes 786440 | tf_op jit(solution)/shard_map/ppermute | solution.py:169
  12.0 1.4 %collective-permute-start.7 = (bf16[256,512]{1,0:T(8,128)(2,1)S(1)}, bf16[256,512]{1,0:T(8,128)(2,1)S(1)}, u32[]{:S(2)}, u32[]{:S(2)}) collective-permute-start(bf16[256,512]{1,0:T(8,128)(2,1)S(1)} %collective-permute-done.2.user_ref), channel_id=1, source_target_pairs={{0,3},{1,2},{2,1},{3,0},{4,7},{5,6},{6,5},{7,4},{8,11},{9,10},{10,... | collective-permute-start | bytes 786440 | tf_op jit(solution)/shard_map/ppermute | solution.py:169
  13.5 8.5 %collective-permute-start = (s32[2,8]{1,0:T(2,128)S(1)}, s32[2,8]{1,0:T(2,128)S(1)}, u32[]{:S(2)}, u32[]{:S(2)}) collective-permute-start(s32[2,8]{1,0:T(2,128)S(1)} %bitcast.11), channel_id=1, source_target_pairs={{0,8},{8,0},{16,24},{24,16},{1,9},{9,1},{17,25},{25,17},{2,10},{10... | collective-permute-start | bytes 200 | tf_op jit(solution)/shard_map/ppermute | solution.py:169
  21.9 0.8 %collective-permute-done.oth_ref = s32[2,8]{1,0:T(2,128)S(1)} collective-permute-done((s32[2,8]{1,0:T(2,128)S(1)}, s32[2,8]{1,0:T(2,128)S(1)}, u32[]{:S(2)}, u32[]{:S(2)}) %collective-permute-start) | collective-permute-done | bytes 96 | tf_op jit(solution)/shard_map/ppermute | solution.py:169
  22.7 0.9 %collective-permute-start.9 = (s16[512,128]{1,0:T(8,128)(2,1)S(1)}, s16[512,128]{1,0:T(8,128)(2,1)S(1)}, u32[]{:S(2)}, u32[]{:S(2)}) collective-permute-start(s16[512,128]{1,0:T(8,128)(2,1)S(1)} %get-tuple-element.18), channel_id=1, source_target_pairs={{0,2},{1,3},{2,0},{3,1},{4,6},{5,7},{6,4},{7,5},{8,14},{9,15},{10,... | collective-permute-start | bytes 393224 | tf_op jit(solution)/shard_map/ppermute | solution.py:175
  23.6 2.3 %collective-permute-start.10 = (s16[512,128]{1,0:T(8,128)(2,1)S(1)}, s16[512,128]{1,0:T(8,128)(2,1)S(1)}, u32[]{:S(2)}, u32[]{:S(2)}) collective-permute-start(s16[512,128]{1,0:T(8,128)(2,1)S(1)} %get-tuple-element.19), channel_id=1, source_target_pairs={{0,3},{1,2},{2,1},{3,0},{4,7},{5,6},{6,5},{7,4},{8,15},{9,14},{10,... | collective-permute-start | bytes 393224 | tf_op jit(solution)/shard_map/ppermute | solution.py:175
  25.9 3.2 %collective-permute-done.9.rest_4_ = s16[512,128]{1,0:T(8,128)(2,1)S(1)} collective-permute-done((s16[512,128]{1,0:T(8,128)(2,1)S(1)}, s16[512,128]{1,0:T(8,128)(2,1)S(1)}, u32[]{:S(2)}, u32[]{:S(2)}) %collective-permute-start.9) | collective-permute-done | bytes 131104 | tf_op jit(solution)/shard_map/ppermute | solution.py:175
  30.5 2.0 %collective-permute-done.10.rest_5_ = s16[512,128]{1,0:T(8,128)(2,1)S(1)} collective-permute-done((s16[512,128]{1,0:T(8,128)(2,1)S(1)}, s16[512,128]{1,0:T(8,128)(2,1)S(1)}, u32[]{:S(2)}, u32[]{:S(2)}) %collective-permute-start.10) | collective-permute-done | bytes 131104 | tf_op jit(solution)/shard_map/ppermute | solution.py:175
  32.5 2.4 %shard_map.81 = (bf16[256,512]{1,0:T(8,128)(2,1)S(1)}, bf16[256,512]{1,0:T(8,128)(2,1)S(1)}, bf16[256,512]{1,0:T(8,128)(2,1)S(1)}, bf16[12,128,128]{2,1,0:T(8,128)(2,1)S(1)}) custom-call(s32[2,8]{1,0:T(2,128)S(1)} %bitcast.12, s32[2,8]{1,0:T(2,128)S(1)} %collective-permute-done.oth_ref, bf16[768,512]{1,0:T(8,128)(2,1)S(1)} %copy-done.1, ...), custom_call_target="tpu_custom_call" | custom-call | flops 805306368 | bytes 4194304 | tf_op jit(solution)/shard_map/pallas_call | solution.py:234
  34.9 2.3 %collective-permute-start.13 = (bf16[256,512]{1,0:T(8,128)(2,1)S(1)}, bf16[256,512]{1,0:T(8,128)(2,1)S(1)}, u32[]{:S(2)}, u32[]{:S(2)}) collective-permute-start(bf16[256,512]{1,0:T(8,128)(2,1)S(1)} %get-tuple-element.22), channel_id=1, source_target_pairs={{0,3},{1,2},{2,1},{3,0},{4,7},{5,6},{6,5},{7,4},{8,11},{9,10},{10,... | collective-permute-start | bytes 786440 | tf_op jit(solution)/shard_map/ppermute | solution.py:169
  37.2 1.3 %collective-permute-start.11 = (bf16[256,512]{1,0:T(8,128)(2,1)S(1)}, bf16[256,512]{1,0:T(8,128)(2,1)S(1)}, u32[]{:S(2)}, u32[]{:S(2)}) collective-permute-start(bf16[256,512]{1,0:T(8,128)(2,1)S(1)} %get-tuple-element.20), channel_id=1, source_target_pairs={{0,1},{1,0},{2,3},{3,2},{4,5},{5,4},{6,7},{7,6},{8,9},{9,8},{10,11... | collective-permute-start | bytes 786440 | tf_op jit(solution)/shard_map/ppermute | solution.py:169
  38.5 2.0 %shard_map.80 = (f32[256,512]{1,0:T(8,128)S(1)}, f32[768,512]{1,0:T(8,128)S(1)}, f32[512,512]{1,0:T(8,128)S(1)}) custom-call(s32[2,8]{1,0:T(2,128)S(1)} %bitcast.13, s32[2,8]{1,0:T(2,128)S(1)} %collective-permute-done.oth_ref, bf16[768,512]{1,0:T(8,128)(2,1)S(1)} %copy-done.1, bf16[512,512]{1,0:T(8,128)(2,1)S(1)} %shard_map.77.gram_ref, ...), custom_call_target="tpu_custom_call" | custom-call | flops 469762048 | bytes 4194304 | tf_op jit(solution)/shard_map/pallas_call | solution.py:223
  40.5 2.2 %shard_map.82 = (f32[384,512]{1,0:T(8,128)S(1)}, bf16[384,512]{1,0:T(8,128)(2,1)S(1)}) custom-call(s32[2,8]{1,0:T(2,128)S(1)} %bitcast.14, s32[2,8]{1,0:T(2,128)S(1)} %collective-permute-done.oth_ref, bf16[768,512]{1,0:T(8,128)(2,1)S(1)} %copy-done.1, f32[768,512]{1,0:T(8,128)S(1)} %get-tuple-element.23.part_ref, ...), custom_call_target="tpu_custom_call" | custom-call | flops 1006632960 | bytes 8388608 | tf_op jit(solution)/shard_map/pallas_call | solution.py:243
  42.7 4.3 %collective-permute-start.16 = (bf16[384,512]{1,0:T(8,128)(2,1)S(1)}, bf16[384,512]{1,0:T(8,128)(2,1)S(1)}, u32[]{:S(2)}, u32[]{:S(2)}) collective-permute-start(bf16[384,512]{1,0:T(8,128)(2,1)S(1)} %get-tuple-element.27), channel_id=1, source_target_pairs={{0,8},{8,0},{16,24},{24,16},{1,9},{9,1},{17,25},{25,17},{2,10},{10... | collective-permute-start | bytes 1179656 | tf_op jit(solution)/shard_map/ppermute | solution.py:169
  47.0 1.8 %collective-permute-done.12 = bf16[256,512]{1,0:T(8,128)(2,1)S(1)} collective-permute-done((bf16[256,512]{1,0:T(8,128)(2,1)S(1)}, bf16[256,512]{1,0:T(8,128)(2,1)S(1)}, u32[]{:S(2)}, u32[]{:S(2)}) %collective-permute-start.12) | collective-permute-done | bytes 262176 | tf_op jit(solution)/shard_map/ppermute | solution.py:169
  50.1 1.5 %collective-permute-start.17 = (bf16[384,512]{1,0:T(8,128)(2,1)S(1)}, bf16[384,512]{1,0:T(8,128)(2,1)S(1)}, u32[]{:S(2)}, u32[]{:S(2)}) collective-permute-start(bf16[384,512]{1,0:T(8,128)(2,1)S(1)} %add_convert_fusion), channel_id=1, source_target_pairs={{0,16},{8,24},{16,0},{24,8},{1,17},{9,25},{17,1},{25,9},{2,18},{10... | collective-permute-start | bytes 1179656 | tf_op jit(solution)/shard_map/ppermute | solution.py:169
  51.6 11.9 %collective-permute-start.15 = (bf16[128,512]{1,0:T(8,128)(2,1)S(1)}, bf16[128,512]{1,0:T(8,128)(2,1)S(1)}, u32[]{:S(2)}, u32[]{:S(2)}) collective-permute-start(bf16[128,512]{1,0:T(8,128)(2,1)S(1)} %slice.9), channel_id=1, source_target_pairs={{0,8},{8,0},{16,24},{24,16},{1,9},{9,1},{17,25},{25,17},{2,10},{10... | collective-permute-start | bytes 393224 | tf_op jit(solution)/shard_map/ppermute | solution.py:169
  64.6 0.8 %multiply_subtract_fusion = f32[128,512]{1,0:T(8,128)} fusion(bf16[128,512]{1,0:T(8,128)(2,1)S(1)} %collective-permute-done.15, bf16[128,512]{1,0:T(8,128)(2,1)S(1)} %copy-done.4, bf16[256,512]{1,0:T(8,128)(2,1)S(1)} %collective-permute-done.14), kind=kLoop, calls=%fused_computation.8 | loop fusion | flops 393216 | bytes 655360 | tf_op jit(solution)/shard_map/sub | solution.py:257
  66.0 1.5 %fusion.1 = f32[768,512]{1,0:T(8,128)} fusion(f32[384,512]{1,0:T(8,128)S(1)} %convert_add_fusion, f32[384,512]{1,0:T(8,128)S(1)} %convert_add_fusion.1, bf16[768,512]{1,0:T(8,128)(2,1)S(1)} %copy-done.1, pred[]{:T(512)S(6)} %eq.5), kind=kLoop, calls=%fused_computation.2 | loop fusion | flops 2359296 | bytes 3932161 | tf_op jit(solution)/shard_map/sub | solution.py:271
  (40 shorter events, 6.3 us)
Async XLA Ops:
  0.6 3.9 %collective-permute-start.1 = (bf16[128,512]{1,0:T(8,128)(2,1)}, bf16[128,512]{1,0:T(8,128)(2,1)S(1)}, u32[]{:S(2)}, u32[]{:S(2)}) collective-permute-start(bf16[128,512]{1,0:T(8,128)(2,1)} %param.6), channel_id=1, source_target_pairs={{0,8},{8,0},{16,24},{24,16},{1,9},{9,1},{17,25},{25,17},{2,10},{10... | collective-permute-start | bytes 393224 | tf_op jit(solution)/shard_map/ppermute | solution.py:169
  1.8 1.2 %copy-start = (f32[1,16,128,128]{3,2,1,0:T(8,128)S(1)}, f32[1,16,128,128]{3,2,1,0:T(8,128)}, u32[]{:S(2)}) copy-start(f32[1,16,128,128]{3,2,1,0:T(8,128)} %param.8) | copy-start | bytes 3145732
  3.7 9.7 %copy-start.3 = (s32[1,8,2]{1,2,0:T(2,128)S(1)}, s32[1,8,2]{1,2,0:T(2,128)}, u32[]{:S(2)}) copy-start(s32[1,8,2]{1,2,0:T(2,128)} %param.10) | copy-start | bytes 196
  3.7 26.1 %copy-start.1 = (bf16[768,512]{1,0:T(8,128)(2,1)S(1)}, bf16[768,512]{1,0:T(8,128)(2,1)}, u32[]{:S(2)}) copy-start(bf16[768,512]{1,0:T(8,128)(2,1)} %item_ref.7) | copy-start | bytes 2359300
  4.4 1.7 %collective-permute-start.3 = (s16[1024,128]{1,0:T(8,128)(2,1)S(1)}, s16[1024,128]{1,0:T(8,128)(2,1)S(1)}, u32[]{:S(2)}, u32[]{:S(2)}) collective-permute-start(s16[1024,128]{1,0:T(8,128)(2,1)S(1)} %shard_map.78), channel_id=1, source_target_pairs={{0,8},{8,0},{16,24},{24,16},{1,9},{9,1},{17,25},{25,17},{2,10},{10... | collective-permute-start | bytes 786440 | tf_op jit(solution)/shard_map/ppermute | solution.py:169
  5.5 4.5 %collective-permute-start.2 = (bf16[256,512]{1,0:T(8,128)(2,1)S(1)}, bf16[256,512]{1,0:T(8,128)(2,1)S(1)}, u32[]{:S(2)}, u32[]{:S(2)}) collective-permute-start(bf16[256,512]{1,0:T(8,128)(2,1)S(1)} %pad_maximum_fusion), channel_id=1, source_target_pairs={{0,0},{1,1},{2,2},{3,3},{4,4},{5,5},{6,6},{7,7},{8,12},{9,13},{10,... | collective-permute-start | bytes 786440 | tf_op jit(solution)/shard_map/ppermute | solution.py:175
  6.9 16.7 %collective-permute-start.8 = (s16[512,128]{1,0:T(8,128)(2,1)S(1)}, s16[512,128]{1,0:T(8,128)(2,1)S(1)}, u32[]{:S(2)}, u32[]{:S(2)}) collective-permute-start(s16[512,128]{1,0:T(8,128)(2,1)S(1)} %get-tuple-element.17), channel_id=1, source_target_pairs={{0,1},{1,0},{2,3},{3,2},{4,5},{5,4},{6,7},{7,6},{8,13},{9,12},{10,... | collective-permute-start | bytes 393224 | tf_op jit(solution)/shard_map/ppermute | solution.py:175
  10.0 22.5 %collective-permute-start.5 = (bf16[256,512]{1,0:T(8,128)(2,1)S(1)}, bf16[256,512]{1,0:T(8,128)(2,1)S(1)}, u32[]{:S(2)}, u32[]{:S(2)}) collective-permute-start(bf16[256,512]{1,0:T(8,128)(2,1)S(1)} %collective-permute-done.2.user_ref), channel_id=1, source_target_pairs={{0,1},{1,0},{2,3},{3,2},{4,5},{5,4},{6,7},{7,6},{8,9},{9,8},{10,11... | collective-permute-start | bytes 786440 | tf_op jit(solution)/shard_map/ppermute | solution.py:169
  10.0 22.4 %collective-permute-start.6 = (bf16[256,512]{1,0:T(8,128)(2,1)S(1)}, bf16[256,512]{1,0:T(8,128)(2,1)S(1)}, u32[]{:S(2)}, u32[]{:S(2)}) collective-permute-start(bf16[256,512]{1,0:T(8,128)(2,1)S(1)} %collective-permute-done.2.user_ref), channel_id=1, source_target_pairs={{0,2},{1,3},{2,0},{3,1},{4,6},{5,7},{6,4},{7,5},{8,10},{9,11},{10,... | collective-permute-start | bytes 786440 | tf_op jit(solution)/shard_map/ppermute | solution.py:169
  12.0 20.5 %collective-permute-start.7 = (bf16[256,512]{1,0:T(8,128)(2,1)S(1)}, bf16[256,512]{1,0:T(8,128)(2,1)S(1)}, u32[]{:S(2)}, u32[]{:S(2)}) collective-permute-start(bf16[256,512]{1,0:T(8,128)(2,1)S(1)} %collective-permute-done.2.user_ref), channel_id=1, source_target_pairs={{0,3},{1,2},{2,1},{3,0},{4,7},{5,6},{6,5},{7,4},{8,11},{9,10},{10,... | collective-permute-start | bytes 786440 | tf_op jit(solution)/shard_map/ppermute | solution.py:169
  13.5 9.3 %collective-permute-start = (s32[2,8]{1,0:T(2,128)S(1)}, s32[2,8]{1,0:T(2,128)S(1)}, u32[]{:S(2)}, u32[]{:S(2)}) collective-permute-start(s32[2,8]{1,0:T(2,128)S(1)} %bitcast.11), channel_id=1, source_target_pairs={{0,8},{8,0},{16,24},{24,16},{1,9},{9,1},{17,25},{25,17},{2,10},{10... | collective-permute-start | bytes 200 | tf_op jit(solution)/shard_map/ppermute | solution.py:169
  22.7 6.4 %collective-permute-start.9 = (s16[512,128]{1,0:T(8,128)(2,1)S(1)}, s16[512,128]{1,0:T(8,128)(2,1)S(1)}, u32[]{:S(2)}, u32[]{:S(2)}) collective-permute-start(s16[512,128]{1,0:T(8,128)(2,1)S(1)} %get-tuple-element.18), channel_id=1, source_target_pairs={{0,2},{1,3},{2,0},{3,1},{4,6},{5,7},{6,4},{7,5},{8,14},{9,15},{10,... | collective-permute-start | bytes 393224 | tf_op jit(solution)/shard_map/ppermute | solution.py:175
  23.6 8.9 %collective-permute-start.10 = (s16[512,128]{1,0:T(8,128)(2,1)S(1)}, s16[512,128]{1,0:T(8,128)(2,1)S(1)}, u32[]{:S(2)}, u32[]{:S(2)}) collective-permute-start(s16[512,128]{1,0:T(8,128)(2,1)S(1)} %get-tuple-element.19), channel_id=1, source_target_pairs={{0,3},{1,2},{2,1},{3,0},{4,7},{5,6},{6,5},{7,4},{8,15},{9,14},{10,... | collective-permute-start | bytes 393224 | tf_op jit(solution)/shard_map/ppermute | solution.py:175
  29.2 9.3 %collective-permute-start.4 = (s16[512,128]{1,0:T(8,128)(2,1)S(1)}, s16[512,128]{1,0:T(8,128)(2,1)S(1)}, u32[]{:S(2)}, u32[]{:S(2)}) collective-permute-start(s16[512,128]{1,0:T(8,128)(2,1)S(1)} %get-tuple-element.15), channel_id=1, source_target_pairs={{0,0},{1,1},{2,2},{3,3},{4,4},{5,5},{6,6},{7,7},{8,12},{9,13},{10,... | collective-permute-start | bytes 393224 | tf_op jit(solution)/shard_map/ppermute | solution.py:175
  34.9 12.0 %collective-permute-start.13 = (bf16[256,512]{1,0:T(8,128)(2,1)S(1)}, bf16[256,512]{1,0:T(8,128)(2,1)S(1)}, u32[]{:S(2)}, u32[]{:S(2)}) collective-permute-start(bf16[256,512]{1,0:T(8,128)(2,1)S(1)} %get-tuple-element.22), channel_id=1, source_target_pairs={{0,3},{1,2},{2,1},{3,0},{4,7},{5,6},{6,5},{7,4},{8,11},{9,10},{10,... | collective-permute-start | bytes 786440 | tf_op jit(solution)/shard_map/ppermute | solution.py:169
  37.2 11.6 %collective-permute-start.12 = (bf16[256,512]{1,0:T(8,128)(2,1)S(1)}, bf16[256,512]{1,0:T(8,128)(2,1)S(1)}, u32[]{:S(2)}, u32[]{:S(2)}) collective-permute-start(bf16[256,512]{1,0:T(8,128)(2,1)S(1)} %get-tuple-element.21), channel_id=1, source_target_pairs={{0,2},{1,3},{2,0},{3,1},{4,6},{5,7},{6,4},{7,5},{8,10},{9,11},{10,... | collective-permute-start | bytes 786440 | tf_op jit(solution)/shard_map/ppermute | solution.py:169
  37.2 11.9 %collective-permute-start.11 = (bf16[256,512]{1,0:T(8,128)(2,1)S(1)}, bf16[256,512]{1,0:T(8,128)(2,1)S(1)}, u32[]{:S(2)}, u32[]{:S(2)}) collective-permute-start(bf16[256,512]{1,0:T(8,128)(2,1)S(1)} %get-tuple-element.20), channel_id=1, source_target_pairs={{0,1},{1,0},{2,3},{3,2},{4,5},{5,4},{6,7},{7,6},{8,9},{9,8},{10,11... | collective-permute-start | bytes 786440 | tf_op jit(solution)/shard_map/ppermute | solution.py:169
  42.7 7.3 %collective-permute-start.16 = (bf16[384,512]{1,0:T(8,128)(2,1)S(1)}, bf16[384,512]{1,0:T(8,128)(2,1)S(1)}, u32[]{:S(2)}, u32[]{:S(2)}) collective-permute-start(bf16[384,512]{1,0:T(8,128)(2,1)S(1)} %get-tuple-element.27), channel_id=1, source_target_pairs={{0,8},{8,0},{16,24},{24,16},{1,9},{9,1},{17,25},{25,17},{2,10},{10... | collective-permute-start | bytes 1179656 | tf_op jit(solution)/shard_map/ppermute | solution.py:169
  49.1 15.4 %copy-start.4 = (bf16[128,512]{1,0:T(8,128)(2,1)S(1)}, bf16[128,512]{1,0:T(8,128)(2,1)}, u32[]{:S(2)}) copy-start(bf16[128,512]{1,0:T(8,128)(2,1)} %param.6) | copy-start | bytes 393220
  49.3 2.4 %collective-permute-start.14 = (bf16[256,512]{1,0:T(8,128)(2,1)S(1)}, bf16[256,512]{1,0:T(8,128)(2,1)S(1)}, u32[]{:S(2)}, u32[]{:S(2)}) collective-permute-start(bf16[256,512]{1,0:T(8,128)(2,1)S(1)} %add_convert_fusion.1), channel_id=1, source_target_pairs={{0,0},{1,1},{2,2},{3,3},{4,4},{5,5},{6,6},{7,7},{8,12},{9,13},{10,... | collective-permute-start | bytes 786440 | tf_op jit(solution)/shard_map/ppermute | solution.py:175
  50.1 13.6 %collective-permute-start.17 = (bf16[384,512]{1,0:T(8,128)(2,1)S(1)}, bf16[384,512]{1,0:T(8,128)(2,1)S(1)}, u32[]{:S(2)}, u32[]{:S(2)}) collective-permute-start(bf16[384,512]{1,0:T(8,128)(2,1)S(1)} %add_convert_fusion), channel_id=1, source_target_pairs={{0,16},{8,24},{16,0},{24,8},{1,17},{9,25},{17,1},{25,9},{2,18},{10... | collective-permute-start | bytes 1179656 | tf_op jit(solution)/shard_map/ppermute | solution.py:169
  51.6 12.9 %collective-permute-start.15 = (bf16[128,512]{1,0:T(8,128)(2,1)S(1)}, bf16[128,512]{1,0:T(8,128)(2,1)S(1)}, u32[]{:S(2)}, u32[]{:S(2)}) collective-permute-start(bf16[128,512]{1,0:T(8,128)(2,1)S(1)} %slice.9), channel_id=1, source_target_pairs={{0,8},{8,0},{16,24},{24,16},{1,9},{9,1},{17,25},{25,17},{2,10},{10... | collective-permute-start | bytes 393224 | tf_op jit(solution)/shard_map/ppermute | solution.py:169
  63.6 1.9 %collective-permute-start.18 = (bf16[384,512]{1,0:T(8,128)(2,1)S(1)}, bf16[384,512]{1,0:T(8,128)(2,1)S(1)}, u32[]{:S(2)}, u32[]{:S(2)}) collective-permute-start(bf16[384,512]{1,0:T(8,128)(2,1)S(1)} %add_convert_fusion), channel_id=1, source_target_pairs={{0,8},{8,0},{16,24},{24,16},{1,9},{9,1},{17,25},{25,17},{2,10},{10... | collective-permute-start | bytes 1179656 | tf_op jit(solution)/shard_map/ppermute | solution.py:169
  63.7 2.2 %collective-permute-start.19 = (bf16[384,512]{1,0:T(8,128)(2,1)S(1)}, bf16[384,512]{1,0:T(8,128)(2,1)S(1)}, u32[]{:S(2)}, u32[]{:S(2)}) collective-permute-start(bf16[384,512]{1,0:T(8,128)(2,1)S(1)} %collective-permute-done.17), channel_id=1, source_target_pairs={{0,8},{8,0},{16,24},{24,16},{1,9},{9,1},{17,25},{25,17},{2,10},{10... | collective-permute-start | bytes 1179656 | tf_op jit(solution)/shard_map/ppermute | solution.py:169
  (1 other events, 0.7 us)

commit v3 on v1

v3 whole, which is shorter than its diff:
```python
import functools
import math

import jax
import jax.numpy as jnp
from jax import lax
from jax.experimental import pallas as pl
from jax.experimental.pallas import tpu as pltpu
from jax.sharding import PartitionSpec as P

CONFIDENCE = 40.0
STEPS = 65535.0
OFFSET = 32768
BF = jnp.bfloat16
F32 = jnp.float32

VM = pl.BlockSpec(memory_space=pltpu.VMEM)
SM = pl.BlockSpec(memory_space=pltpu.SMEM)
ANY = pl.BlockSpec(memory_space=pl.ANY)
ROWS = (((1,), (1,)), ((), ()))
COLS = (((0,), (0,)), ((), ()))


def call(body, outs, in_specs, flops, moved, scratch=(), mib=24):
    return pl.pallas_call(
        body,
        out_shape=outs,
        in_specs=in_specs,
        out_specs=jax.tree.map(lambda _: VM, outs),
        scratch_shapes=scratch,
        compiler_params=pltpu.CompilerParams(vmem_limit_bytes=mib << 20),
        cost_estimate=pl.CostEstimate(flops=flops, bytes_accessed=moved, transcendentals=0),
    )


def spread_body(n, limit, pair_ref, count_ref, rate_ref, *rest):
    outs, where = rest[: n // 2], rest[n // 2]
    me, (blocks, width, _) = lax.axis_index("row"), rate_ref.shape
    for s in range(n * limit):
        where[s] = -1
    for i in range(blocks):
        @pl.when(i < count_ref[0])
        def _():
            where[pair_ref[1, i]] = i
    for j, out_ref in enumerate(outs):
        for side in range(2):
            for c in range(limit):
                i = where[(me ^ (2 * j + side)) * limit + c]
                rate = rate_ref[jnp.maximum(i, 0)]
                code = jnp.where(i >= 0, (rate * STEPS + 0.5).astype(jnp.int32), 0) - OFFSET
                at = (side * limit + c) * width
                out_ref[at : at + width] = code.astype(jnp.int16)


def halves_body(*refs):
    out_ref = refs[-1]
    for j, ref in enumerate(refs[:-1]):
        rows = ref.shape[0] // 2
        out_ref[j * rows : (j + 1) * rows] = ref[rows:]


def gram_body(item_ref, gram_ref, copy_ref, sem):
    copy = pltpu.make_async_copy(item_ref, copy_ref, sem)
    copy.start()
    copy.wait()
    items = copy_ref[...]
    gram_ref[...] = lax.dot_general(items, items, COLS, preferred_element_type=F32).astype(BF)


def score_body(m, more, item_ref, gram_ref, *rest):
    users, rest = rest[:m], rest[m:]
    total, rest = (rest[0][...], rest[1:]) if more else (None, rest)
    score_ref, user_ref, last_ref, all_ref = rest
    width = users[0].shape[0]
    for j in range(m):
        all_ref[j * width : (j + 1) * width] = users[j][...]
    every = all_ref[...]
    score_ref[...] = lax.dot_general(every, item_ref[...], ROWS, preferred_element_type=F32)
    user_ref[...] = jnp.dot(every, gram_ref[...], preferred_element_type=F32)
    cross = lax.dot_general(every, every, COLS, preferred_element_type=F32)
    if more:
        cross = (total + cross).astype(BF)
        last_ref[...] = jnp.dot(item_ref[...], cross, preferred_element_type=F32)
    else:
        last_ref[...] = cross


def error_body(n, limit, width, send_ref, item_ref, near_ref, far_ref, near_gram, far_gram, part_ref, *rest):
    far = n // 2
    users, codes, outs = rest[:n], rest[n : n + far + 1], rest[n + far + 1 : 2 * n + far + 1]
    mine_ref, other_ref, sum_ref = rest[2 * n + far + 1 :]
    me = lax.axis_index("row")
    core = lax.axis_index("grp") % 2
    sum_ref[...] = part_ref[...]
    for k in [*range(far, n), *range(far)]:
        left = users[k][...]
        score_ref, gram_ref, row = (near_ref, near_gram, k) if k < far else (far_ref, far_gram, k - far)
        row = slice(row * width, (row + 1) * width)
        errors, rights, spots = [], [], []
        for c in range(limit):
            at = pl.ds(pl.multiple_of(send_ref[c, me ^ k] * width, width), width)
            code_ref, place = (codes[k // 2], c) if k % 2 == 0 else (codes[far], k // 2 * limit + c)
            code = code_ref[place * width : (place + 1) * width].astype(jnp.int32) + OFFSET
            weighted = CONFIDENCE * (code.astype(F32) * (1.0 / STEPS))
            error = weighted * score_ref[row, at] - 1.0 - weighted
            errors.append(jnp.where(code > 0, error, 0.0).astype(BF))
            rights.append(item_ref[at])
            spots.append(at)
        error = jnp.concatenate(errors, axis=1)
        total = gram_ref[row] + jnp.dot(
            error, jnp.concatenate(rights), preferred_element_type=F32
        )
        outs[k][...] = total.astype(outs[k].dtype)
        terms = lax.dot_general(error, left, COLS, preferred_element_type=F32)
        for c, at in enumerate(spots):
            sum_ref[at] += terms[c * width : (c + 1) * width].astype(BF).astype(F32)
    half = mine_ref.shape[0]
    other_ref[...] = sum_ref[pl.ds(pl.multiple_of((1 - core) * half, half), half)].astype(BF)
    mine_ref[...] = sum_ref[pl.ds(pl.multiple_of(core * half, half), half)]


def swap(x, axis, k):
    return lax.ppermute(x, axis, [(i, i ^ k) for i in range(lax.axis_size(axis))])


def shards(users, items, ratings, pair_list, send_list, counts):
    n = lax.axis_size("row")
    grp_n = lax.axis_size("grp")
    width = ratings.shape[2]
    factors = users.shape[1]
    limit = send_list.shape[2]
    item_rows = items.shape[0]
    user_rows = users.shape[0]
    far = n // 2
    total_users = user_rows * grp_n * n
    total_items = item_rows * n
    sds = jax.ShapeDtypeStruct

    pairs = jnp.swapaxes(pair_list[0], 0, 1)
    sends = jnp.swapaxes(send_list[0], 0, 1)

    over = swap(users, "row", far)
    codes = call(
        functools.partial(spread_body, n, limit),
        [sds((2 * limit * width, width), jnp.int16)] * far,
        [SM, SM, VM],
        0,
        ratings.size * 6,
        [pltpu.SMEM((n * limit,), jnp.int32)],
    )(pairs, counts, ratings[0])
    blocks = [users] + [swap(users, "row", k) for k in range(1, far)]
    blocks[1], *late = lax.optimization_barrier((blocks[1], *codes[1 : far // 2]))
    blocks += [over] + [swap(over, "row", k) for k in range(1, far)]
    along = {j: swap(codes[j], "row", 2 * j) for j in range(far // 2, far)}
    along.update({j: swap(late[j - 1], "row", 2 * j) for j in range(1, far // 2)})
    along = [codes[0]] + [along[j] for j in range(1, far)]
    passed = call(
        halves_body,
        sds((far * limit * width, width), jnp.int16),
        [VM] * far,
        2 * 10**10,
        4 * far * limit * width * width,
    )(*along)
    codes = [*along, swap(passed, "row", 1)]

    cross_flops = 2 * user_rows * factors**2
    item_flops = 2 * item_rows * factors**2
    score_flops = 2 * user_rows * factors * item_rows
    gram, rows = call(
        gram_body,
        [sds((factors, factors), BF), sds((item_rows, factors), BF)],
        [ANY],
        item_flops,
        items.size * 4,
        [pltpu.SemaphoreType.DMA],
    )(items)
    score_out = [sds((far * user_rows, item_rows), F32), sds((far * user_rows, factors), F32)]
    every = [pltpu.VMEM((far * user_rows, factors), BF)]
    near_score, near_gram, cross = call(
        functools.partial(score_body, far, False),
        score_out + [sds((factors, factors), F32)],
        [VM] * (2 + far),
        40 * far * (score_flops + 2 * cross_flops),
        4 << 20,
        every,
    )(rows, gram, *blocks[:far])
    far_score, far_gram, item_part = call(
        functools.partial(score_body, far, True),
        score_out + [sds((item_rows, factors), F32)],
        [VM] * (3 + far),
        40 * (far * (score_flops + 2 * cross_flops) + item_flops),
        4 << 20,
        every,
    )(rows, gram, *blocks[far:], cross)
    half = item_rows // 2
    *parts, mine, other = call(
        functools.partial(error_body, n, limit, width),
        [sds((user_rows, factors), F32 if k in (0, far) else BF) for k in range(n)]
        + [sds((half, factors), F32), sds((half, factors), BF)],
        [SM] + [VM] * (7 + n + far),
        8 * n * limit * user_rows * factors * width,
        8 << 20,
        [pltpu.VMEM((item_rows, factors), F32)],
    )(sends, rows, near_score, far_score, near_gram, far_gram, item_part, *blocks, *codes)

    across = parts[far]
    for k in range(1, far):
        across += swap(parts[far + k], "row", k).astype(F32)
    user_sum = parts[0]
    for k in range(1, far):
        user_sum += swap(parts[k], "row", k).astype(F32)
    user_sum += swap(across.astype(BF), "row", far).astype(F32)
    new_users = users.astype(F32) - 4.0 / math.sqrt(total_items) * user_sum

    core = lax.axis_index("grp") % 2
    pair_sum = mine + swap(other, "grp", 1).astype(F32)
    if grp_n == 4:
        here = pair_sum.astype(BF)
        there = swap(here, "grp", 2)
        first = here.astype(F32) + there.astype(F32)
        second = swap(here, "grp", 1).astype(F32) + swap(there, "grp", 1).astype(F32)
    else:
        peers = [list(range(c, grp_n, 2)) for c in range(2)]
        first = lax.psum(pair_sum, "grp", axis_index_groups=peers)
        second = swap(first, "grp", 1)
    item_sum = jnp.where(
        core == 0, jnp.concatenate([first, second]), jnp.concatenate([second, first])
    )
    new_items = rows.astype(F32) - 8.0 / math.sqrt(total_users) * item_sum
    return (new_users, new_items)


def solution(mesh):
    in_specs = (
        P(("grp", "row"), None),
        P("row", None),
        P(("grp", "row"), None, None, None),
        P(("grp", "row"), None, None),
        P(("grp", "row"), None, None),
        P(("grp", "row")),
    )
    out_specs = (P(("grp", "row"), None), P("row", None))
    return jax.shard_map(shards, mesh=mesh, in_specs=in_specs, out_specs=out_specs, check_vma=False)
```

time: 59.7 us -> 56.9 us (0.953)
  starting transfers between devices: 36.7 us -> 28 us
  waiting for transfers between devices: 7.53 us -> 15.4 us
  local copies, waits for them, and re-layouts: 3.92 us -> 3.03 us
  Pallas kernels: 6.92 us -> 6.17 us
    ppermute x25 -> x22, starting transfers between devices: 36.7 us -> 28 us  [swap(): lax.ppermute(x, axis, [(i, i ^ k) for i in range(lax.axis_size(axis))])]
    ppermute x25 -> x22, waiting for transfers between devices: 7.53 us -> 15.4 us  [swap(): lax.ppermute(x, axis, [(i, i ^ k) for i in range(lax.axis_size(axis))])]
    unnamed x12 -> x10, local copies, waits for them, and re-layouts: 3.92 us -> 3.03 us
    pallas_call x3 -> x5, Pallas kernels: 4.83 us -> 4.32 us  [the longest x1 1.65 us: shards(): call(functools.partial(score_body, far, True), score_out + [sds((item_row...]
  transfers between devices with their start and end apart: 25 -> 22, of which waited for: 4 -> 8; matrix products, arithmetic and copies ran while one was open for 2% -> 2% of each run, Pallas kernels for 8% -> 8%
where the time goes in v3:
time: 56.9 us; the launch traced here: 56.7 us
  starting transfers between devices  28 us (49%)
  waiting for transfers between devices  15.4 us (27%)
  Pallas kernels  6.17 us (11%)
  local copies, waits for them, and re-layouts  3.03 us (5%)
  other arithmetic  2.71 us (5%)
  between operations  1.42 us (2%)
    ppermute x22, starting transfers between devices, swap(): lax.ppermute(x, axis, [(i, i ^ k) for i in range(lax.axis_size(axis))])  28 us
    ppermute x22, waiting for transfers between devices, swap(): lax.ppermute(x, axis, [(i, i ^ k) for i in range(lax.axis_size(axis))])  15.4 us
    unnamed x10, local copies, waits for them, and re-layouts  3.03 us
    pallas_call x1, Pallas kernels, shards(): call(functools.partial(error_body, n, limit, width), [sds((user_rows, fac...  1.86 us
    pallas_call x1, Pallas kernels, shards(): call(functools.partial(score_body, far, True), score_out + [sds((item_row...  1.65 us
    sub x1, other arithmetic, shards(): new_items = rows.astype(F32) - 8.0 / math.sqrt(total_users) * item_sum  1.5 us
    pallas_call x1, Pallas kernels, shards(): call(functools.partial(score_body, far, False), score_out + [sds((factors...  1.15 us
  transfers between devices with their start and end apart: 22, of which 8 were waited for; matrix products, arithmetic and copies ran while one was open for 2% of the time, Pallas kernels for 8%

profile of v3, /device:TPU:0, one launch (start us, length us, event | category | flops | bytes accessed | tf_op | source)
XLA Modules:
  0.0 56.7 jit_solution(15226994152490582484)
XLA Ops:
  0.6 3.0 %collective-permute-start = (bf16[128,512]{1,0:T(8,128)(2,1)}, bf16[128,512]{1,0:T(8,128)(2,1)S(1)}, u32[]{:S(2)}, u32[]{:S(2)}) collective-permute-start(bf16[128,512]{1,0:T(8,128)(2,1)} %rest_0_.3), channel_id=1, source_target_pairs={{0,1},{1,0},{2,3},{3,2},{4,5},{5,4},{6,7},{7,6},{8,9},{9,8},{10,11... | collective-permute-start | bytes 393224 | tf_op jit(solution)/shard_map/ppermute | solution.py:123
  3.7 1.6 %collective-permute-start.1 = (bf16[128,512]{1,0:T(8,128)(2,1)}, bf16[128,512]{1,0:T(8,128)(2,1)S(1)}, u32[]{:S(2)}, u32[]{:S(2)}) collective-permute-start(bf16[128,512]{1,0:T(8,128)(2,1)} %rest_0_.3), channel_id=1, source_target_pairs={{0,2},{1,3},{2,0},{3,1},{4,6},{5,7},{6,4},{7,5},{8,10},{9,11},{10,... | collective-permute-start | bytes 393224 | tf_op jit(solution)/shard_map/ppermute | solution.py:123
  5.2 2.6 %collective-permute-start.3 = (bf16[128,512]{1,0:T(8,128)(2,1)}, bf16[128,512]{1,0:T(8,128)(2,1)S(1)}, u32[]{:S(2)}, u32[]{:S(2)}) collective-permute-start(bf16[128,512]{1,0:T(8,128)(2,1)} %rest_0_.3), channel_id=1, source_target_pairs={{0,4},{1,5},{2,6},{3,7},{4,0},{5,1},{6,2},{7,3},{8,12},{9,13},{10,... | collective-permute-start | bytes 393224 | tf_op jit(solution)/shard_map/ppermute | solution.py:123
  8.9 1.2 %copy-done = f32[1,16,128,128]{3,2,1,0:T(8,128)S(1)} copy-done((f32[1,16,128,128]{3,2,1,0:T(8,128)S(1)}, f32[1,16,128,128]{3,2,1,0:T(8,128)}, u32[]{:S(2)}) %copy-start) | copy-done | bytes 1048600
  13.5 4.0 %collective-permute-start.9 = (s16[512,128]{1,0:T(8,128)(2,1)S(1)}, s16[512,128]{1,0:T(8,128)(2,1)S(1)}, u32[]{:S(2)}, u32[]{:S(2)}) collective-permute-start(s16[512,128]{1,0:T(8,128)(2,1)S(1)} %get-tuple-element.39), channel_id=1, source_target_pairs={{0,6},{1,7},{2,4},{3,5},{4,2},{5,3},{6,0},{7,1},{8,14},{9,15},{10,... | collective-permute-start | bytes 393224 | tf_op jit(solution)/shard_map/ppermute | solution.py:123
  17.5 1.6 %collective-permute-start.4 = (bf16[128,512]{1,0:T(8,128)(2,1)S(1)}, bf16[128,512]{1,0:T(8,128)(2,1)S(1)}, u32[]{:S(2)}, u32[]{:S(2)}) collective-permute-start(bf16[128,512]{1,0:T(8,128)(2,1)S(1)} %collective-permute-done.3.rest_0_.rest_4_), channel_id=1, source_target_pairs={{0,1},{1,0},{2,3},{3,2},{4,5},{5,4},{6,7},{7,6},{8,9},{9,8},{10,11... | collective-permute-start | bytes 393224 | tf_op jit(solution)/shard_map/ppermute | solution.py:123
  19.1 2.0 %collective-permute-start.5 = (bf16[128,512]{1,0:T(8,128)(2,1)S(1)}, bf16[128,512]{1,0:T(8,128)(2,1)S(1)}, u32[]{:S(2)}, u32[]{:S(2)}) collective-permute-start(bf16[128,512]{1,0:T(8,128)(2,1)S(1)} %collective-permute-done.3.rest_0_.rest_4_), channel_id=1, source_target_pairs={{0,2},{1,3},{2,0},{3,1},{4,6},{5,7},{6,4},{7,5},{8,10},{9,11},{10,... | collective-permute-start | bytes 393224 | tf_op jit(solution)/shard_map/ppermute | solution.py:123
  22.2 1.8 %collective-permute-done.8.refs_2_.rest_10_ = s16[512,128]{1,0:T(8,128)(2,1)S(1)} collective-permute-done((s16[512,128]{1,0:T(8,128)(2,1)S(1)}, s16[512,128]{1,0:T(8,128)(2,1)S(1)}, u32[]{:S(2)}, u32[]{:S(2)}) %collective-permute-start.8) | collective-permute-done | bytes 131104 | tf_op jit(solution)/shard_map/ppermute | solution.py:123
  24.1 2.0 %collective-permute-done.7.refs_1_.rest_9_ = s16[512,128]{1,0:T(8,128)(2,1)S(1)} collective-permute-done((s16[512,128]{1,0:T(8,128)(2,1)S(1)}, s16[512,128]{1,0:T(8,128)(2,1)S(1)}, u32[]{:S(2)}, u32[]{:S(2)}) %collective-permute-start.7) | collective-permute-done | bytes 131104 | tf_op jit(solution)/shard_map/ppermute | solution.py:123
  26.1 1.3 %collective-permute-start.10 = (s16[1024,128]{1,0:T(8,128)(2,1)S(1)}, s16[1024,128]{1,0:T(8,128)(2,1)S(1)}, u32[]{:S(2)}, u32[]{:S(2)}) collective-permute-start(s16[1024,128]{1,0:T(8,128)(2,1)S(1)} %shard_map.81), channel_id=1, source_target_pairs={{0,1},{1,0},{2,3},{3,2},{4,5},{5,4},{6,7},{7,6},{8,9},{9,8},{10,11... | collective-permute-start | bytes 786440 | tf_op jit(solution)/shard_map/ppermute | solution.py:123
  27.4 1.4 %collective-permute-done.5.rest_2_.rest_6_ = bf16[128,512]{1,0:T(8,128)(2,1)S(1)} collective-permute-done((bf16[128,512]{1,0:T(8,128)(2,1)S(1)}, bf16[128,512]{1,0:T(8,128)(2,1)S(1)}, u32[]{:S(2)}, u32[]{:S(2)}) %collective-permute-start.5) | collective-permute-done | bytes 131104 | tf_op jit(solution)/shard_map/ppermute | solution.py:123
  28.9 2.2 %collective-permute-done.6.rest_3_.rest_7_ = bf16[128,512]{1,0:T(8,128)(2,1)S(1)} collective-permute-done((bf16[128,512]{1,0:T(8,128)(2,1)S(1)}, bf16[128,512]{1,0:T(8,128)(2,1)S(1)}, u32[]{:S(2)}, u32[]{:S(2)}) %collective-permute-start.6) | collective-permute-done | bytes 131104 | tf_op jit(solution)/shard_map/ppermute | solution.py:123
  31.1 1.6 %shard_map.80 = (f32[512,768]{1,0:T(8,128)S(1)}, f32[512,512]{1,0:T(8,128)S(1)}, f32[768,512]{1,0:T(8,128)S(1)}) custom-call(bf16[768,512]{1,0:T(8,128)(2,1)S(1)} %get-tuple-element.26.item_ref, bf16[512,512]{1,0:T(8,128)(2,1)S(1)} %get-tuple-element.27.gram_ref, bf16[128,512]{1,0:T(8,128)(2,1)S(1)} %collective-permute-done.3.rest_0_.rest_4_, ...), custom_call_target="tpu_custom_call" | custom-call | flops 53687091200 | bytes 4194304 | tf_op jit(solution)/shard_map/pallas_call | solution.py:187
  33.8 1.9 %shard_map.82 = (f32[128,512]{1,0:T(8,128)S(1)}, bf16[128,512]{1,0:T(8,128)(2,1)S(1)}, bf16[128,512]{1,0:T(8,128)(2,1)S(1)}, bf16[128,512]{1,0:T(8,128)(2,1)S(1)...) custom-call(s32[2,8]{1,0:T(2,128)S(1)} %bitcast.9, ...), custom_call_target="tpu_custom_call" | custom-call | flops 1073741824 | bytes 8388608 | tf_op jit(solution)/shard_map/pallas_call | solution.py:196
  36.6 1.5 %collective-permute-start.15 = (bf16[128,512]{1,0:T(8,128)(2,1)S(1)}, bf16[128,512]{1,0:T(8,128)(2,1)S(1)}, u32[]{:S(2)}, u32[]{:S(2)}) collective-permute-start(bf16[128,512]{1,0:T(8,128)(2,1)S(1)} %get-tuple-element.46), channel_id=1, source_target_pairs={{0,2},{1,3},{2,0},{3,1},{4,6},{5,7},{6,4},{7,5},{8,10},{9,11},{10,... | collective-permute-start | bytes 393224 | tf_op jit(solution)/shard_map/ppermute | solution.py:123
  38.0 1.3 %collective-permute-start.16 = (bf16[128,512]{1,0:T(8,128)(2,1)S(1)}, bf16[128,512]{1,0:T(8,128)(2,1)S(1)}, u32[]{:S(2)}, u32[]{:S(2)}) collective-permute-start(bf16[128,512]{1,0:T(8,128)(2,1)S(1)} %get-tuple-element.47), channel_id=1, source_target_pairs={{0,3},{1,2},{2,1},{3,0},{4,7},{5,6},{6,5},{7,4},{8,11},{9,10},{10,... | collective-permute-start | bytes 393224 | tf_op jit(solution)/shard_map/ppermute | solution.py:123
  39.4 1.5 %collective-permute-start.19 = (bf16[384,512]{1,0:T(8,128)(2,1)S(1)}, bf16[384,512]{1,0:T(8,128)(2,1)S(1)}, u32[]{:S(2)}, u32[]{:S(2)}) collective-permute-start(bf16[384,512]{1,0:T(8,128)(2,1)S(1)} %add_convert_fusion), channel_id=1, source_target_pairs={{0,16},{8,24},{16,0},{24,8},{1,17},{9,25},{17,1},{25,9},{2,18},{10... | collective-permute-start | bytes 1179656 | tf_op jit(solution)/shard_map/ppermute | solution.py:123
  41.7 1.5 %collective-permute-start.12 = (bf16[128,512]{1,0:T(8,128)(2,1)S(1)}, bf16[128,512]{1,0:T(8,128)(2,1)S(1)}, u32[]{:S(2)}, u32[]{:S(2)}) collective-permute-start(bf16[128,512]{1,0:T(8,128)(2,1)S(1)} %get-tuple-element.42), channel_id=1, source_target_pairs={{0,2},{1,3},{2,0},{3,1},{4,6},{5,7},{6,4},{7,5},{8,10},{9,11},{10,... | collective-permute-start | bytes 393224 | tf_op jit(solution)/shard_map/ppermute | solution.py:123
  43.2 1.7 %collective-permute-start.13 = (bf16[128,512]{1,0:T(8,128)(2,1)S(1)}, bf16[128,512]{1,0:T(8,128)(2,1)S(1)}, u32[]{:S(2)}, u32[]{:S(2)}) collective-permute-start(bf16[128,512]{1,0:T(8,128)(2,1)S(1)} %get-tuple-element.43), channel_id=1, source_target_pairs={{0,3},{1,2},{2,1},{3,0},{4,7},{5,6},{6,5},{7,4},{8,11},{9,10},{10,... | collective-permute-start | bytes 393224 | tf_op jit(solution)/shard_map/ppermute | solution.py:123
  45.0 1.5 %collective-permute-done.16 = bf16[128,512]{1,0:T(8,128)(2,1)S(1)} collective-permute-done((bf16[128,512]{1,0:T(8,128)(2,1)S(1)}, bf16[128,512]{1,0:T(8,128)(2,1)S(1)}, u32[]{:S(2)}, u32[]{:S(2)}) %collective-permute-start.16) | collective-permute-done | bytes 131104 | tf_op jit(solution)/shard_map/ppermute | solution.py:123
  46.5 2.3 %collective-permute-start.17 = (bf16[128,512]{1,0:T(8,128)(2,1)S(1)}, bf16[128,512]{1,0:T(8,128)(2,1)S(1)}, u32[]{:S(2)}, u32[]{:S(2)}) collective-permute-start(bf16[128,512]{1,0:T(8,128)(2,1)S(1)} %add_convert_fusion.1), channel_id=1, source_target_pairs={{0,4},{1,5},{2,6},{3,7},{4,0},{5,1},{6,2},{7,3},{8,12},{9,13},{10,... | collective-permute-start | bytes 393224 | tf_op jit(solution)/shard_map/ppermute | solution.py:123
  48.9 1.3 %collective-permute-done.19 = bf16[384,512]{1,0:T(8,128)(2,1)S(1)} collective-permute-done((bf16[384,512]{1,0:T(8,128)(2,1)S(1)}, bf16[384,512]{1,0:T(8,128)(2,1)S(1)}, u32[]{:S(2)}, u32[]{:S(2)}) %collective-permute-start.19) | collective-permute-done | bytes 393248 | tf_op jit(solution)/shard_map/ppermute | solution.py:123
  50.1 4.0 %collective-permute-done.13 = bf16[128,512]{1,0:T(8,128)(2,1)S(1)} collective-permute-done((bf16[128,512]{1,0:T(8,128)(2,1)S(1)}, bf16[128,512]{1,0:T(8,128)(2,1)S(1)}, u32[]{:S(2)}, u32[]{:S(2)}) %collective-permute-start.13) | collective-permute-done | bytes 131104 | tf_op jit(solution)/shard_map/ppermute | solution.py:123
  55.2 1.5 %fusion.1 = f32[768,512]{1,0:T(8,128)} fusion(f32[384,512]{1,0:T(8,128)S(1)} %convert_add_fusion, f32[384,512]{1,0:T(8,128)S(1)} %convert_add_fusion.1, bf16[768,512]{1,0:T(8,128)(2,1)S(1)} %get-tuple-element.26.item_ref, pred[]{:T(512)S(6)} %eq.5), kind=kLoop, calls=%fused_computation.2 | loop fusion | flops 2359296 | bytes 3932161 | tf_op jit(solution)/shard_map/sub | solution.py:229
  (42 shorter events, 8.9 us)
Async XLA Ops:
  0.6 12.9 %collective-permute-start = (bf16[128,512]{1,0:T(8,128)(2,1)}, bf16[128,512]{1,0:T(8,128)(2,1)S(1)}, u32[]{:S(2)}, u32[]{:S(2)}) collective-permute-start(bf16[128,512]{1,0:T(8,128)(2,1)} %rest_0_.3), channel_id=1, source_target_pairs={{0,1},{1,0},{2,3},{3,2},{4,5},{5,4},{6,7},{7,6},{8,9},{9,8},{10,11... | collective-permute-start | bytes 393224 | tf_op jit(solution)/shard_map/ppermute | solution.py:123
  3.7 13.9 %collective-permute-start.1 = (bf16[128,512]{1,0:T(8,128)(2,1)}, bf16[128,512]{1,0:T(8,128)(2,1)S(1)}, u32[]{:S(2)}, u32[]{:S(2)}) collective-permute-start(bf16[128,512]{1,0:T(8,128)(2,1)} %rest_0_.3), channel_id=1, source_target_pairs={{0,2},{1,3},{2,0},{3,1},{4,6},{5,7},{6,4},{7,5},{8,10},{9,11},{10,... | collective-permute-start | bytes 393224 | tf_op jit(solution)/shard_map/ppermute | solution.py:123
  5.2 12.3 %collective-permute-start.3 = (bf16[128,512]{1,0:T(8,128)(2,1)}, bf16[128,512]{1,0:T(8,128)(2,1)S(1)}, u32[]{:S(2)}, u32[]{:S(2)}) collective-permute-start(bf16[128,512]{1,0:T(8,128)(2,1)} %rest_0_.3), channel_id=1, source_target_pairs={{0,4},{1,5},{2,6},{3,7},{4,0},{5,1},{6,2},{7,3},{8,12},{9,13},{10,... | collective-permute-start | bytes 393224 | tf_op jit(solution)/shard_map/ppermute | solution.py:123
  7.8 11.3 %collective-permute-start.2 = (bf16[128,512]{1,0:T(8,128)(2,1)}, bf16[128,512]{1,0:T(8,128)(2,1)S(1)}, u32[]{:S(2)}, u32[]{:S(2)}) collective-permute-start(bf16[128,512]{1,0:T(8,128)(2,1)} %rest_0_.3), channel_id=1, source_target_pairs={{0,3},{1,2},{2,1},{3,0},{4,7},{5,6},{6,5},{7,4},{8,11},{9,10},{10,... | collective-permute-start | bytes 393224 | tf_op jit(solution)/shard_map/ppermute | solution.py:123
  10.8 10.3 %copy-start.1 = (bf16[128,512]{1,0:T(8,128)(2,1)S(1)}, bf16[128,512]{1,0:T(8,128)(2,1)}, u32[]{:S(2)}) copy-start(bf16[128,512]{1,0:T(8,128)(2,1)} %rest_0_.3) | copy-start | bytes 393220
  11.6 12.4 %collective-permute-start.8 = (s16[512,128]{1,0:T(8,128)(2,1)S(1)}, s16[512,128]{1,0:T(8,128)(2,1)S(1)}, u32[]{:S(2)}, u32[]{:S(2)}) collective-permute-start(s16[512,128]{1,0:T(8,128)(2,1)S(1)} %get-tuple-element.38), channel_id=1, source_target_pairs={{0,4},{1,5},{2,6},{3,7},{4,0},{5,1},{6,2},{7,3},{8,12},{9,13},{10,... | collective-permute-start | bytes 393224 | tf_op jit(solution)/shard_map/ppermute | solution.py:123
  13.5 10.6 %collective-permute-start.9 = (s16[512,128]{1,0:T(8,128)(2,1)S(1)}, s16[512,128]{1,0:T(8,128)(2,1)S(1)}, u32[]{:S(2)}, u32[]{:S(2)}) collective-permute-start(s16[512,128]{1,0:T(8,128)(2,1)S(1)} %get-tuple-element.39), channel_id=1, source_target_pairs={{0,6},{1,7},{2,4},{3,5},{4,2},{5,3},{6,0},{7,1},{8,14},{9,15},{10,... | collective-permute-start | bytes 393224 | tf_op jit(solution)/shard_map/ppermute | solution.py:123
  17.5 8.6 %collective-permute-start.7 = (s16[512,128]{1,0:T(8,128)(2,1)S(1)}, s16[512,128]{1,0:T(8,128)(2,1)S(1)}, u32[]{:S(2)}, u32[]{:S(2)}) collective-permute-start(s16[512,128]{1,0:T(8,128)(2,1)S(1)} %get-tuple-element.37), channel_id=1, source_target_pairs={{0,2},{1,3},{2,0},{3,1},{4,6},{5,7},{6,4},{7,5},{8,10},{9,11},{10,... | collective-permute-start | bytes 393224 | tf_op jit(solution)/shard_map/ppermute | solution.py:123
  17.5 9.9 %collective-permute-start.4 = (bf16[128,512]{1,0:T(8,128)(2,1)S(1)}, bf16[128,512]{1,0:T(8,128)(2,1)S(1)}, u32[]{:S(2)}, u32[]{:S(2)}) collective-permute-start(bf16[128,512]{1,0:T(8,128)(2,1)S(1)} %collective-permute-done.3.rest_0_.rest_4_), channel_id=1, source_target_pairs={{0,1},{1,0},{2,3},{3,2},{4,5},{5,4},{6,7},{7,6},{8,9},{9,8},{10,11... | collective-permute-start | bytes 393224 | tf_op jit(solution)/shard_map/ppermute | solution.py:123
  19.1 9.8 %collective-permute-start.5 = (bf16[128,512]{1,0:T(8,128)(2,1)S(1)}, bf16[128,512]{1,0:T(8,128)(2,1)S(1)}, u32[]{:S(2)}, u32[]{:S(2)}) collective-permute-start(bf16[128,512]{1,0:T(8,128)(2,1)S(1)} %collective-permute-done.3.rest_0_.rest_4_), channel_id=1, source_target_pairs={{0,2},{1,3},{2,0},{3,1},{4,6},{5,7},{6,4},{7,5},{8,10},{9,11},{10,... | collective-permute-start | bytes 393224 | tf_op jit(solution)/shard_map/ppermute | solution.py:123
  24.1 7.0 %collective-permute-start.6 = (bf16[128,512]{1,0:T(8,128)(2,1)S(1)}, bf16[128,512]{1,0:T(8,128)(2,1)S(1)}, u32[]{:S(2)}, u32[]{:S(2)}) collective-permute-start(bf16[128,512]{1,0:T(8,128)(2,1)S(1)} %collective-permute-done.3.rest_0_.rest_4_), channel_id=1, source_target_pairs={{0,3},{1,2},{2,1},{3,0},{4,7},{5,6},{6,5},{7,4},{8,11},{9,10},{10,... | collective-permute-start | bytes 393224 | tf_op jit(solution)/shard_map/ppermute | solution.py:123
  26.1 7.7 %collective-permute-start.10 = (s16[1024,128]{1,0:T(8,128)(2,1)S(1)}, s16[1024,128]{1,0:T(8,128)(2,1)S(1)}, u32[]{:S(2)}, u32[]{:S(2)}) collective-permute-start(s16[1024,128]{1,0:T(8,128)(2,1)S(1)} %shard_map.81), channel_id=1, source_target_pairs={{0,1},{1,0},{2,3},{3,2},{4,5},{5,4},{6,7},{7,6},{8,9},{9,8},{10,11... | collective-permute-start | bytes 786440 | tf_op jit(solution)/shard_map/ppermute | solution.py:123
  31.1 2.7 %copy-start.3 = (s32[1,8,2]{1,2,0:T(2,128)S(1)}, s32[1,8,2]{1,2,0:T(2,128)}, u32[]{:S(2)}) copy-start(s32[1,8,2]{1,2,0:T(2,128)} %param.10) | copy-start | bytes 196
  35.7 3.6 %collective-permute-start.18 = (bf16[384,512]{1,0:T(8,128)(2,1)S(1)}, bf16[384,512]{1,0:T(8,128)(2,1)S(1)}, u32[]{:S(2)}, u32[]{:S(2)}) collective-permute-start(bf16[384,512]{1,0:T(8,128)(2,1)S(1)} %get-tuple-element.49), channel_id=1, source_target_pairs={{0,8},{8,0},{16,24},{24,16},{1,9},{9,1},{17,25},{25,17},{2,10},{10... | collective-permute-start | bytes 1179656 | tf_op jit(solution)/shard_map/ppermute | solution.py:123
  35.7 6.0 %collective-permute-start.14 = (bf16[128,512]{1,0:T(8,128)(2,1)S(1)}, bf16[128,512]{1,0:T(8,128)(2,1)S(1)}, u32[]{:S(2)}, u32[]{:S(2)}) collective-permute-start(bf16[128,512]{1,0:T(8,128)(2,1)S(1)} %get-tuple-element.45), channel_id=1, source_target_pairs={{0,1},{1,0},{2,3},{3,2},{4,5},{5,4},{6,7},{7,6},{8,9},{9,8},{10,11... | collective-permute-start | bytes 393224 | tf_op jit(solution)/shard_map/ppermute | solution.py:123
  36.6 6.7 %collective-permute-start.15 = (bf16[128,512]{1,0:T(8,128)(2,1)S(1)}, bf16[128,512]{1,0:T(8,128)(2,1)S(1)}, u32[]{:S(2)}, u32[]{:S(2)}) collective-permute-start(bf16[128,512]{1,0:T(8,128)(2,1)S(1)} %get-tuple-element.46), channel_id=1, source_target_pairs={{0,2},{1,3},{2,0},{3,1},{4,6},{5,7},{6,4},{7,5},{8,10},{9,11},{10,... | collective-permute-start | bytes 393224 | tf_op jit(solution)/shard_map/ppermute | solution.py:123
  38.0 8.4 %collective-permute-start.16 = (bf16[128,512]{1,0:T(8,128)(2,1)S(1)}, bf16[128,512]{1,0:T(8,128)(2,1)S(1)}, u32[]{:S(2)}, u32[]{:S(2)}) collective-permute-start(bf16[128,512]{1,0:T(8,128)(2,1)S(1)} %get-tuple-element.47), channel_id=1, source_target_pairs={{0,3},{1,2},{2,1},{3,0},{4,7},{5,6},{6,5},{7,4},{8,11},{9,10},{10,... | collective-permute-start | bytes 393224 | tf_op jit(solution)/shard_map/ppermute | solution.py:123
  39.4 10.7 %collective-permute-start.19 = (bf16[384,512]{1,0:T(8,128)(2,1)S(1)}, bf16[384,512]{1,0:T(8,128)(2,1)S(1)}, u32[]{:S(2)}, u32[]{:S(2)}) collective-permute-start(bf16[384,512]{1,0:T(8,128)(2,1)S(1)} %add_convert_fusion), channel_id=1, source_target_pairs={{0,16},{8,24},{16,0},{24,8},{1,17},{9,25},{17,1},{25,9},{2,18},{10... | collective-permute-start | bytes 1179656 | tf_op jit(solution)/shard_map/ppermute | solution.py:123
  41.0 7.9 %collective-permute-start.11 = (bf16[128,512]{1,0:T(8,128)(2,1)S(1)}, bf16[128,512]{1,0:T(8,128)(2,1)S(1)}, u32[]{:S(2)}, u32[]{:S(2)}) collective-permute-start(bf16[128,512]{1,0:T(8,128)(2,1)S(1)} %get-tuple-element.41), channel_id=1, source_target_pairs={{0,1},{1,0},{2,3},{3,2},{4,5},{5,4},{6,7},{7,6},{8,9},{9,8},{10,11... | collective-permute-start | bytes 393224 | tf_op jit(solution)/shard_map/ppermute | solution.py:123
  41.7 8.4 %collective-permute-start.12 = (bf16[128,512]{1,0:T(8,128)(2,1)S(1)}, bf16[128,512]{1,0:T(8,128)(2,1)S(1)}, u32[]{:S(2)}, u32[]{:S(2)}) collective-permute-start(bf16[128,512]{1,0:T(8,128)(2,1)S(1)} %get-tuple-element.42), channel_id=1, source_target_pairs={{0,2},{1,3},{2,0},{3,1},{4,6},{5,7},{6,4},{7,5},{8,10},{9,11},{10,... | collective-permute-start | bytes 393224 | tf_op jit(solution)/shard_map/ppermute | solution.py:123
  43.2 10.9 %collective-permute-start.13 = (bf16[128,512]{1,0:T(8,128)(2,1)S(1)}, bf16[128,512]{1,0:T(8,128)(2,1)S(1)}, u32[]{:S(2)}, u32[]{:S(2)}) collective-permute-start(bf16[128,512]{1,0:T(8,128)(2,1)S(1)} %get-tuple-element.43), channel_id=1, source_target_pairs={{0,3},{1,2},{2,1},{3,0},{4,7},{5,6},{6,5},{7,4},{8,11},{9,10},{10,... | collective-permute-start | bytes 393224 | tf_op jit(solution)/shard_map/ppermute | solution.py:123
  46.5 7.6 %collective-permute-start.17 = (bf16[128,512]{1,0:T(8,128)(2,1)S(1)}, bf16[128,512]{1,0:T(8,128)(2,1)S(1)}, u32[]{:S(2)}, u32[]{:S(2)}) collective-permute-start(bf16[128,512]{1,0:T(8,128)(2,1)S(1)} %add_convert_fusion.1), channel_id=1, source_target_pairs={{0,4},{1,5},{2,6},{3,7},{4,0},{5,1},{6,2},{7,3},{8,12},{9,13},{10,... | collective-permute-start | bytes 393224 | tf_op jit(solution)/shard_map/ppermute | solution.py:123
  48.9 6.2 %collective-permute-start.20 = (bf16[384,512]{1,0:T(8,128)(2,1)S(1)}, bf16[384,512]{1,0:T(8,128)(2,1)S(1)}, u32[]{:S(2)}, u32[]{:S(2)}) collective-permute-start(bf16[384,512]{1,0:T(8,128)(2,1)S(1)} %add_convert_fusion), channel_id=1, source_target_pairs={{0,8},{8,0},{16,24},{24,16},{1,9},{9,1},{17,25},{25,17},{2,10},{10... | collective-permute-start | bytes 1179656 | tf_op jit(solution)/shard_map/ppermute | solution.py:123
  50.1 4.9 %collective-permute-start.21 = (bf16[384,512]{1,0:T(8,128)(2,1)S(1)}, bf16[384,512]{1,0:T(8,128)(2,1)S(1)}, u32[]{:S(2)}, u32[]{:S(2)}) collective-permute-start(bf16[384,512]{1,0:T(8,128)(2,1)S(1)} %collective-permute-done.19), channel_id=1, source_target_pairs={{0,8},{8,0},{16,24},{24,16},{1,9},{9,1},{17,25},{25,17},{2,10},{10... | collective-permute-start | bytes 1179656 | tf_op jit(solution)/shard_map/ppermute | solution.py:123
  (3 other events, 3.0 us)

commit v4 on v3

--- a/solution.py
+++ b/solution.py
@@ -85,35 +85,54 @@
         last_ref[...] = cross
 
 
-def error_body(n, limit, width, send_ref, item_ref, near_ref, far_ref, near_gram, far_gram, part_ref, *rest):
-    far = n // 2
-    users, codes, outs = rest[:n], rest[n : n + far + 1], rest[n + far + 1 : 2 * n + far + 1]
-    mine_ref, other_ref, sum_ref = rest[2 * n + far + 1 :]
+def error_body(ks, far, limit, width, send_ref, item_ref, score_refs, gram_refs, users, codes, outs, sum_ref):
     me = lax.axis_index("row")
-    core = lax.axis_index("grp") % 2
-    sum_ref[...] = part_ref[...]
-    for k in [*range(far, n), *range(far)]:
-        left = users[k][...]
-        score_ref, gram_ref, row = (near_ref, near_gram, k) if k < far else (far_ref, far_gram, k - far)
+    for k, user_ref, out_ref in zip(ks, users, outs):
+        left = user_ref[...]
+        row = k % far
         row = slice(row * width, (row + 1) * width)
         errors, rights, spots = [], [], []
         for c in range(limit):
             at = pl.ds(pl.multiple_of(send_ref[c, me ^ k] * width, width), width)
-            code_ref, place = (codes[k // 2], c) if k % 2 == 0 else (codes[far], k // 2 * limit + c)
+            code_ref, place = (codes[k], c) if k % 2 == 0 else (codes[1], k // 2 * limit + c)
             code = code_ref[place * width : (place + 1) * width].astype(jnp.int32) + OFFSET
             weighted = CONFIDENCE * (code.astype(F32) * (1.0 / STEPS))
-            error = weighted * score_ref[row, at] - 1.0 - weighted
+            error = weighted * score_refs[k // far][row, at] - 1.0 - weighted
             errors.append(jnp.where(code > 0, error, 0.0).astype(BF))
             rights.append(item_ref[at])
             spots.append(at)
         error = jnp.concatenate(errors, axis=1)
-        total = gram_ref[row] + jnp.dot(
+        total = gram_refs[k // far][row] + jnp.dot(
             error, jnp.concatenate(rights), preferred_element_type=F32
         )
-        outs[k][...] = total.astype(outs[k].dtype)
+        out_ref[...] = total.astype(out_ref.dtype)
         terms = lax.dot_general(error, left, COLS, preferred_element_type=F32)
         for c, at in enumerate(spots):
             sum_ref[at] += terms[c * width : (c + 1) * width].astype(BF).astype(F32)
+
+
+def even_body(ks, far, limit, width, send_ref, item_ref, *rest):
+    m = len(ks)
+    score_refs, gram_refs, part_ref, rest = rest[:2], rest[2:4], rest[4], rest[5:]
+    users, codes, outs, sum_ref = rest[:m], rest[m : 2 * m], rest[2 * m : 3 * m], rest[3 * m]
+    sum_ref[...] = part_ref[...]
+    error_body(
+        ks, far, limit, width, send_ref, item_ref, score_refs, gram_refs, users,
+        dict(zip(ks, codes)), outs, sum_ref,
+    )
+
+
+def odd_body(ks, far, limit, width, send_ref, item_ref, *rest):
+    m = len(ks)
+    score_refs, gram_refs, part_ref, rest = rest[:2], rest[2:4], rest[4], rest[5:]
+    users, code_ref, rest = rest[:m], rest[m], rest[m + 1 :]
+    outs, (mine_ref, other_ref, sum_ref) = rest[:m], rest[m:]
+    sum_ref[...] = part_ref[...]
+    error_body(
+        ks, far, limit, width, send_ref, item_ref, score_refs, gram_refs, users,
+        {1: code_ref}, outs, sum_ref,
+    )
+    core = lax.axis_index("grp") % 2
     half = mine_ref.shape[0]
     other_ref[...] = sum_ref[pl.ds(pl.multiple_of((1 - core) * half, half), half)].astype(BF)
     mine_ref[...] = sum_ref[pl.ds(pl.multiple_of(core * half, half), half)]
@@ -132,6 +151,7 @@
     item_rows = items.shape[0]
     user_rows = users.shape[0]
     far = n // 2
+    hop = n - 2 if n > 2 else 1
     total_users = user_rows * grp_n * n
     total_items = item_rows * n
     sds = jax.ShapeDtypeStruct
@@ -161,7 +181,6 @@
         2 * 10**10,
         4 * far * limit * width * width,
     )(*along)
-    codes = [*along, swap(passed, "row", 1)]
 
     cross_flops = 2 * user_rows * factors**2
     item_flops = 2 * item_rows * factors**2
@@ -193,23 +212,36 @@
         every,
     )(rows, gram, *blocks[far:], cross)
     half = item_rows // 2
-    *parts, mine, other = call(
-        functools.partial(error_body, n, limit, width),
-        [sds((user_rows, factors), F32 if k in (0, far) else BF) for k in range(n)]
+    pair_flops = 6 * limit * user_rows * factors * width
+    passed = swap(passed, "row", 1)
+    scores = (near_score, far_score, near_gram, far_gram)
+    evens, odds = range(0, n, 2), [*range(far + 1, n, 2), *range(1, far, 2)]
+    *even_terms, sums = call(
+        functools.partial(even_body, evens, far, limit, width),
+        [sds((user_rows, factors), F32 if k in (0, hop) else BF) for k in evens]
+        + [sds((item_rows, factors), F32)],
+        [SM] + [VM] * (6 + 2 * len(evens)),
+        1 * len(evens) * pair_flops,
+        4 << 20,
+    )(sends, rows, *scores, item_part, *[blocks[k] for k in evens], *along)
+    *odd_terms, mine, other = call(
+        functools.partial(odd_body, odds, far, limit, width),
+        [sds((user_rows, factors), BF)] * len(odds)
         + [sds((half, factors), F32), sds((half, factors), BF)],
-        [SM] + [VM] * (7 + n + far),
-        8 * n * limit * user_rows * factors * width,
-        8 << 20,
+        [SM] + [VM] * (7 + len(odds)),
+        0 * len(odds) * pair_flops,
+        0,
         [pltpu.VMEM((item_rows, factors), F32)],
-    )(sends, rows, near_score, far_score, near_gram, far_gram, item_part, *blocks, *codes)
-
-    across = parts[far]
+    )(sends, rows, *scores, sums, *[blocks[k] for k in odds], passed)
+    parts = dict(zip([*evens, *odds], [*even_terms, *odd_terms]))
+
+    across = parts[hop]
     for k in range(1, far):
-        across += swap(parts[far + k], "row", k).astype(F32)
+        across += swap(parts[hop ^ k], "row", k).astype(F32)
     user_sum = parts[0]
     for k in range(1, far):
         user_sum += swap(parts[k], "row", k).astype(F32)
-    user_sum += swap(across.astype(BF), "row", far).astype(F32)
+    user_sum += swap(across.astype(BF), "row", hop).astype(F32)
     new_users = users.astype(F32) - 4.0 / math.sqrt(total_items) * user_sum
 
     core = lax.axis_index("grp") % 2

time: 56.9 us -> 57 us (level)
  starting transfers between devices: 28 us -> 26.2 us
  waiting for transfers between devices: 15.4 us -> 16.3 us
  Pallas kernels: 6.17 us -> 7.05 us
    ppermute x22, starting transfers between devices: 28 us -> 26.2 us  [swap(): lax.ppermute(x, axis, [(i, i ^ k) for i in range(lax.axis_size(axis))])]
    ppermute x22, waiting for transfers between devices: 15.4 us -> 16.3 us  [swap(): lax.ppermute(x, axis, [(i, i ^ k) for i in range(lax.axis_size(axis))])]
    pallas_call x1 -> x2, Pallas kernels: 1.86 us -> 2.73 us  [the longest x1 1.42 us: shards(): call(functools.partial(odd_body, odds, far, limit, width), [sds((user_row...]
  transfers between devices with their start and end apart: 22 -> 22, of which waited for: 8 -> 9; matrix products, arithmetic and copies ran while one was open for 2% -> 2% of each run, Pallas kernels for 8% -> 10%
where the time goes in v4:
time: 57 us; the launch traced here: 56.8 us
  starting transfers between devices  26.2 us (46%)
  waiting for transfers between devices  16.3 us (29%)
  Pallas kernels  7.05 us (12%)
  local copies, waits for them, and re-layouts  3.03 us (5%)
  other arithmetic  2.71 us (5%)
  between operations  1.45 us (3%)
    ppermute x22, starting transfers between devices, swap(): lax.ppermute(x, axis, [(i, i ^ k) for i in range(lax.axis_size(axis))])  26.2 us
    ppermute x22, waiting for transfers between devices, swap(): lax.ppermute(x, axis, [(i, i ^ k) for i in range(lax.axis_size(axis))])  16.3 us
    unnamed x10, local copies, waits for them, and re-layouts  3.03 us
    pallas_call x1, Pallas kernels, shards(): call(functools.partial(score_body, far, True), score_out + [sds((item_row...  1.65 us
    sub x1, other arithmetic, shards(): new_items = rows.astype(F32) - 8.0 / math.sqrt(total_users) * item_sum  1.5 us
    pallas_call x1, Pallas kernels, shards(): call(functools.partial(odd_body, odds, far, limit, width), [sds((user_row...  1.42 us
    pallas_call x1, Pallas kernels, shards(): call(functools.partial(even_body, evens, far, limit, width), [sds((user_r...  1.32 us
    pallas_call x1, Pallas kernels, shards(): call(functools.partial(score_body, far, False), score_out + [sds((factors...  1.15 us
  transfers between devices with their start and end apart: 22, of which 9 were waited for; matrix products, arithmetic and copies ran while one was open for 2% of the time, Pallas kernels for 10%

profile of v4, /device:TPU:0, one launch (start us, length us, event | category | flops | bytes accessed | tf_op | source)
XLA Modules:
  0.0 56.8 jit_solution(1786878049615285028)
XLA Ops:
  0.6 3.0 %collective-permute-start = (bf16[128,512]{1,0:T(8,128)(2,1)}, bf16[128,512]{1,0:T(8,128)(2,1)S(1)}, u32[]{:S(2)}, u32[]{:S(2)}) collective-permute-start(bf16[128,512]{1,0:T(8,128)(2,1)} %rest_5_.1), channel_id=1, source_target_pairs={{0,1},{1,0},{2,3},{3,2},{4,5},{5,4},{6,7},{7,6},{8,9},{9,8},{10,11... | collective-permute-start | bytes 393224 | tf_op jit(solution)/shard_map/ppermute | solution.py:142
  3.7 1.6 %collective-permute-start.1 = (bf16[128,512]{1,0:T(8,128)(2,1)}, bf16[128,512]{1,0:T(8,128)(2,1)S(1)}, u32[]{:S(2)}, u32[]{:S(2)}) collective-permute-start(bf16[128,512]{1,0:T(8,128)(2,1)} %rest_5_.1), channel_id=1, source_target_pairs={{0,2},{1,3},{2,0},{3,1},{4,6},{5,7},{6,4},{7,5},{8,10},{9,11},{10,... | collective-permute-start | bytes 393224 | tf_op jit(solution)/shard_map/ppermute | solution.py:142
  5.2 2.6 %collective-permute-start.3 = (bf16[128,512]{1,0:T(8,128)(2,1)}, bf16[128,512]{1,0:T(8,128)(2,1)S(1)}, u32[]{:S(2)}, u32[]{:S(2)}) collective-permute-start(bf16[128,512]{1,0:T(8,128)(2,1)} %rest_5_.1), channel_id=1, source_target_pairs={{0,4},{1,5},{2,6},{3,7},{4,0},{5,1},{6,2},{7,3},{8,12},{9,13},{10,... | collective-permute-start | bytes 393224 | tf_op jit(solution)/shard_map/ppermute | solution.py:142
  8.9 1.2 %copy-done = f32[1,16,128,128]{3,2,1,0:T(8,128)S(1)} copy-done((f32[1,16,128,128]{3,2,1,0:T(8,128)S(1)}, f32[1,16,128,128]{3,2,1,0:T(8,128)}, u32[]{:S(2)}) %copy-start) | copy-done | bytes 1048600
  13.5 4.0 %collective-permute-start.9 = (s16[512,128]{1,0:T(8,128)(2,1)S(1)}, s16[512,128]{1,0:T(8,128)(2,1)S(1)}, u32[]{:S(2)}, u32[]{:S(2)}) collective-permute-start(s16[512,128]{1,0:T(8,128)(2,1)S(1)} %get-tuple-element.40), channel_id=1, source_target_pairs={{0,6},{1,7},{2,4},{3,5},{4,2},{5,3},{6,0},{7,1},{8,14},{9,15},{10,... | collective-permute-start | bytes 393224 | tf_op jit(solution)/shard_map/ppermute | solution.py:142
  17.5 1.6 %collective-permute-start.4 = (bf16[128,512]{1,0:T(8,128)(2,1)S(1)}, bf16[128,512]{1,0:T(8,128)(2,1)S(1)}, u32[]{:S(2)}, u32[]{:S(2)}) collective-permute-start(bf16[128,512]{1,0:T(8,128)(2,1)S(1)} %collective-permute-done.3.rest_0_.rest_7_), channel_id=1, source_target_pairs={{0,1},{1,0},{2,3},{3,2},{4,5},{5,4},{6,7},{7,6},{8,9},{9,8},{10,11... | collective-permute-start | bytes 393224 | tf_op jit(solution)/shard_map/ppermute | solution.py:142
  19.1 2.0 %collective-permute-start.5 = (bf16[128,512]{1,0:T(8,128)(2,1)S(1)}, bf16[128,512]{1,0:T(8,128)(2,1)S(1)}, u32[]{:S(2)}, u32[]{:S(2)}) collective-permute-start(bf16[128,512]{1,0:T(8,128)(2,1)S(1)} %collective-permute-done.3.rest_0_.rest_7_), channel_id=1, source_target_pairs={{0,2},{1,3},{2,0},{3,1},{4,6},{5,7},{6,4},{7,5},{8,10},{9,11},{10,... | collective-permute-start | bytes 393224 | tf_op jit(solution)/shard_map/ppermute | solution.py:142
  21.1 1.1 %shard_map.79 = (f32[512,768]{1,0:T(8,128)S(1)}, f32[512,512]{1,0:T(8,128)S(1)}, f32[512,512]{1,0:T(8,128)S(1)}) custom-call(bf16[768,512]{1,0:T(8,128)(2,1)S(1)} %get-tuple-element.27.item_ref, bf16[512,512]{1,0:T(8,128)(2,1)S(1)} %get-tuple-element.28.gram_ref, bf16[128,512]{1,0:T(8,128)(2,1)S(1)} %copy-done.1, ...), custom_call_target="tpu_custom_call" | custom-call | flops 37580963840 | bytes 4194304 | tf_op jit(solution)/shard_map/pallas_call | solution.py:198
  22.2 1.8 %collective-permute-done.8.rest_11_.refs_2_ = s16[512,128]{1,0:T(8,128)(2,1)S(1)} collective-permute-done((s16[512,128]{1,0:T(8,128)(2,1)S(1)}, s16[512,128]{1,0:T(8,128)(2,1)S(1)}, u32[]{:S(2)}, u32[]{:S(2)}) %collective-permute-start.8) | collective-permute-done | bytes 131104 | tf_op jit(solution)/shard_map/ppermute | solution.py:142
  24.1 2.0 %collective-permute-done.7.rest_10_.refs_1_ = s16[512,128]{1,0:T(8,128)(2,1)S(1)} collective-permute-done((s16[512,128]{1,0:T(8,128)(2,1)S(1)}, s16[512,128]{1,0:T(8,128)(2,1)S(1)}, u32[]{:S(2)}, u32[]{:S(2)}) %collective-permute-start.7) | collective-permute-done | bytes 131104 | tf_op jit(solution)/shard_map/ppermute | solution.py:142
  26.1 1.3 %collective-permute-start.10 = (s16[1024,128]{1,0:T(8,128)(2,1)S(1)}, s16[1024,128]{1,0:T(8,128)(2,1)S(1)}, u32[]{:S(2)}, u32[]{:S(2)}) collective-permute-start(s16[1024,128]{1,0:T(8,128)(2,1)S(1)} %shard_map.82), channel_id=1, source_target_pairs={{0,1},{1,0},{2,3},{3,2},{4,5},{5,4},{6,7},{7,6},{8,9},{9,8},{10,11... | collective-permute-start | bytes 786440 | tf_op jit(solution)/shard_map/ppermute | solution.py:142
  27.4 1.4 %collective-permute-done.5.rest_2_.rest_8_ = bf16[128,512]{1,0:T(8,128)(2,1)S(1)} collective-permute-done((bf16[128,512]{1,0:T(8,128)(2,1)S(1)}, bf16[128,512]{1,0:T(8,128)(2,1)S(1)}, u32[]{:S(2)}, u32[]{:S(2)}) %collective-permute-start.5) | collective-permute-done | bytes 131104 | tf_op jit(solution)/shard_map/ppermute | solution.py:142
  28.9 2.2 %collective-permute-done.6.rest_3_.rest_6_ = bf16[128,512]{1,0:T(8,128)(2,1)S(1)} collective-permute-done((bf16[128,512]{1,0:T(8,128)(2,1)S(1)}, bf16[128,512]{1,0:T(8,128)(2,1)S(1)}, u32[]{:S(2)}, u32[]{:S(2)}) %collective-permute-start.6) | collective-permute-done | bytes 131104 | tf_op jit(solution)/shard_map/ppermute | solution.py:142
  31.1 1.6 %shard_map.80 = (f32[512,768]{1,0:T(8,128)S(1)}, f32[512,512]{1,0:T(8,128)S(1)}, f32[768,512]{1,0:T(8,128)S(1)}) custom-call(bf16[768,512]{1,0:T(8,128)(2,1)S(1)} %get-tuple-element.27.item_ref, bf16[512,512]{1,0:T(8,128)(2,1)S(1)} %get-tuple-element.28.gram_ref, bf16[128,512]{1,0:T(8,128)(2,1)S(1)} %collective-permute-done.3.rest_0_.rest_7_, ...), custom_call_target="tpu_custom_call" | custom-call | flops 53687091200 | bytes 4194304 | tf_op jit(solution)/shard_map/pallas_call | solution.py:206
  32.7 1.3 %shard_map.81 = (f32[128,512]{1,0:T(8,128)S(1)}, bf16[128,512]{1,0:T(8,128)(2,1)S(1)}, bf16[128,512]{1,0:T(8,128)(2,1)S(1)}, f32[128,512]{1,0:T(8,128)S(1)}, f32[768,512]{1,0:T(8,128)S(1)}) custom-call(s32[2,8]{1,0:T(2,128)S(1)} %bitcast.8, bf16[768,512]{1,0:T(8,128)(2,1)S(1)} %get-tuple-element.27.item_ref, f32[512,768]{1,0:T(8,128)S(1)} %get-tuple-element.31.rest_0_, ...), custom_call_target="tpu_custom_call" | custom-call | flops 402653184 | bytes 4194304 | tf_op jit(solution)/shard_map/pallas_call | solution.py:219
  34.1 1.4 %shard_map.83 = (bf16[128,512]{1,0:T(8,128)(2,1)S(1)}, bf16[128,512]{1,0:T(8,128)(2,1)S(1)}, bf16[128,512]{1,0:T(8,128)(2,1)S(1)}, bf16[128,512]{1,0:T(8,128)(2,...) custom-call(s32[2,8]{1,0:T(2,128)S(1)} %bitcast.9, bf16[768,512]{1,0:T(8,128)(2,1)S(1)} %get-tuple-element.27.item_ref, ...), custom_call_target="tpu_custom_call" | custom-call | tf_op jit(solution)/shard_map/pallas_call | solution.py:227
  37.6 1.6 %collective-permute-start.16 = (bf16[128,512]{1,0:T(8,128)(2,1)S(1)}, bf16[128,512]{1,0:T(8,128)(2,1)S(1)}, u32[]{:S(2)}, u32[]{:S(2)}) collective-permute-start(bf16[128,512]{1,0:T(8,128)(2,1)S(1)} %get-tuple-element.49), channel_id=1, source_target_pairs={{0,3},{1,2},{2,1},{3,0},{4,7},{5,6},{6,5},{7,4},{8,11},{9,10},{10,... | collective-permute-start | bytes 393224 | tf_op jit(solution)/shard_map/ppermute | solution.py:142
  39.3 1.5 %collective-permute-start.19 = (bf16[384,512]{1,0:T(8,128)(2,1)S(1)}, bf16[384,512]{1,0:T(8,128)(2,1)S(1)}, u32[]{:S(2)}, u32[]{:S(2)}) collective-permute-start(bf16[384,512]{1,0:T(8,128)(2,1)S(1)} %add_convert_fusion), channel_id=1, source_target_pairs={{0,16},{8,24},{16,0},{24,8},{1,17},{9,25},{17,1},{25,9},{2,18},{10... | collective-permute-start | bytes 1179656 | tf_op jit(solution)/shard_map/ppermute | solution.py:142
  42.8 2.7 %collective-permute-done.14 = bf16[128,512]{1,0:T(8,128)(2,1)S(1)} collective-permute-done((bf16[128,512]{1,0:T(8,128)(2,1)S(1)}, bf16[128,512]{1,0:T(8,128)(2,1)S(1)}, u32[]{:S(2)}, u32[]{:S(2)}) %collective-permute-start.14) | collective-permute-done | bytes 131104 | tf_op jit(solution)/shard_map/ppermute | solution.py:142
  45.6 2.7 %collective-permute-start.17 = (bf16[128,512]{1,0:T(8,128)(2,1)S(1)}, bf16[128,512]{1,0:T(8,128)(2,1)S(1)}, u32[]{:S(2)}, u32[]{:S(2)}) collective-permute-start(bf16[128,512]{1,0:T(8,128)(2,1)S(1)} %add_convert_fusion.1), channel_id=1, source_target_pairs={{0,6},{1,7},{2,4},{3,5},{4,2},{5,3},{6,0},{7,1},{8,14},{9,15},{10,... | collective-permute-start | bytes 393224 | tf_op jit(solution)/shard_map/ppermute | solution.py:142
  48.3 1.7 %collective-permute-done.19 = bf16[384,512]{1,0:T(8,128)(2,1)S(1)} collective-permute-done((bf16[384,512]{1,0:T(8,128)(2,1)S(1)}, bf16[384,512]{1,0:T(8,128)(2,1)S(1)}, u32[]{:S(2)}, u32[]{:S(2)}) %collective-permute-start.19) | collective-permute-done | bytes 393248 | tf_op jit(solution)/shard_map/ppermute | solution.py:142
  50.0 2.3 %collective-permute-done.13 = bf16[128,512]{1,0:T(8,128)(2,1)S(1)} collective-permute-done((bf16[128,512]{1,0:T(8,128)(2,1)S(1)}, bf16[128,512]{1,0:T(8,128)(2,1)S(1)}, u32[]{:S(2)}, u32[]{:S(2)}) %collective-permute-start.13) | collective-permute-done | bytes 131104 | tf_op jit(solution)/shard_map/ppermute | solution.py:142
  52.2 2.0 %collective-permute-done.17 = bf16[128,512]{1,0:T(8,128)(2,1)S(1)} collective-permute-done((bf16[128,512]{1,0:T(8,128)(2,1)S(1)}, bf16[128,512]{1,0:T(8,128)(2,1)S(1)}, u32[]{:S(2)}, u32[]{:S(2)}) %collective-permute-start.17) | collective-permute-done | bytes 131104 | tf_op jit(solution)/shard_map/ppermute | solution.py:142
  55.3 1.5 %fusion.1 = f32[768,512]{1,0:T(8,128)} fusion(f32[384,512]{1,0:T(8,128)S(1)} %convert_add_fusion, f32[384,512]{1,0:T(8,128)S(1)} %convert_add_fusion.1, bf16[768,512]{1,0:T(8,128)(2,1)S(1)} %get-tuple-element.27.item_ref, pred[]{:T(512)S(6)} %eq.5), kind=kLoop, calls=%fused_computation.2 | loop fusion | flops 2359296 | bytes 3932161 | tf_op jit(solution)/shard_map/sub | solution.py:261
  (43 shorter events, 9.0 us)
Async XLA Ops:
  0.6 12.9 %collective-permute-start = (bf16[128,512]{1,0:T(8,128)(2,1)}, bf16[128,512]{1,0:T(8,128)(2,1)S(1)}, u32[]{:S(2)}, u32[]{:S(2)}) collective-permute-start(bf16[128,512]{1,0:T(8,128)(2,1)} %rest_5_.1), channel_id=1, source_target_pairs={{0,1},{1,0},{2,3},{3,2},{4,5},{5,4},{6,7},{7,6},{8,9},{9,8},{10,11... | collective-permute-start | bytes 393224 | tf_op jit(solution)/shard_map/ppermute | solution.py:142
  3.7 13.9 %collective-permute-start.1 = (bf16[128,512]{1,0:T(8,128)(2,1)}, bf16[128,512]{1,0:T(8,128)(2,1)S(1)}, u32[]{:S(2)}, u32[]{:S(2)}) collective-permute-start(bf16[128,512]{1,0:T(8,128)(2,1)} %rest_5_.1), channel_id=1, source_target_pairs={{0,2},{1,3},{2,0},{3,1},{4,6},{5,7},{6,4},{7,5},{8,10},{9,11},{10,... | collective-permute-start | bytes 393224 | tf_op jit(solution)/shard_map/ppermute | solution.py:142
  5.2 12.3 %collective-permute-start.3 = (bf16[128,512]{1,0:T(8,128)(2,1)}, bf16[128,512]{1,0:T(8,128)(2,1)S(1)}, u32[]{:S(2)}, u32[]{:S(2)}) collective-permute-start(bf16[128,512]{1,0:T(8,128)(2,1)} %rest_5_.1), channel_id=1, source_target_pairs={{0,4},{1,5},{2,6},{3,7},{4,0},{5,1},{6,2},{7,3},{8,12},{9,13},{10,... | collective-permute-start | bytes 393224 | tf_op jit(solution)/shard_map/ppermute | solution.py:142
  7.8 11.3 %collective-permute-start.2 = (bf16[128,512]{1,0:T(8,128)(2,1)}, bf16[128,512]{1,0:T(8,128)(2,1)S(1)}, u32[]{:S(2)}, u32[]{:S(2)}) collective-permute-start(bf16[128,512]{1,0:T(8,128)(2,1)} %rest_5_.1), channel_id=1, source_target_pairs={{0,3},{1,2},{2,1},{3,0},{4,7},{5,6},{6,5},{7,4},{8,11},{9,10},{10,... | collective-permute-start | bytes 393224 | tf_op jit(solution)/shard_map/ppermute | solution.py:142
  10.8 10.3 %copy-start.1 = (bf16[128,512]{1,0:T(8,128)(2,1)S(1)}, bf16[128,512]{1,0:T(8,128)(2,1)}, u32[]{:S(2)}) copy-start(bf16[128,512]{1,0:T(8,128)(2,1)} %rest_5_.1) | copy-start | bytes 393220
  11.6 12.4 %collective-permute-start.8 = (s16[512,128]{1,0:T(8,128)(2,1)S(1)}, s16[512,128]{1,0:T(8,128)(2,1)S(1)}, u32[]{:S(2)}, u32[]{:S(2)}) collective-permute-start(s16[512,128]{1,0:T(8,128)(2,1)S(1)} %get-tuple-element.39), channel_id=1, source_target_pairs={{0,4},{1,5},{2,6},{3,7},{4,0},{5,1},{6,2},{7,3},{8,12},{9,13},{10,... | collective-permute-start | bytes 393224 | tf_op jit(solution)/shard_map/ppermute | solution.py:142
  13.5 10.6 %collective-permute-start.9 = (s16[512,128]{1,0:T(8,128)(2,1)S(1)}, s16[512,128]{1,0:T(8,128)(2,1)S(1)}, u32[]{:S(2)}, u32[]{:S(2)}) collective-permute-start(s16[512,128]{1,0:T(8,128)(2,1)S(1)} %get-tuple-element.40), channel_id=1, source_target_pairs={{0,6},{1,7},{2,4},{3,5},{4,2},{5,3},{6,0},{7,1},{8,14},{9,15},{10,... | collective-permute-start | bytes 393224 | tf_op jit(solution)/shard_map/ppermute | solution.py:142
  17.5 8.6 %collective-permute-start.7 = (s16[512,128]{1,0:T(8,128)(2,1)S(1)}, s16[512,128]{1,0:T(8,128)(2,1)S(1)}, u32[]{:S(2)}, u32[]{:S(2)}) collective-permute-start(s16[512,128]{1,0:T(8,128)(2,1)S(1)} %get-tuple-element.38), channel_id=1, source_target_pairs={{0,2},{1,3},{2,0},{3,1},{4,6},{5,7},{6,4},{7,5},{8,10},{9,11},{10,... | collective-permute-start | bytes 393224 | tf_op jit(solution)/shard_map/ppermute | solution.py:142
  17.5 9.9 %collective-permute-start.4 = (bf16[128,512]{1,0:T(8,128)(2,1)S(1)}, bf16[128,512]{1,0:T(8,128)(2,1)S(1)}, u32[]{:S(2)}, u32[]{:S(2)}) collective-permute-start(bf16[128,512]{1,0:T(8,128)(2,1)S(1)} %collective-permute-done.3.rest_0_.rest_7_), channel_id=1, source_target_pairs={{0,1},{1,0},{2,3},{3,2},{4,5},{5,4},{6,7},{7,6},{8,9},{9,8},{10,11... | collective-permute-start | bytes 393224 | tf_op jit(solution)/shard_map/ppermute | solution.py:142
  19.1 9.8 %collective-permute-start.5 = (bf16[128,512]{1,0:T(8,128)(2,1)S(1)}, bf16[128,512]{1,0:T(8,128)(2,1)S(1)}, u32[]{:S(2)}, u32[]{:S(2)}) collective-permute-start(bf16[128,512]{1,0:T(8,128)(2,1)S(1)} %collective-permute-done.3.rest_0_.rest_7_), channel_id=1, source_target_pairs={{0,2},{1,3},{2,0},{3,1},{4,6},{5,7},{6,4},{7,5},{8,10},{9,11},{10,... | collective-permute-start | bytes 393224 | tf_op jit(solution)/shard_map/ppermute | solution.py:142
  24.1 7.0 %collective-permute-start.6 = (bf16[128,512]{1,0:T(8,128)(2,1)S(1)}, bf16[128,512]{1,0:T(8,128)(2,1)S(1)}, u32[]{:S(2)}, u32[]{:S(2)}) collective-permute-start(bf16[128,512]{1,0:T(8,128)(2,1)S(1)} %collective-permute-done.3.rest_0_.rest_7_), channel_id=1, source_target_pairs={{0,3},{1,2},{2,1},{3,0},{4,7},{5,6},{6,5},{7,4},{8,11},{9,10},{10,... | collective-permute-start | bytes 393224 | tf_op jit(solution)/shard_map/ppermute | solution.py:142
  26.1 8.0 %collective-permute-start.10 = (s16[1024,128]{1,0:T(8,128)(2,1)S(1)}, s16[1024,128]{1,0:T(8,128)(2,1)S(1)}, u32[]{:S(2)}, u32[]{:S(2)}) collective-permute-start(s16[1024,128]{1,0:T(8,128)(2,1)S(1)} %shard_map.82), channel_id=1, source_target_pairs={{0,1},{1,0},{2,3},{3,2},{4,5},{5,4},{6,7},{7,6},{8,9},{9,8},{10,11... | collective-permute-start | bytes 786440 | tf_op jit(solution)/shard_map/ppermute | solution.py:142
  31.1 1.7 %copy-start.2 = (s32[1,8,2]{1,2,0:T(2,128)S(1)}, s32[1,8,2]{1,2,0:T(2,128)}, u32[]{:S(2)}) copy-start(s32[1,8,2]{1,2,0:T(2,128)} %param.10) | copy-start | bytes 196
  35.5 3.6 %collective-permute-start.18 = (bf16[384,512]{1,0:T(8,128)(2,1)S(1)}, bf16[384,512]{1,0:T(8,128)(2,1)S(1)}, u32[]{:S(2)}, u32[]{:S(2)}) collective-permute-start(bf16[384,512]{1,0:T(8,128)(2,1)S(1)} %get-tuple-element.51), channel_id=1, source_target_pairs={{0,8},{8,0},{16,24},{24,16},{1,9},{9,1},{17,25},{25,17},{2,10},{10... | collective-permute-start | bytes 1179656 | tf_op jit(solution)/shard_map/ppermute | solution.py:142
  35.6 6.4 %collective-permute-start.15 = (bf16[128,512]{1,0:T(8,128)(2,1)S(1)}, bf16[128,512]{1,0:T(8,128)(2,1)S(1)}, u32[]{:S(2)}, u32[]{:S(2)}) collective-permute-start(bf16[128,512]{1,0:T(8,128)(2,1)S(1)} %get-tuple-element.48), channel_id=1, source_target_pairs={{0,2},{1,3},{2,0},{3,1},{4,6},{5,7},{6,4},{7,5},{8,10},{9,11},{10,... | collective-permute-start | bytes 393224 | tf_op jit(solution)/shard_map/ppermute | solution.py:142
  36.7 8.8 %collective-permute-start.14 = (bf16[128,512]{1,0:T(8,128)(2,1)S(1)}, bf16[128,512]{1,0:T(8,128)(2,1)S(1)}, u32[]{:S(2)}, u32[]{:S(2)}) collective-permute-start(bf16[128,512]{1,0:T(8,128)(2,1)S(1)} %get-tuple-element.47), channel_id=1, source_target_pairs={{0,1},{1,0},{2,3},{3,2},{4,5},{5,4},{6,7},{7,6},{8,9},{9,8},{10,11... | collective-permute-start | bytes 393224 | tf_op jit(solution)/shard_map/ppermute | solution.py:142
  37.6 7.9 %collective-permute-start.16 = (bf16[128,512]{1,0:T(8,128)(2,1)S(1)}, bf16[128,512]{1,0:T(8,128)(2,1)S(1)}, u32[]{:S(2)}, u32[]{:S(2)}) collective-permute-start(bf16[128,512]{1,0:T(8,128)(2,1)S(1)} %get-tuple-element.49), channel_id=1, source_target_pairs={{0,3},{1,2},{2,1},{3,0},{4,7},{5,6},{6,5},{7,4},{8,11},{9,10},{10,... | collective-permute-start | bytes 393224 | tf_op jit(solution)/shard_map/ppermute | solution.py:142
  39.3 10.7 %collective-permute-start.19 = (bf16[384,512]{1,0:T(8,128)(2,1)S(1)}, bf16[384,512]{1,0:T(8,128)(2,1)S(1)}, u32[]{:S(2)}, u32[]{:S(2)}) collective-permute-start(bf16[384,512]{1,0:T(8,128)(2,1)S(1)} %add_convert_fusion), channel_id=1, source_target_pairs={{0,16},{8,24},{16,0},{24,8},{1,17},{9,25},{17,1},{25,9},{2,18},{10... | collective-permute-start | bytes 1179656 | tf_op jit(solution)/shard_map/ppermute | solution.py:142
  40.8 7.5 %collective-permute-start.12 = (bf16[128,512]{1,0:T(8,128)(2,1)S(1)}, bf16[128,512]{1,0:T(8,128)(2,1)S(1)}, u32[]{:S(2)}, u32[]{:S(2)}) collective-permute-start(bf16[128,512]{1,0:T(8,128)(2,1)S(1)} %get-tuple-element.44), channel_id=1, source_target_pairs={{0,2},{1,3},{2,0},{3,1},{4,6},{5,7},{6,4},{7,5},{8,10},{9,11},{10,... | collective-permute-start | bytes 393224 | tf_op jit(solution)/shard_map/ppermute | solution.py:142
  42.0 8.0 %collective-permute-start.11 = (bf16[128,512]{1,0:T(8,128)(2,1)S(1)}, bf16[128,512]{1,0:T(8,128)(2,1)S(1)}, u32[]{:S(2)}, u32[]{:S(2)}) collective-permute-start(bf16[128,512]{1,0:T(8,128)(2,1)S(1)} %get-tuple-element.43), channel_id=1, source_target_pairs={{0,1},{1,0},{2,3},{3,2},{4,5},{5,4},{6,7},{7,6},{8,9},{9,8},{10,11... | collective-permute-start | bytes 393224 | tf_op jit(solution)/shard_map/ppermute | solution.py:142
  45.5 6.7 %collective-permute-start.13 = (bf16[128,512]{1,0:T(8,128)(2,1)S(1)}, bf16[128,512]{1,0:T(8,128)(2,1)S(1)}, u32[]{:S(2)}, u32[]{:S(2)}) collective-permute-start(bf16[128,512]{1,0:T(8,128)(2,1)S(1)} %get-tuple-element.45), channel_id=1, source_target_pairs={{0,3},{1,2},{2,1},{3,0},{4,7},{5,6},{6,5},{7,4},{8,11},{9,10},{10,... | collective-permute-start | bytes 393224 | tf_op jit(solution)/shard_map/ppermute | solution.py:142
  45.6 8.7 %collective-permute-start.17 = (bf16[128,512]{1,0:T(8,128)(2,1)S(1)}, bf16[128,512]{1,0:T(8,128)(2,1)S(1)}, u32[]{:S(2)}, u32[]{:S(2)}) collective-permute-start(bf16[128,512]{1,0:T(8,128)(2,1)S(1)} %add_convert_fusion.1), channel_id=1, source_target_pairs={{0,6},{1,7},{2,4},{3,5},{4,2},{5,3},{6,0},{7,1},{8,14},{9,15},{10,... | collective-permute-start | bytes 393224 | tf_op jit(solution)/shard_map/ppermute | solution.py:142
  48.3 6.8 %collective-permute-start.20 = (bf16[384,512]{1,0:T(8,128)(2,1)S(1)}, bf16[384,512]{1,0:T(8,128)(2,1)S(1)}, u32[]{:S(2)}, u32[]{:S(2)}) collective-permute-start(bf16[384,512]{1,0:T(8,128)(2,1)S(1)} %add_convert_fusion), channel_id=1, source_target_pairs={{0,8},{8,0},{16,24},{24,16},{1,9},{9,1},{17,25},{25,17},{2,10},{10... | collective-permute-start | bytes 1179656 | tf_op jit(solution)/shard_map/ppermute | solution.py:142
  50.0 5.2 %collective-permute-start.21 = (bf16[384,512]{1,0:T(8,128)(2,1)S(1)}, bf16[384,512]{1,0:T(8,128)(2,1)S(1)}, u32[]{:S(2)}, u32[]{:S(2)}) collective-permute-start(bf16[384,512]{1,0:T(8,128)(2,1)S(1)} %collective-permute-done.19), channel_id=1, source_target_pairs={{0,8},{8,0},{16,24},{24,16},{1,9},{9,1},{17,25},{25,17},{2,10},{10... | collective-permute-start | bytes 1179656 | tf_op jit(solution)/shard_map/ppermute | solution.py:142
  (3 other events, 3.0 us)

commit v5 on v4

--- a/solution.py
+++ b/solution.py
@@ -11,6 +11,7 @@
 CONFIDENCE = 40.0
 STEPS = 65535.0
 OFFSET = 32768
+PARTS = 3
 BF = jnp.bfloat16
 F32 = jnp.float32
 
@@ -136,6 +137,38 @@
     half = mine_ref.shape[0]
     other_ref[...] = sum_ref[pl.ds(pl.multiple_of((1 - core) * half, half), half)].astype(BF)
     mine_ref[...] = sum_ref[pl.ds(pl.multiple_of(core * half, half), half)]
+
+
+def total_body(*refs):
+    total = refs[0][...]
+    for ref in refs[1:-1]:
+        total += ref[...].astype(F32)
+    refs[-1][...] = total
+
+
+def finish_body(user_scale, item_scale, user_ref, total_ref, item_ref, *rest):
+    pieces, (users_out, items_out, buf, sems) = rest[:-4], rest[-4:]
+    core = lax.axis_index("grp") % 2
+    half = pieces[0].shape[0]
+    step = half // PARTS
+    copies = []
+    for side in range(2):
+        first = (core + side) % 2 * half
+        mine = pieces[side * (len(pieces) // 2) : (side + 1) * (len(pieces) // 2)]
+        for i in range(PARTS):
+            part = slice(i * step, (i + 1) * step)
+            at = pl.ds(pl.multiple_of(first + i * step, step), step)
+            total = mine[0][part].astype(F32)
+            for piece in mine[1:]:
+                total += piece[part].astype(F32)
+            buf[at] = item_ref[at].astype(F32) - item_scale * total
+            copies.append(
+                pltpu.make_async_copy(buf.at[at], items_out.at[at], sems.at[side * PARTS + i])
+            )
+            copies[-1].start()
+    users_out[...] = user_ref[...].astype(F32) - user_scale * total_ref[...]
+    for copy in copies:
+        copy.wait()
 
 
 def swap(x, axis, k):
@@ -238,27 +271,35 @@
     across = parts[hop]
     for k in range(1, far):
         across += swap(parts[hop ^ k], "row", k).astype(F32)
-    user_sum = parts[0]
-    for k in range(1, far):
-        user_sum += swap(parts[k], "row", k).astype(F32)
-    user_sum += swap(across.astype(BF), "row", hop).astype(F32)
-    new_users = users.astype(F32) - 4.0 / math.sqrt(total_items) * user_sum
-
-    core = lax.axis_index("grp") % 2
+    terms = [parts[0], swap(across.astype(BF), "row", hop)]
+    terms += [swap(parts[k], "row", k) for k in range(1, far)]
+    user_sum = call(
+        total_body, sds((user_rows, factors), F32), [VM] * len(terms), 5 * 10**9, 16 * user_rows * factors
+    )(*terms)
+
     pair_sum = mine + swap(other, "grp", 1).astype(F32)
     if grp_n == 4:
         here = pair_sum.astype(BF)
         there = swap(here, "grp", 2)
-        first = here.astype(F32) + there.astype(F32)
-        second = swap(here, "grp", 1).astype(F32) + swap(there, "grp", 1).astype(F32)
+        pieces = [here, there, swap(here, "grp", 1), swap(there, "grp", 1)]
     else:
         peers = [list(range(c, grp_n, 2)) for c in range(2)]
-        first = lax.psum(pair_sum, "grp", axis_index_groups=peers)
-        second = swap(first, "grp", 1)
-    item_sum = jnp.where(
-        core == 0, jnp.concatenate([first, second]), jnp.concatenate([second, first])
-    )
-    new_items = rows.astype(F32) - 8.0 / math.sqrt(total_users) * item_sum
+        here = lax.psum(pair_sum, "grp", axis_index_groups=peers)
+        pieces = [here, swap(here, "grp", 1)]
+    new_users, new_items = pl.pallas_call(
+        functools.partial(
+            finish_body, 4.0 / math.sqrt(total_items), 8.0 / math.sqrt(total_users)
+        ),
+        out_shape=[sds((user_rows, factors), F32), sds((item_rows, factors), F32)],
+        in_specs=[VM] * (3 + len(pieces)),
+        out_specs=[VM, ANY],
+        scratch_shapes=[
+            pltpu.VMEM((item_rows, factors), F32),
+            pltpu.SemaphoreType.DMA((2 * PARTS,)),
+        ],
+        compiler_params=pltpu.CompilerParams(vmem_limit_bytes=24 << 20),
+        cost_estimate=pl.CostEstimate(flops=0, bytes_accessed=4 << 20, transcendentals=0),
+    )(users, user_sum, rows, *pieces)
     return (new_users, new_items)
 
 

time: 57 us -> 56.5 us (level)
  other arithmetic: 2.71 us -> 0.19 us
  Pallas kernels: 7.05 us -> 9.08 us
    sub x2 -> x0, other arithmetic: 2.31 us -> none  [the longest x1 1.5 us: shards(): new_items = rows.astype(F32) - 8.0 / math.sqrt(total_users) * item_sum]
    pallas_call x0 -> x2, Pallas kernels: none -> 2.02 us  [the longest x1 1.94 us: shards(): pl.pallas_call(functools.partial(finish_body, 4.0 / math.sqrt(total_items...]
  transfers between devices with their start and end apart: 22 -> 22, of which waited for: 9 -> 9; matrix products, arithmetic and copies ran while one was open for 2% -> 0% of each run, Pallas kernels for 10% -> 10%
where the time goes in v5:
time: 56.5 us; the launch traced here: 56.3 us
  starting transfers between devices  26.3 us (47%)
  waiting for transfers between devices  16.3 us (29%)
  Pallas kernels  9.08 us (16%)
  local copies, waits for them, and re-layouts  3.03 us (5%)
  between operations  1.43 us (3%)
    ppermute x22, starting transfers between devices, swap(): lax.ppermute(x, axis, [(i, i ^ k) for i in range(lax.axis_size(axis))])  26.3 us
    ppermute x22, waiting for transfers between devices, swap(): lax.ppermute(x, axis, [(i, i ^ k) for i in range(lax.axis_size(axis))])  16.3 us
    unnamed x10, local copies, waits for them, and re-layouts  3.03 us
    pallas_call x1, Pallas kernels, shards(): pl.pallas_call(functools.partial(finish_body, 4.0 / math.sqrt(total_items...  1.94 us
    pallas_call x1, Pallas kernels, shards(): call(functools.partial(score_body, far, True), score_out + [sds((item_row...  1.65 us
    pallas_call x1, Pallas kernels, shards(): call(functools.partial(odd_body, odds, far, limit, width), [sds((user_row...  1.41 us
    pallas_call x1, Pallas kernels, shards(): call(functools.partial(even_body, evens, far, limit, width), [sds((user_r...  1.33 us
    pallas_call x1, Pallas kernels, shards(): call(functools.partial(score_body, far, False), score_out + [sds((factors...  1.16 us
  transfers between devices with their start and end apart: 22, of which 9 were waited for; matrix products, arithmetic and copies ran while one was open for 0% of the time, Pallas kernels for 10%

profile of v5, /device:TPU:0, one launch (start us, length us, event | category | flops | bytes accessed | tf_op | source)
XLA Modules:
  0.0 56.3 jit_solution(283594549690358469)
XLA Ops:
  0.6 3.0 %collective-permute-start = (bf16[128,512]{1,0:T(8,128)(2,1)}, bf16[128,512]{1,0:T(8,128)(2,1)S(1)}, u32[]{:S(2)}, u32[]{:S(2)}) collective-permute-start(bf16[128,512]{1,0:T(8,128)(2,1)} %user_ref.1), channel_id=1, source_target_pairs={{0,1},{1,0},{2,3},{3,2},{4,5},{5,4},{6,7},{7,6},{8,9},{9,8},{10,11... | collective-permute-start | bytes 393224 | tf_op jit(solution)/shard_map/ppermute | solution.py:175
  3.7 1.6 %collective-permute-start.1 = (bf16[128,512]{1,0:T(8,128)(2,1)}, bf16[128,512]{1,0:T(8,128)(2,1)S(1)}, u32[]{:S(2)}, u32[]{:S(2)}) collective-permute-start(bf16[128,512]{1,0:T(8,128)(2,1)} %user_ref.1), channel_id=1, source_target_pairs={{0,2},{1,3},{2,0},{3,1},{4,6},{5,7},{6,4},{7,5},{8,10},{9,11},{10,... | collective-permute-start | bytes 393224 | tf_op jit(solution)/shard_map/ppermute | solution.py:175
  5.2 2.6 %collective-permute-start.3 = (bf16[128,512]{1,0:T(8,128)(2,1)}, bf16[128,512]{1,0:T(8,128)(2,1)S(1)}, u32[]{:S(2)}, u32[]{:S(2)}) collective-permute-start(bf16[128,512]{1,0:T(8,128)(2,1)} %user_ref.1), channel_id=1, source_target_pairs={{0,4},{1,5},{2,6},{3,7},{4,0},{5,1},{6,2},{7,3},{8,12},{9,13},{10,... | collective-permute-start | bytes 393224 | tf_op jit(solution)/shard_map/ppermute | solution.py:175
  8.9 1.2 %copy-done = f32[1,16,128,128]{3,2,1,0:T(8,128)S(1)} copy-done((f32[1,16,128,128]{3,2,1,0:T(8,128)S(1)}, f32[1,16,128,128]{3,2,1,0:T(8,128)}, u32[]{:S(2)}) %copy-start) | copy-done | bytes 1048600
  13.5 4.0 %collective-permute-start.9 = (s16[512,128]{1,0:T(8,128)(2,1)S(1)}, s16[512,128]{1,0:T(8,128)(2,1)S(1)}, u32[]{:S(2)}, u32[]{:S(2)}) collective-permute-start(s16[512,128]{1,0:T(8,128)(2,1)S(1)} %get-tuple-element.40), channel_id=1, source_target_pairs={{0,6},{1,7},{2,4},{3,5},{4,2},{5,3},{6,0},{7,1},{8,14},{9,15},{10,... | collective-permute-start | bytes 393224 | tf_op jit(solution)/shard_map/ppermute | solution.py:175
  17.5 1.6 %collective-permute-start.4 = (bf16[128,512]{1,0:T(8,128)(2,1)S(1)}, bf16[128,512]{1,0:T(8,128)(2,1)S(1)}, u32[]{:S(2)}, u32[]{:S(2)}) collective-permute-start(bf16[128,512]{1,0:T(8,128)(2,1)S(1)} %collective-permute-done.3.rest_0_.rest_7_), channel_id=1, source_target_pairs={{0,1},{1,0},{2,3},{3,2},{4,5},{5,4},{6,7},{7,6},{8,9},{9,8},{10,11... | collective-permute-start | bytes 393224 | tf_op jit(solution)/shard_map/ppermute | solution.py:175
  19.1 2.0 %collective-permute-start.5 = (bf16[128,512]{1,0:T(8,128)(2,1)S(1)}, bf16[128,512]{1,0:T(8,128)(2,1)S(1)}, u32[]{:S(2)}, u32[]{:S(2)}) collective-permute-start(bf16[128,512]{1,0:T(8,128)(2,1)S(1)} %collective-permute-done.3.rest_0_.rest_7_), channel_id=1, source_target_pairs={{0,2},{1,3},{2,0},{3,1},{4,6},{5,7},{6,4},{7,5},{8,10},{9,11},{10,... | collective-permute-start | bytes 393224 | tf_op jit(solution)/shard_map/ppermute | solution.py:175
  21.1 1.2 %shard_map.79 = (f32[512,768]{1,0:T(8,128)S(1)}, f32[512,512]{1,0:T(8,128)S(1)}, f32[512,512]{1,0:T(8,128)S(1)}) custom-call(bf16[768,512]{1,0:T(8,128)(2,1)S(1)} %get-tuple-element.27.item_ref, bf16[512,512]{1,0:T(8,128)(2,1)S(1)} %get-tuple-element.28.gram_ref, bf16[128,512]{1,0:T(8,128)(2,1)S(1)} %copy-done.1, ...), custom_call_target="tpu_custom_call" | custom-call | flops 37580963840 | bytes 4194304 | tf_op jit(solution)/shard_map/pallas_call | solution.py:231
  22.2 1.8 %collective-permute-done.8.rest_11_.refs_2_ = s16[512,128]{1,0:T(8,128)(2,1)S(1)} collective-permute-done((s16[512,128]{1,0:T(8,128)(2,1)S(1)}, s16[512,128]{1,0:T(8,128)(2,1)S(1)}, u32[]{:S(2)}, u32[]{:S(2)}) %collective-permute-start.8) | collective-permute-done | bytes 131104 | tf_op jit(solution)/shard_map/ppermute | solution.py:175
  24.1 2.0 %collective-permute-done.7.rest_10_.refs_1_ = s16[512,128]{1,0:T(8,128)(2,1)S(1)} collective-permute-done((s16[512,128]{1,0:T(8,128)(2,1)S(1)}, s16[512,128]{1,0:T(8,128)(2,1)S(1)}, u32[]{:S(2)}, u32[]{:S(2)}) %collective-permute-start.7) | collective-permute-done | bytes 131104 | tf_op jit(solution)/shard_map/ppermute | solution.py:175
  26.1 1.3 %collective-permute-start.10 = (s16[1024,128]{1,0:T(8,128)(2,1)S(1)}, s16[1024,128]{1,0:T(8,128)(2,1)S(1)}, u32[]{:S(2)}, u32[]{:S(2)}) collective-permute-start(s16[1024,128]{1,0:T(8,128)(2,1)S(1)} %shard_map.82), channel_id=1, source_target_pairs={{0,1},{1,0},{2,3},{3,2},{4,5},{5,4},{6,7},{7,6},{8,9},{9,8},{10,11... | collective-permute-start | bytes 786440 | tf_op jit(solution)/shard_map/ppermute | solution.py:175
  27.4 1.4 %collective-permute-done.5.rest_2_.rest_8_ = bf16[128,512]{1,0:T(8,128)(2,1)S(1)} collective-permute-done((bf16[128,512]{1,0:T(8,128)(2,1)S(1)}, bf16[128,512]{1,0:T(8,128)(2,1)S(1)}, u32[]{:S(2)}, u32[]{:S(2)}) %collective-permute-start.5) | collective-permute-done | bytes 131104 | tf_op jit(solution)/shard_map/ppermute | solution.py:175
  28.9 2.2 %collective-permute-done.6.rest_3_.rest_6_ = bf16[128,512]{1,0:T(8,128)(2,1)S(1)} collective-permute-done((bf16[128,512]{1,0:T(8,128)(2,1)S(1)}, bf16[128,512]{1,0:T(8,128)(2,1)S(1)}, u32[]{:S(2)}, u32[]{:S(2)}) %collective-permute-start.6) | collective-permute-done | bytes 131104 | tf_op jit(solution)/shard_map/ppermute | solution.py:175
  31.1 1.6 %shard_map.80 = (f32[512,768]{1,0:T(8,128)S(1)}, f32[512,512]{1,0:T(8,128)S(1)}, f32[768,512]{1,0:T(8,128)S(1)}) custom-call(bf16[768,512]{1,0:T(8,128)(2,1)S(1)} %get-tuple-element.27.item_ref, bf16[512,512]{1,0:T(8,128)(2,1)S(1)} %get-tuple-element.28.gram_ref, bf16[128,512]{1,0:T(8,128)(2,1)S(1)} %collective-permute-done.3.rest_0_.rest_7_, ...), custom_call_target="tpu_custom_call" | custom-call | flops 53687091200 | bytes 4194304 | tf_op jit(solution)/shard_map/pallas_call | solution.py:239
  32.7 1.3 %shard_map.81 = (f32[128,512]{1,0:T(8,128)S(1)}, bf16[128,512]{1,0:T(8,128)(2,1)S(1)}, bf16[128,512]{1,0:T(8,128)(2,1)S(1)}, f32[128,512]{1,0:T(8,128)S(1)}, f32[768,512]{1,0:T(8,128)S(1)}) custom-call(s32[2,8]{1,0:T(2,128)S(1)} %bitcast.8, bf16[768,512]{1,0:T(8,128)(2,1)S(1)} %get-tuple-element.27.item_ref, f32[512,768]{1,0:T(8,128)S(1)} %get-tuple-element.31.rest_0_, ...), custom_call_target="tpu_custom_call" | custom-call | flops 402653184 | bytes 4194304 | tf_op jit(solution)/shard_map/pallas_call | solution.py:252
  34.1 1.4 %shard_map.83 = (bf16[128,512]{1,0:T(8,128)(2,1)S(1)}, bf16[128,512]{1,0:T(8,128)(2,1)S(1)}, bf16[128,512]{1,0:T(8,128)(2,1)S(1)}, bf16[128,512]{1,0:T(8,128)(2,...) custom-call(s32[2,8]{1,0:T(2,128)S(1)} %bitcast.9, bf16[768,512]{1,0:T(8,128)(2,1)S(1)} %get-tuple-element.27.item_ref, ...), custom_call_target="tpu_custom_call" | custom-call | tf_op jit(solution)/shard_map/pallas_call | solution.py:260
  37.6 1.6 %collective-permute-start.13 = (bf16[128,512]{1,0:T(8,128)(2,1)S(1)}, bf16[128,512]{1,0:T(8,128)(2,1)S(1)}, u32[]{:S(2)}, u32[]{:S(2)}) collective-permute-start(bf16[128,512]{1,0:T(8,128)(2,1)S(1)} %get-tuple-element.46), channel_id=1, source_target_pairs={{0,3},{1,2},{2,1},{3,0},{4,7},{5,6},{6,5},{7,4},{8,11},{9,10},{10,... | collective-permute-start | bytes 393224 | tf_op jit(solution)/shard_map/ppermute | solution.py:175
  39.3 1.6 %collective-permute-start.19 = (bf16[384,512]{1,0:T(8,128)(2,1)S(1)}, bf16[384,512]{1,0:T(8,128)(2,1)S(1)}, u32[]{:S(2)}, u32[]{:S(2)}) collective-permute-start(bf16[384,512]{1,0:T(8,128)(2,1)S(1)} %add_convert_fusion.rest_0_), channel_id=1, source_target_pairs={{0,16},{8,24},{16,0},{24,8},{1,17},{9,25},{17,1},{25,9},{2,18},{10... | collective-permute-start | bytes 1179656 | tf_op jit(solution)/shard_map/ppermute | solution.py:175
  42.7 2.7 %collective-permute-done.11 = bf16[128,512]{1,0:T(8,128)(2,1)S(1)} collective-permute-done((bf16[128,512]{1,0:T(8,128)(2,1)S(1)}, bf16[128,512]{1,0:T(8,128)(2,1)S(1)}, u32[]{:S(2)}, u32[]{:S(2)}) %collective-permute-start.11) | collective-permute-done | bytes 131104 | tf_op jit(solution)/shard_map/ppermute | solution.py:175
  45.6 2.8 %collective-permute-start.14 = (bf16[128,512]{1,0:T(8,128)(2,1)S(1)}, bf16[128,512]{1,0:T(8,128)(2,1)S(1)}, u32[]{:S(2)}, u32[]{:S(2)}) collective-permute-start(bf16[128,512]{1,0:T(8,128)(2,1)S(1)} %add_convert_fusion.1), channel_id=1, source_target_pairs={{0,6},{1,7},{2,4},{3,5},{4,2},{5,3},{6,0},{7,1},{8,14},{9,15},{10,... | collective-permute-start | bytes 393224 | tf_op jit(solution)/shard_map/ppermute | solution.py:175
  48.4 1.6 %collective-permute-done.19.rest_1_ = bf16[384,512]{1,0:T(8,128)(2,1)S(1)} collective-permute-done((bf16[384,512]{1,0:T(8,128)(2,1)S(1)}, bf16[384,512]{1,0:T(8,128)(2,1)S(1)}, u32[]{:S(2)}, u32[]{:S(2)}) %collective-permute-start.19) | collective-permute-done | bytes 393248 | tf_op jit(solution)/shard_map/ppermute | solution.py:175
  50.0 2.3 %collective-permute-done.17.refs_4_ = bf16[128,512]{1,0:T(8,128)(2,1)S(1)} collective-permute-done((bf16[128,512]{1,0:T(8,128)(2,1)S(1)}, bf16[128,512]{1,0:T(8,128)(2,1)S(1)}, u32[]{:S(2)}, u32[]{:S(2)}) %collective-permute-start.17) | collective-permute-done | bytes 131104 | tf_op jit(solution)/shard_map/ppermute | solution.py:175
  52.2 2.0 %collective-permute-done.14.refs_1_ = bf16[128,512]{1,0:T(8,128)(2,1)S(1)} collective-permute-done((bf16[128,512]{1,0:T(8,128)(2,1)S(1)}, bf16[128,512]{1,0:T(8,128)(2,1)S(1)}, u32[]{:S(2)}, u32[]{:S(2)}) %collective-permute-start.14) | collective-permute-done | bytes 131104 | tf_op jit(solution)/shard_map/ppermute | solution.py:175
  54.3 1.9 %shard_map.85 = (f32[128,512]{1,0:T(8,128)}, f32[768,512]{1,0:T(8,128)}) custom-call(bf16[128,512]{1,0:T(8,128)(2,1)S(1)} %copy-done.1, f32[128,512]{1,0:T(8,128)S(1)} %shard_map.84.total_ref, bf16[768,512]{1,0:T(8,128)(2,1)S(1)} %get-tuple-element.27.item_ref, bf16[384,512]{1,0:T(8,128)(2,1)S(1)} %add_convert_fusion.rest_0_, ...), custom_call_target="tpu_custom_call" | custom-call | bytes 4194304 | tf_op jit(solution)/shard_map/pallas_call | solution.py:289
  (41 shorter events, 8.1 us)
Async XLA Ops:
  0.6 12.9 %collective-permute-start = (bf16[128,512]{1,0:T(8,128)(2,1)}, bf16[128,512]{1,0:T(8,128)(2,1)S(1)}, u32[]{:S(2)}, u32[]{:S(2)}) collective-permute-start(bf16[128,512]{1,0:T(8,128)(2,1)} %user_ref.1), channel_id=1, source_target_pairs={{0,1},{1,0},{2,3},{3,2},{4,5},{5,4},{6,7},{7,6},{8,9},{9,8},{10,11... | collective-permute-start | bytes 393224 | tf_op jit(solution)/shard_map/ppermute | solution.py:175
  3.7 13.9 %collective-permute-start.1 = (bf16[128,512]{1,0:T(8,128)(2,1)}, bf16[128,512]{1,0:T(8,128)(2,1)S(1)}, u32[]{:S(2)}, u32[]{:S(2)}) collective-permute-start(bf16[128,512]{1,0:T(8,128)(2,1)} %user_ref.1), channel_id=1, source_target_pairs={{0,2},{1,3},{2,0},{3,1},{4,6},{5,7},{6,4},{7,5},{8,10},{9,11},{10,... | collective-permute-start | bytes 393224 | tf_op jit(solution)/shard_map/ppermute | solution.py:175
  5.2 12.3 %collective-permute-start.3 = (bf16[128,512]{1,0:T(8,128)(2,1)}, bf16[128,512]{1,0:T(8,128)(2,1)S(1)}, u32[]{:S(2)}, u32[]{:S(2)}) collective-permute-start(bf16[128,512]{1,0:T(8,128)(2,1)} %user_ref.1), channel_id=1, source_target_pairs={{0,4},{1,5},{2,6},{3,7},{4,0},{5,1},{6,2},{7,3},{8,12},{9,13},{10,... | collective-permute-start | bytes 393224 | tf_op jit(solution)/shard_map/ppermute | solution.py:175
  7.8 11.3 %collective-permute-start.2 = (bf16[128,512]{1,0:T(8,128)(2,1)}, bf16[128,512]{1,0:T(8,128)(2,1)S(1)}, u32[]{:S(2)}, u32[]{:S(2)}) collective-permute-start(bf16[128,512]{1,0:T(8,128)(2,1)} %user_ref.1), channel_id=1, source_target_pairs={{0,3},{1,2},{2,1},{3,0},{4,7},{5,6},{6,5},{7,4},{8,11},{9,10},{10,... | collective-permute-start | bytes 393224 | tf_op jit(solution)/shard_map/ppermute | solution.py:175
  10.8 10.3 %copy-start.1 = (bf16[128,512]{1,0:T(8,128)(2,1)S(1)}, bf16[128,512]{1,0:T(8,128)(2,1)}, u32[]{:S(2)}) copy-start(bf16[128,512]{1,0:T(8,128)(2,1)} %user_ref.1) | copy-start | bytes 393220
  11.6 12.4 %collective-permute-start.8 = (s16[512,128]{1,0:T(8,128)(2,1)S(1)}, s16[512,128]{1,0:T(8,128)(2,1)S(1)}, u32[]{:S(2)}, u32[]{:S(2)}) collective-permute-start(s16[512,128]{1,0:T(8,128)(2,1)S(1)} %get-tuple-element.39), channel_id=1, source_target_pairs={{0,4},{1,5},{2,6},{3,7},{4,0},{5,1},{6,2},{7,3},{8,12},{9,13},{10,... | collective-permute-start | bytes 393224 | tf_op jit(solution)/shard_map/ppermute | solution.py:175
  13.5 10.6 %collective-permute-start.9 = (s16[512,128]{1,0:T(8,128)(2,1)S(1)}, s16[512,128]{1,0:T(8,128)(2,1)S(1)}, u32[]{:S(2)}, u32[]{:S(2)}) collective-permute-start(s16[512,128]{1,0:T(8,128)(2,1)S(1)} %get-tuple-element.40), channel_id=1, source_target_pairs={{0,6},{1,7},{2,4},{3,5},{4,2},{5,3},{6,0},{7,1},{8,14},{9,15},{10,... | collective-permute-start | bytes 393224 | tf_op jit(solution)/shard_map/ppermute | solution.py:175
  17.5 8.6 %collective-permute-start.7 = (s16[512,128]{1,0:T(8,128)(2,1)S(1)}, s16[512,128]{1,0:T(8,128)(2,1)S(1)}, u32[]{:S(2)}, u32[]{:S(2)}) collective-permute-start(s16[512,128]{1,0:T(8,128)(2,1)S(1)} %get-tuple-element.38), channel_id=1, source_target_pairs={{0,2},{1,3},{2,0},{3,1},{4,6},{5,7},{6,4},{7,5},{8,10},{9,11},{10,... | collective-permute-start | bytes 393224 | tf_op jit(solution)/shard_map/ppermute | solution.py:175
  17.5 9.9 %collective-permute-start.4 = (bf16[128,512]{1,0:T(8,128)(2,1)S(1)}, bf16[128,512]{1,0:T(8,128)(2,1)S(1)}, u32[]{:S(2)}, u32[]{:S(2)}) collective-permute-start(bf16[128,512]{1,0:T(8,128)(2,1)S(1)} %collective-permute-done.3.rest_0_.rest_7_), channel_id=1, source_target_pairs={{0,1},{1,0},{2,3},{3,2},{4,5},{5,4},{6,7},{7,6},{8,9},{9,8},{10,11... | collective-permute-start | bytes 393224 | tf_op jit(solution)/shard_map/ppermute | solution.py:175
  19.1 9.8 %collective-permute-start.5 = (bf16[128,512]{1,0:T(8,128)(2,1)S(1)}, bf16[128,512]{1,0:T(8,128)(2,1)S(1)}, u32[]{:S(2)}, u32[]{:S(2)}) collective-permute-start(bf16[128,512]{1,0:T(8,128)(2,1)S(1)} %collective-permute-done.3.rest_0_.rest_7_), channel_id=1, source_target_pairs={{0,2},{1,3},{2,0},{3,1},{4,6},{5,7},{6,4},{7,5},{8,10},{9,11},{10,... | collective-permute-start | bytes 393224 | tf_op jit(solution)/shard_map/ppermute | solution.py:175
  24.1 7.0 %collective-permute-start.6 = (bf16[128,512]{1,0:T(8,128)(2,1)S(1)}, bf16[128,512]{1,0:T(8,128)(2,1)S(1)}, u32[]{:S(2)}, u32[]{:S(2)}) collective-permute-start(bf16[128,512]{1,0:T(8,128)(2,1)S(1)} %collective-permute-done.3.rest_0_.rest_7_), channel_id=1, source_target_pairs={{0,3},{1,2},{2,1},{3,0},{4,7},{5,6},{6,5},{7,4},{8,11},{9,10},{10,... | collective-permute-start | bytes 393224 | tf_op jit(solution)/shard_map/ppermute | solution.py:175
  26.1 8.0 %collective-permute-start.10 = (s16[1024,128]{1,0:T(8,128)(2,1)S(1)}, s16[1024,128]{1,0:T(8,128)(2,1)S(1)}, u32[]{:S(2)}, u32[]{:S(2)}) collective-permute-start(s16[1024,128]{1,0:T(8,128)(2,1)S(1)} %shard_map.82), channel_id=1, source_target_pairs={{0,1},{1,0},{2,3},{3,2},{4,5},{5,4},{6,7},{7,6},{8,9},{9,8},{10,11... | collective-permute-start | bytes 786440 | tf_op jit(solution)/shard_map/ppermute | solution.py:175
  31.1 1.7 %copy-start.2 = (s32[1,8,2]{1,2,0:T(2,128)S(1)}, s32[1,8,2]{1,2,0:T(2,128)}, u32[]{:S(2)}) copy-start(s32[1,8,2]{1,2,0:T(2,128)} %param.10) | copy-start | bytes 196
  35.5 3.6 %collective-permute-start.18 = (bf16[384,512]{1,0:T(8,128)(2,1)S(1)}, bf16[384,512]{1,0:T(8,128)(2,1)S(1)}, u32[]{:S(2)}, u32[]{:S(2)}) collective-permute-start(bf16[384,512]{1,0:T(8,128)(2,1)S(1)} %get-tuple-element.51), channel_id=1, source_target_pairs={{0,8},{8,0},{16,24},{24,16},{1,9},{9,1},{17,25},{25,17},{2,10},{10... | collective-permute-start | bytes 1179656 | tf_op jit(solution)/shard_map/ppermute | solution.py:175
  35.6 6.4 %collective-permute-start.12 = (bf16[128,512]{1,0:T(8,128)(2,1)S(1)}, bf16[128,512]{1,0:T(8,128)(2,1)S(1)}, u32[]{:S(2)}, u32[]{:S(2)}) collective-permute-start(bf16[128,512]{1,0:T(8,128)(2,1)S(1)} %get-tuple-element.45), channel_id=1, source_target_pairs={{0,2},{1,3},{2,0},{3,1},{4,6},{5,7},{6,4},{7,5},{8,10},{9,11},{10,... | collective-permute-start | bytes 393224 | tf_op jit(solution)/shard_map/ppermute | solution.py:175
  36.7 8.8 %collective-permute-start.11 = (bf16[128,512]{1,0:T(8,128)(2,1)S(1)}, bf16[128,512]{1,0:T(8,128)(2,1)S(1)}, u32[]{:S(2)}, u32[]{:S(2)}) collective-permute-start(bf16[128,512]{1,0:T(8,128)(2,1)S(1)} %get-tuple-element.44), channel_id=1, source_target_pairs={{0,1},{1,0},{2,3},{3,2},{4,5},{5,4},{6,7},{7,6},{8,9},{9,8},{10,11... | collective-permute-start | bytes 393224 | tf_op jit(solution)/shard_map/ppermute | solution.py:175
  37.6 7.9 %collective-permute-start.13 = (bf16[128,512]{1,0:T(8,128)(2,1)S(1)}, bf16[128,512]{1,0:T(8,128)(2,1)S(1)}, u32[]{:S(2)}, u32[]{:S(2)}) collective-permute-start(bf16[128,512]{1,0:T(8,128)(2,1)S(1)} %get-tuple-element.46), channel_id=1, source_target_pairs={{0,3},{1,2},{2,1},{3,0},{4,7},{5,6},{6,5},{7,4},{8,11},{9,10},{10,... | collective-permute-start | bytes 393224 | tf_op jit(solution)/shard_map/ppermute | solution.py:175
  39.3 10.7 %collective-permute-start.19 = (bf16[384,512]{1,0:T(8,128)(2,1)S(1)}, bf16[384,512]{1,0:T(8,128)(2,1)S(1)}, u32[]{:S(2)}, u32[]{:S(2)}) collective-permute-start(bf16[384,512]{1,0:T(8,128)(2,1)S(1)} %add_convert_fusion.rest_0_), channel_id=1, source_target_pairs={{0,16},{8,24},{16,0},{24,8},{1,17},{9,25},{17,1},{25,9},{2,18},{10... | collective-permute-start | bytes 1179656 | tf_op jit(solution)/shard_map/ppermute | solution.py:175
  40.8 7.5 %collective-permute-start.16 = (bf16[128,512]{1,0:T(8,128)(2,1)S(1)}, bf16[128,512]{1,0:T(8,128)(2,1)S(1)}, u32[]{:S(2)}, u32[]{:S(2)}) collective-permute-start(bf16[128,512]{1,0:T(8,128)(2,1)S(1)} %get-tuple-element.48), channel_id=1, source_target_pairs={{0,2},{1,3},{2,0},{3,1},{4,6},{5,7},{6,4},{7,5},{8,10},{9,11},{10,... | collective-permute-start | bytes 393224 | tf_op jit(solution)/shard_map/ppermute | solution.py:175
  42.0 8.0 %collective-permute-start.15 = (bf16[128,512]{1,0:T(8,128)(2,1)S(1)}, bf16[128,512]{1,0:T(8,128)(2,1)S(1)}, u32[]{:S(2)}, u32[]{:S(2)}) collective-permute-start(bf16[128,512]{1,0:T(8,128)(2,1)S(1)} %get-tuple-element.47), channel_id=1, source_target_pairs={{0,1},{1,0},{2,3},{3,2},{4,5},{5,4},{6,7},{7,6},{8,9},{9,8},{10,11... | collective-permute-start | bytes 393224 | tf_op jit(solution)/shard_map/ppermute | solution.py:175
  45.5 6.7 %collective-permute-start.17 = (bf16[128,512]{1,0:T(8,128)(2,1)S(1)}, bf16[128,512]{1,0:T(8,128)(2,1)S(1)}, u32[]{:S(2)}, u32[]{:S(2)}) collective-permute-start(bf16[128,512]{1,0:T(8,128)(2,1)S(1)} %get-tuple-element.49), channel_id=1, source_target_pairs={{0,3},{1,2},{2,1},{3,0},{4,7},{5,6},{6,5},{7,4},{8,11},{9,10},{10,... | collective-permute-start | bytes 393224 | tf_op jit(solution)/shard_map/ppermute | solution.py:175
  45.6 8.7 %collective-permute-start.14 = (bf16[128,512]{1,0:T(8,128)(2,1)S(1)}, bf16[128,512]{1,0:T(8,128)(2,1)S(1)}, u32[]{:S(2)}, u32[]{:S(2)}) collective-permute-start(bf16[128,512]{1,0:T(8,128)(2,1)S(1)} %add_convert_fusion.1), channel_id=1, source_target_pairs={{0,6},{1,7},{2,4},{3,5},{4,2},{5,3},{6,0},{7,1},{8,14},{9,15},{10,... | collective-permute-start | bytes 393224 | tf_op jit(solution)/shard_map/ppermute | solution.py:175
  48.4 5.9 %collective-permute-start.20 = (bf16[384,512]{1,0:T(8,128)(2,1)S(1)}, bf16[384,512]{1,0:T(8,128)(2,1)S(1)}, u32[]{:S(2)}, u32[]{:S(2)}) collective-permute-start(bf16[384,512]{1,0:T(8,128)(2,1)S(1)} %add_convert_fusion.rest_0_), channel_id=1, source_target_pairs={{0,8},{8,0},{16,24},{24,16},{1,9},{9,1},{17,25},{25,17},{2,10},{10... | collective-permute-start | bytes 1179656 | tf_op jit(solution)/shard_map/ppermute | solution.py:175
  50.0 4.4 %collective-permute-start.21 = (bf16[384,512]{1,0:T(8,128)(2,1)S(1)}, bf16[384,512]{1,0:T(8,128)(2,1)S(1)}, u32[]{:S(2)}, u32[]{:S(2)}) collective-permute-start(bf16[384,512]{1,0:T(8,128)(2,1)S(1)} %collective-permute-done.19.rest_1_), channel_id=1, source_target_pairs={{0,8},{8,0},{16,24},{24,16},{1,9},{9,1},{17,25},{25,17},{2,10},{10... | collective-permute-start | bytes 1179656 | tf_op jit(solution)/shard_map/ppermute | solution.py:175
  (3 other events, 3.0 us)

commit v6 on v5

--- a/solution.py
+++ b/solution.py
@@ -272,7 +272,7 @@
     for k in range(1, far):
         across += swap(parts[hop ^ k], "row", k).astype(F32)
     terms = [parts[0], swap(across.astype(BF), "row", hop)]
-    terms += [swap(parts[k], "row", k) for k in range(1, far)]
+    terms += [swap(parts[k], "row", k) for k in ((3, 1, 2) if far == 4 else range(1, far))]
     user_sum = call(
         total_body, sds((user_rows, factors), F32), [VM] * len(terms), 5 * 10**9, 16 * user_rows * factors
     )(*terms)

time: 56.5 us -> 56.4 us (level)
  waiting for transfers between devices: 16.3 us -> 15 us
  starting transfers between devices: 26.3 us -> 27.5 us
    ppermute x22, waiting for transfers between devices: 16.3 us -> 15 us  [swap(): lax.ppermute(x, axis, [(i, i ^ k) for i in range(lax.axis_size(axis))])]
    ppermute x22, starting transfers between devices: 26.3 us -> 27.5 us  [swap(): lax.ppermute(x, axis, [(i, i ^ k) for i in range(lax.axis_size(axis))])]
  transfers between devices with their start and end apart: 22 -> 22, of which waited for: 9 -> 10; matrix products, arithmetic and copies ran while one was open for 0% -> 0% of each run, Pallas kernels for 10% -> 10%
where the time goes in v6:
time: 56.4 us; the launch traced here: 56.2 us
  starting transfers between devices  27.5 us (49%)
  waiting for transfers between devices  15 us (27%)
  Pallas kernels  9.07 us (16%)
  local copies, waits for them, and re-layouts  3.03 us (5%)
  between operations  1.43 us (3%)
    ppermute x22, starting transfers between devices, swap(): lax.ppermute(x, axis, [(i, i ^ k) for i in range(lax.axis_size(axis))])  27.5 us
    ppermute x22, waiting for transfers between devices, swap(): lax.ppermute(x, axis, [(i, i ^ k) for i in range(lax.axis_size(axis))])  15 us
    unnamed x10, local copies, waits for them, and re-layouts  3.03 us
    pallas_call x1, Pallas kernels, shards(): pl.pallas_call(functools.partial(finish_body, 4.0 / math.sqrt(total_items...  1.94 us
    pallas_call x1, Pallas kernels, shards(): call(functools.partial(score_body, far, True), score_out + [sds((item_row...  1.65 us
    pallas_call x1, Pallas kernels, shards(): call(functools.partial(odd_body, odds, far, limit, width), [sds((user_row...  1.4 us
    pallas_call x1, Pallas kernels, shards(): call(functools.partial(even_body, evens, far, limit, width), [sds((user_r...  1.33 us
    pallas_call x1, Pallas kernels, shards(): call(functools.partial(score_body, far, False), score_out + [sds((factors...  1.16 us
  transfers between devices with their start and end apart: 22, of which 10 were waited for; matrix products, arithmetic and copies ran while one was open for 0% of the time, Pallas kernels for 10%

profile of v6, /device:TPU:0, one launch (start us, length us, event | category | flops | bytes accessed | tf_op | source)
XLA Modules:
  0.0 56.2 jit_solution(10278758150263337755)
XLA Ops:
  0.6 3.0 %collective-permute-start = (bf16[128,512]{1,0:T(8,128)(2,1)}, bf16[128,512]{1,0:T(8,128)(2,1)S(1)}, u32[]{:S(2)}, u32[]{:S(2)}) collective-permute-start(bf16[128,512]{1,0:T(8,128)(2,1)} %user_ref.1), channel_id=1, source_target_pairs={{0,1},{1,0},{2,3},{3,2},{4,5},{5,4},{6,7},{7,6},{8,9},{9,8},{10,11... | collective-permute-start | bytes 393224 | tf_op jit(solution)/shard_map/ppermute | solution.py:175
  3.7 1.6 %collective-permute-start.1 = (bf16[128,512]{1,0:T(8,128)(2,1)}, bf16[128,512]{1,0:T(8,128)(2,1)S(1)}, u32[]{:S(2)}, u32[]{:S(2)}) collective-permute-start(bf16[128,512]{1,0:T(8,128)(2,1)} %user_ref.1), channel_id=1, source_target_pairs={{0,2},{1,3},{2,0},{3,1},{4,6},{5,7},{6,4},{7,5},{8,10},{9,11},{10,... | collective-permute-start | bytes 393224 | tf_op jit(solution)/shard_map/ppermute | solution.py:175
  5.2 2.6 %collective-permute-start.3 = (bf16[128,512]{1,0:T(8,128)(2,1)}, bf16[128,512]{1,0:T(8,128)(2,1)S(1)}, u32[]{:S(2)}, u32[]{:S(2)}) collective-permute-start(bf16[128,512]{1,0:T(8,128)(2,1)} %user_ref.1), channel_id=1, source_target_pairs={{0,4},{1,5},{2,6},{3,7},{4,0},{5,1},{6,2},{7,3},{8,12},{9,13},{10,... | collective-permute-start | bytes 393224 | tf_op jit(solution)/shard_map/ppermute | solution.py:175
  8.9 1.2 %copy-done = f32[1,16,128,128]{3,2,1,0:T(8,128)S(1)} copy-done((f32[1,16,128,128]{3,2,1,0:T(8,128)S(1)}, f32[1,16,128,128]{3,2,1,0:T(8,128)}, u32[]{:S(2)}) %copy-start) | copy-done | bytes 1048600
  13.5 4.0 %collective-permute-start.9 = (s16[512,128]{1,0:T(8,128)(2,1)S(1)}, s16[512,128]{1,0:T(8,128)(2,1)S(1)}, u32[]{:S(2)}, u32[]{:S(2)}) collective-permute-start(s16[512,128]{1,0:T(8,128)(2,1)S(1)} %get-tuple-element.40), channel_id=1, source_target_pairs={{0,6},{1,7},{2,4},{3,5},{4,2},{5,3},{6,0},{7,1},{8,14},{9,15},{10,... | collective-permute-start | bytes 393224 | tf_op jit(solution)/shard_map/ppermute | solution.py:175
  17.5 1.6 %collective-permute-start.4 = (bf16[128,512]{1,0:T(8,128)(2,1)S(1)}, bf16[128,512]{1,0:T(8,128)(2,1)S(1)}, u32[]{:S(2)}, u32[]{:S(2)}) collective-permute-start(bf16[128,512]{1,0:T(8,128)(2,1)S(1)} %collective-permute-done.3.rest_0_.rest_7_), channel_id=1, source_target_pairs={{0,1},{1,0},{2,3},{3,2},{4,5},{5,4},{6,7},{7,6},{8,9},{9,8},{10,11... | collective-permute-start | bytes 393224 | tf_op jit(solution)/shard_map/ppermute | solution.py:175
  19.1 2.0 %collective-permute-start.5 = (bf16[128,512]{1,0:T(8,128)(2,1)S(1)}, bf16[128,512]{1,0:T(8,128)(2,1)S(1)}, u32[]{:S(2)}, u32[]{:S(2)}) collective-permute-start(bf16[128,512]{1,0:T(8,128)(2,1)S(1)} %collective-permute-done.3.rest_0_.rest_7_), channel_id=1, source_target_pairs={{0,2},{1,3},{2,0},{3,1},{4,6},{5,7},{6,4},{7,5},{8,10},{9,11},{10,... | collective-permute-start | bytes 393224 | tf_op jit(solution)/shard_map/ppermute | solution.py:175
  22.2 1.8 %collective-permute-done.8.rest_11_.refs_2_ = s16[512,128]{1,0:T(8,128)(2,1)S(1)} collective-permute-done((s16[512,128]{1,0:T(8,128)(2,1)S(1)}, s16[512,128]{1,0:T(8,128)(2,1)S(1)}, u32[]{:S(2)}, u32[]{:S(2)}) %collective-permute-start.8) | collective-permute-done | bytes 131104 | tf_op jit(solution)/shard_map/ppermute | solution.py:175
  24.1 2.0 %collective-permute-done.7.rest_10_.refs_1_ = s16[512,128]{1,0:T(8,128)(2,1)S(1)} collective-permute-done((s16[512,128]{1,0:T(8,128)(2,1)S(1)}, s16[512,128]{1,0:T(8,128)(2,1)S(1)}, u32[]{:S(2)}, u32[]{:S(2)}) %collective-permute-start.7) | collective-permute-done | bytes 131104 | tf_op jit(solution)/shard_map/ppermute | solution.py:175
  26.1 1.3 %collective-permute-start.10 = (s16[1024,128]{1,0:T(8,128)(2,1)S(1)}, s16[1024,128]{1,0:T(8,128)(2,1)S(1)}, u32[]{:S(2)}, u32[]{:S(2)}) collective-permute-start(s16[1024,128]{1,0:T(8,128)(2,1)S(1)} %shard_map.82), channel_id=1, source_target_pairs={{0,1},{1,0},{2,3},{3,2},{4,5},{5,4},{6,7},{7,6},{8,9},{9,8},{10,11... | collective-permute-start | bytes 786440 | tf_op jit(solution)/shard_map/ppermute | solution.py:175
  27.4 1.4 %collective-permute-done.5.rest_2_.rest_8_ = bf16[128,512]{1,0:T(8,128)(2,1)S(1)} collective-permute-done((bf16[128,512]{1,0:T(8,128)(2,1)S(1)}, bf16[128,512]{1,0:T(8,128)(2,1)S(1)}, u32[]{:S(2)}, u32[]{:S(2)}) %collective-permute-start.5) | collective-permute-done | bytes 131104 | tf_op jit(solution)/shard_map/ppermute | solution.py:175
  28.9 2.2 %collective-permute-done.6.rest_3_.rest_6_ = bf16[128,512]{1,0:T(8,128)(2,1)S(1)} collective-permute-done((bf16[128,512]{1,0:T(8,128)(2,1)S(1)}, bf16[128,512]{1,0:T(8,128)(2,1)S(1)}, u32[]{:S(2)}, u32[]{:S(2)}) %collective-permute-start.6) | collective-permute-done | bytes 131104 | tf_op jit(solution)/shard_map/ppermute | solution.py:175
  31.1 1.6 %shard_map.80 = (f32[512,768]{1,0:T(8,128)S(1)}, f32[512,512]{1,0:T(8,128)S(1)}, f32[768,512]{1,0:T(8,128)S(1)}) custom-call(bf16[768,512]{1,0:T(8,128)(2,1)S(1)} %get-tuple-element.27.item_ref, bf16[512,512]{1,0:T(8,128)(2,1)S(1)} %get-tuple-element.28.gram_ref, bf16[128,512]{1,0:T(8,128)(2,1)S(1)} %collective-permute-done.3.rest_0_.rest_7_, ...), custom_call_target="tpu_custom_call" | custom-call | flops 53687091200 | bytes 4194304 | tf_op jit(solution)/shard_map/pallas_call | solution.py:239
  32.7 1.3 %shard_map.81 = (f32[128,512]{1,0:T(8,128)S(1)}, bf16[128,512]{1,0:T(8,128)(2,1)S(1)}, bf16[128,512]{1,0:T(8,128)(2,1)S(1)}, f32[128,512]{1,0:T(8,128)S(1)}, f32[768,512]{1,0:T(8,128)S(1)}) custom-call(s32[2,8]{1,0:T(2,128)S(1)} %bitcast.8, bf16[768,512]{1,0:T(8,128)(2,1)S(1)} %get-tuple-element.27.item_ref, f32[512,768]{1,0:T(8,128)S(1)} %get-tuple-element.31.rest_0_, ...), custom_call_target="tpu_custom_call" | custom-call | flops 402653184 | bytes 4194304 | tf_op jit(solution)/shard_map/pallas_call | solution.py:252
  34.1 1.4 %shard_map.83 = (bf16[128,512]{1,0:T(8,128)(2,1)S(1)}, bf16[128,512]{1,0:T(8,128)(2,1)S(1)}, bf16[128,512]{1,0:T(8,128)(2,1)S(1)}, bf16[128,512]{1,0:T(8,128)(2,...) custom-call(s32[2,8]{1,0:T(2,128)S(1)} %bitcast.9, bf16[768,512]{1,0:T(8,128)(2,1)S(1)} %get-tuple-element.27.item_ref, ...), custom_call_target="tpu_custom_call" | custom-call | tf_op jit(solution)/shard_map/pallas_call | solution.py:260
  37.6 1.6 %collective-permute-start.13 = (bf16[128,512]{1,0:T(8,128)(2,1)S(1)}, bf16[128,512]{1,0:T(8,128)(2,1)S(1)}, u32[]{:S(2)}, u32[]{:S(2)}) collective-permute-start(bf16[128,512]{1,0:T(8,128)(2,1)S(1)} %get-tuple-element.46), channel_id=1, source_target_pairs={{0,3},{1,2},{2,1},{3,0},{4,7},{5,6},{6,5},{7,4},{8,11},{9,10},{10,... | collective-permute-start | bytes 393224 | tf_op jit(solution)/shard_map/ppermute | solution.py:175
  39.3 1.5 %collective-permute-start.19 = (bf16[384,512]{1,0:T(8,128)(2,1)S(1)}, bf16[384,512]{1,0:T(8,128)(2,1)S(1)}, u32[]{:S(2)}, u32[]{:S(2)}) collective-permute-start(bf16[384,512]{1,0:T(8,128)(2,1)S(1)} %add_convert_fusion.rest_0_), channel_id=1, source_target_pairs={{0,16},{8,24},{16,0},{24,8},{1,17},{9,25},{17,1},{25,9},{2,18},{10... | collective-permute-start | bytes 1179656 | tf_op jit(solution)/shard_map/ppermute | solution.py:175
  41.9 1.4 %collective-permute-start.15 = (bf16[128,512]{1,0:T(8,128)(2,1)S(1)}, bf16[128,512]{1,0:T(8,128)(2,1)S(1)}, u32[]{:S(2)}, u32[]{:S(2)}) collective-permute-start(bf16[128,512]{1,0:T(8,128)(2,1)S(1)} %get-tuple-element.47), channel_id=1, source_target_pairs={{0,3},{1,2},{2,1},{3,0},{4,7},{5,6},{6,5},{7,4},{8,11},{9,10},{10,... | collective-permute-start | bytes 393224 | tf_op jit(solution)/shard_map/ppermute | solution.py:175
  43.3 1.8 %collective-permute-done.11 = bf16[128,512]{1,0:T(8,128)(2,1)S(1)} collective-permute-done((bf16[128,512]{1,0:T(8,128)(2,1)S(1)}, bf16[128,512]{1,0:T(8,128)(2,1)S(1)}, u32[]{:S(2)}, u32[]{:S(2)}) %collective-permute-start.11) | collective-permute-done | bytes 131104 | tf_op jit(solution)/shard_map/ppermute | solution.py:175
  45.7 2.9 %collective-permute-start.14 = (bf16[128,512]{1,0:T(8,128)(2,1)S(1)}, bf16[128,512]{1,0:T(8,128)(2,1)S(1)}, u32[]{:S(2)}, u32[]{:S(2)}) collective-permute-start(bf16[128,512]{1,0:T(8,128)(2,1)S(1)} %add_convert_fusion.1), channel_id=1, source_target_pairs={{0,6},{1,7},{2,4},{3,5},{4,2},{5,3},{6,0},{7,1},{8,14},{9,15},{10,... | collective-permute-start | bytes 393224 | tf_op jit(solution)/shard_map/ppermute | solution.py:175
  48.6 1.3 %collective-permute-done.19.rest_1_ = bf16[384,512]{1,0:T(8,128)(2,1)S(1)} collective-permute-done((bf16[384,512]{1,0:T(8,128)(2,1)S(1)}, bf16[384,512]{1,0:T(8,128)(2,1)S(1)}, u32[]{:S(2)}, u32[]{:S(2)}) %collective-permute-start.19) | collective-permute-done | bytes 393248 | tf_op jit(solution)/shard_map/ppermute | solution.py:175
  50.2 1.3 %collective-permute-done.16.refs_3_ = bf16[128,512]{1,0:T(8,128)(2,1)S(1)} collective-permute-done((bf16[128,512]{1,0:T(8,128)(2,1)S(1)}, bf16[128,512]{1,0:T(8,128)(2,1)S(1)}, u32[]{:S(2)}, u32[]{:S(2)}) %collective-permute-start.16) | collective-permute-done | bytes 131104 | tf_op jit(solution)/shard_map/ppermute | solution.py:175
  51.5 2.6 %collective-permute-done.14.refs_1_ = bf16[128,512]{1,0:T(8,128)(2,1)S(1)} collective-permute-done((bf16[128,512]{1,0:T(8,128)(2,1)S(1)}, bf16[128,512]{1,0:T(8,128)(2,1)S(1)}, u32[]{:S(2)}, u32[]{:S(2)}) %collective-permute-start.14) | collective-permute-done | bytes 131104 | tf_op jit(solution)/shard_map/ppermute | solution.py:175
  54.3 1.9 %shard_map.85 = (f32[128,512]{1,0:T(8,128)}, f32[768,512]{1,0:T(8,128)}) custom-call(bf16[128,512]{1,0:T(8,128)(2,1)S(1)} %copy-done.1, f32[128,512]{1,0:T(8,128)S(1)} %shard_map.84.total_ref, bf16[768,512]{1,0:T(8,128)(2,1)S(1)} %get-tuple-element.27.item_ref, bf16[384,512]{1,0:T(8,128)(2,1)S(1)} %add_convert_fusion.rest_0_, ...), custom_call_target="tpu_custom_call" | custom-call | bytes 4194304 | tf_op jit(solution)/shard_map/pallas_call | solution.py:289
  (41 shorter events, 9.2 us)
Async XLA Ops:
  0.6 12.9 %collective-permute-start = (bf16[128,512]{1,0:T(8,128)(2,1)}, bf16[128,512]{1,0:T(8,128)(2,1)S(1)}, u32[]{:S(2)}, u32[]{:S(2)}) collective-permute-start(bf16[128,512]{1,0:T(8,128)(2,1)} %user_ref.1), channel_id=1, source_target_pairs={{0,1},{1,0},{2,3},{3,2},{4,5},{5,4},{6,7},{7,6},{8,9},{9,8},{10,11... | collective-permute-start | bytes 393224 | tf_op jit(solution)/shard_map/ppermute | solution.py:175
  3.7 13.9 %collective-permute-start.1 = (bf16[128,512]{1,0:T(8,128)(2,1)}, bf16[128,512]{1,0:T(8,128)(2,1)S(1)}, u32[]{:S(2)}, u32[]{:S(2)}) collective-permute-start(bf16[128,512]{1,0:T(8,128)(2,1)} %user_ref.1), channel_id=1, source_target_pairs={{0,2},{1,3},{2,0},{3,1},{4,6},{5,7},{6,4},{7,5},{8,10},{9,11},{10,... | collective-permute-start | bytes 393224 | tf_op jit(solution)/shard_map/ppermute | solution.py:175
  5.2 12.3 %collective-permute-start.3 = (bf16[128,512]{1,0:T(8,128)(2,1)}, bf16[128,512]{1,0:T(8,128)(2,1)S(1)}, u32[]{:S(2)}, u32[]{:S(2)}) collective-permute-start(bf16[128,512]{1,0:T(8,128)(2,1)} %user_ref.1), channel_id=1, source_target_pairs={{0,4},{1,5},{2,6},{3,7},{4,0},{5,1},{6,2},{7,3},{8,12},{9,13},{10,... | collective-permute-start | bytes 393224 | tf_op jit(solution)/shard_map/ppermute | solution.py:175
  7.8 11.3 %collective-permute-start.2 = (bf16[128,512]{1,0:T(8,128)(2,1)}, bf16[128,512]{1,0:T(8,128)(2,1)S(1)}, u32[]{:S(2)}, u32[]{:S(2)}) collective-permute-start(bf16[128,512]{1,0:T(8,128)(2,1)} %user_ref.1), channel_id=1, source_target_pairs={{0,3},{1,2},{2,1},{3,0},{4,7},{5,6},{6,5},{7,4},{8,11},{9,10},{10,... | collective-permute-start | bytes 393224 | tf_op jit(solution)/shard_map/ppermute | solution.py:175
  10.8 10.3 %copy-start.1 = (bf16[128,512]{1,0:T(8,128)(2,1)S(1)}, bf16[128,512]{1,0:T(8,128)(2,1)}, u32[]{:S(2)}) copy-start(bf16[128,512]{1,0:T(8,128)(2,1)} %user_ref.1) | copy-start | bytes 393220
  11.6 12.4 %collective-permute-start.8 = (s16[512,128]{1,0:T(8,128)(2,1)S(1)}, s16[512,128]{1,0:T(8,128)(2,1)S(1)}, u32[]{:S(2)}, u32[]{:S(2)}) collective-permute-start(s16[512,128]{1,0:T(8,128)(2,1)S(1)} %get-tuple-element.39), channel_id=1, source_target_pairs={{0,4},{1,5},{2,6},{3,7},{4,0},{5,1},{6,2},{7,3},{8,12},{9,13},{10,... | collective-permute-start | bytes 393224 | tf_op jit(solution)/shard_map/ppermute | solution.py:175
  13.5 10.6 %collective-permute-start.9 = (s16[512,128]{1,0:T(8,128)(2,1)S(1)}, s16[512,128]{1,0:T(8,128)(2,1)S(1)}, u32[]{:S(2)}, u32[]{:S(2)}) collective-permute-start(s16[512,128]{1,0:T(8,128)(2,1)S(1)} %get-tuple-element.40), channel_id=1, source_target_pairs={{0,6},{1,7},{2,4},{3,5},{4,2},{5,3},{6,0},{7,1},{8,14},{9,15},{10,... | collective-permute-start | bytes 393224 | tf_op jit(solution)/shard_map/ppermute | solution.py:175
  17.5 8.6 %collective-permute-start.7 = (s16[512,128]{1,0:T(8,128)(2,1)S(1)}, s16[512,128]{1,0:T(8,128)(2,1)S(1)}, u32[]{:S(2)}, u32[]{:S(2)}) collective-permute-start(s16[512,128]{1,0:T(8,128)(2,1)S(1)} %get-tuple-element.38), channel_id=1, source_target_pairs={{0,2},{1,3},{2,0},{3,1},{4,6},{5,7},{6,4},{7,5},{8,10},{9,11},{10,... | collective-permute-start | bytes 393224 | tf_op jit(solution)/shard_map/ppermute | solution.py:175
  17.5 9.9 %collective-permute-start.4 = (bf16[128,512]{1,0:T(8,128)(2,1)S(1)}, bf16[128,512]{1,0:T(8,128)(2,1)S(1)}, u32[]{:S(2)}, u32[]{:S(2)}) collective-permute-start(bf16[128,512]{1,0:T(8,128)(2,1)S(1)} %collective-permute-done.3.rest_0_.rest_7_), channel_id=1, source_target_pairs={{0,1},{1,0},{2,3},{3,2},{4,5},{5,4},{6,7},{7,6},{8,9},{9,8},{10,11... | collective-permute-start | bytes 393224 | tf_op jit(solution)/shard_map/ppermute | solution.py:175
  19.1 9.8 %collective-permute-start.5 = (bf16[128,512]{1,0:T(8,128)(2,1)S(1)}, bf16[128,512]{1,0:T(8,128)(2,1)S(1)}, u32[]{:S(2)}, u32[]{:S(2)}) collective-permute-start(bf16[128,512]{1,0:T(8,128)(2,1)S(1)} %collective-permute-done.3.rest_0_.rest_7_), channel_id=1, source_target_pairs={{0,2},{1,3},{2,0},{3,1},{4,6},{5,7},{6,4},{7,5},{8,10},{9,11},{10,... | collective-permute-start | bytes 393224 | tf_op jit(solution)/shard_map/ppermute | solution.py:175
  24.1 7.0 %collective-permute-start.6 = (bf16[128,512]{1,0:T(8,128)(2,1)S(1)}, bf16[128,512]{1,0:T(8,128)(2,1)S(1)}, u32[]{:S(2)}, u32[]{:S(2)}) collective-permute-start(bf16[128,512]{1,0:T(8,128)(2,1)S(1)} %collective-permute-done.3.rest_0_.rest_7_), channel_id=1, source_target_pairs={{0,3},{1,2},{2,1},{3,0},{4,7},{5,6},{6,5},{7,4},{8,11},{9,10},{10,... | collective-permute-start | bytes 393224 | tf_op jit(solution)/shard_map/ppermute | solution.py:175
  26.1 8.0 %collective-permute-start.10 = (s16[1024,128]{1,0:T(8,128)(2,1)S(1)}, s16[1024,128]{1,0:T(8,128)(2,1)S(1)}, u32[]{:S(2)}, u32[]{:S(2)}) collective-permute-start(s16[1024,128]{1,0:T(8,128)(2,1)S(1)} %shard_map.82), channel_id=1, source_target_pairs={{0,1},{1,0},{2,3},{3,2},{4,5},{5,4},{6,7},{7,6},{8,9},{9,8},{10,11... | collective-permute-start | bytes 786440 | tf_op jit(solution)/shard_map/ppermute | solution.py:175
  31.1 1.7 %copy-start.2 = (s32[1,8,2]{1,2,0:T(2,128)S(1)}, s32[1,8,2]{1,2,0:T(2,128)}, u32[]{:S(2)}) copy-start(s32[1,8,2]{1,2,0:T(2,128)} %param.10) | copy-start | bytes 196
  35.5 3.6 %collective-permute-start.18 = (bf16[384,512]{1,0:T(8,128)(2,1)S(1)}, bf16[384,512]{1,0:T(8,128)(2,1)S(1)}, u32[]{:S(2)}, u32[]{:S(2)}) collective-permute-start(bf16[384,512]{1,0:T(8,128)(2,1)S(1)} %get-tuple-element.51), channel_id=1, source_target_pairs={{0,8},{8,0},{16,24},{24,16},{1,9},{9,1},{17,25},{25,17},{2,10},{10... | collective-permute-start | bytes 1179656 | tf_op jit(solution)/shard_map/ppermute | solution.py:175
  35.6 6.4 %collective-permute-start.12 = (bf16[128,512]{1,0:T(8,128)(2,1)S(1)}, bf16[128,512]{1,0:T(8,128)(2,1)S(1)}, u32[]{:S(2)}, u32[]{:S(2)}) collective-permute-start(bf16[128,512]{1,0:T(8,128)(2,1)S(1)} %get-tuple-element.45), channel_id=1, source_target_pairs={{0,2},{1,3},{2,0},{3,1},{4,6},{5,7},{6,4},{7,5},{8,10},{9,11},{10,... | collective-permute-start | bytes 393224 | tf_op jit(solution)/shard_map/ppermute | solution.py:175
  36.7 8.5 %collective-permute-start.11 = (bf16[128,512]{1,0:T(8,128)(2,1)S(1)}, bf16[128,512]{1,0:T(8,128)(2,1)S(1)}, u32[]{:S(2)}, u32[]{:S(2)}) collective-permute-start(bf16[128,512]{1,0:T(8,128)(2,1)S(1)} %get-tuple-element.44), channel_id=1, source_target_pairs={{0,1},{1,0},{2,3},{3,2},{4,5},{5,4},{6,7},{7,6},{8,9},{9,8},{10,11... | collective-permute-start | bytes 393224 | tf_op jit(solution)/shard_map/ppermute | solution.py:175
  37.6 8.1 %collective-permute-start.13 = (bf16[128,512]{1,0:T(8,128)(2,1)S(1)}, bf16[128,512]{1,0:T(8,128)(2,1)S(1)}, u32[]{:S(2)}, u32[]{:S(2)}) collective-permute-start(bf16[128,512]{1,0:T(8,128)(2,1)S(1)} %get-tuple-element.46), channel_id=1, source_target_pairs={{0,3},{1,2},{2,1},{3,0},{4,7},{5,6},{6,5},{7,4},{8,11},{9,10},{10,... | collective-permute-start | bytes 393224 | tf_op jit(solution)/shard_map/ppermute | solution.py:175
  39.3 10.7 %collective-permute-start.19 = (bf16[384,512]{1,0:T(8,128)(2,1)S(1)}, bf16[384,512]{1,0:T(8,128)(2,1)S(1)}, u32[]{:S(2)}, u32[]{:S(2)}) collective-permute-start(bf16[384,512]{1,0:T(8,128)(2,1)S(1)} %add_convert_fusion.rest_0_), channel_id=1, source_target_pairs={{0,16},{8,24},{16,0},{24,8},{1,17},{9,25},{17,1},{25,9},{2,18},{10... | collective-permute-start | bytes 1179656 | tf_op jit(solution)/shard_map/ppermute | solution.py:175
  40.8 7.8 %collective-permute-start.17 = (bf16[128,512]{1,0:T(8,128)(2,1)S(1)}, bf16[128,512]{1,0:T(8,128)(2,1)S(1)}, u32[]{:S(2)}, u32[]{:S(2)}) collective-permute-start(bf16[128,512]{1,0:T(8,128)(2,1)S(1)} %get-tuple-element.49), channel_id=1, source_target_pairs={{0,2},{1,3},{2,0},{3,1},{4,6},{5,7},{6,4},{7,5},{8,10},{9,11},{10,... | collective-permute-start | bytes 393224 | tf_op jit(solution)/shard_map/ppermute | solution.py:175
  41.9 8.3 %collective-permute-start.15 = (bf16[128,512]{1,0:T(8,128)(2,1)S(1)}, bf16[128,512]{1,0:T(8,128)(2,1)S(1)}, u32[]{:S(2)}, u32[]{:S(2)}) collective-permute-start(bf16[128,512]{1,0:T(8,128)(2,1)S(1)} %get-tuple-element.47), channel_id=1, source_target_pairs={{0,3},{1,2},{2,1},{3,0},{4,7},{5,6},{6,5},{7,4},{8,11},{9,10},{10,... | collective-permute-start | bytes 393224 | tf_op jit(solution)/shard_map/ppermute | solution.py:175
  45.1 6.4 %collective-permute-start.16 = (bf16[128,512]{1,0:T(8,128)(2,1)S(1)}, bf16[128,512]{1,0:T(8,128)(2,1)S(1)}, u32[]{:S(2)}, u32[]{:S(2)}) collective-permute-start(bf16[128,512]{1,0:T(8,128)(2,1)S(1)} %get-tuple-element.48), channel_id=1, source_target_pairs={{0,1},{1,0},{2,3},{3,2},{4,5},{5,4},{6,7},{7,6},{8,9},{9,8},{10,11... | collective-permute-start | bytes 393224 | tf_op jit(solution)/shard_map/ppermute | solution.py:175
  45.7 8.5 %collective-permute-start.14 = (bf16[128,512]{1,0:T(8,128)(2,1)S(1)}, bf16[128,512]{1,0:T(8,128)(2,1)S(1)}, u32[]{:S(2)}, u32[]{:S(2)}) collective-permute-start(bf16[128,512]{1,0:T(8,128)(2,1)S(1)} %add_convert_fusion.1), channel_id=1, source_target_pairs={{0,6},{1,7},{2,4},{3,5},{4,2},{5,3},{6,0},{7,1},{8,14},{9,15},{10,... | collective-permute-start | bytes 393224 | tf_op jit(solution)/shard_map/ppermute | solution.py:175
  48.6 5.6 %collective-permute-start.20 = (bf16[384,512]{1,0:T(8,128)(2,1)S(1)}, bf16[384,512]{1,0:T(8,128)(2,1)S(1)}, u32[]{:S(2)}, u32[]{:S(2)}) collective-permute-start(bf16[384,512]{1,0:T(8,128)(2,1)S(1)} %add_convert_fusion.rest_0_), channel_id=1, source_target_pairs={{0,8},{8,0},{16,24},{24,16},{1,9},{9,1},{17,25},{25,17},{2,10},{10... | collective-permute-start | bytes 1179656 | tf_op jit(solution)/shard_map/ppermute | solution.py:175
  50.0 4.3 %collective-permute-start.21 = (bf16[384,512]{1,0:T(8,128)(2,1)S(1)}, bf16[384,512]{1,0:T(8,128)(2,1)S(1)}, u32[]{:S(2)}, u32[]{:S(2)}) collective-permute-start(bf16[384,512]{1,0:T(8,128)(2,1)S(1)} %collective-permute-done.19.rest_1_), channel_id=1, source_target_pairs={{0,8},{8,0},{16,24},{24,16},{1,9},{9,1},{17,25},{25,17},{2,10},{10... | collective-permute-start | bytes 1179656 | tf_op jit(solution)/shard_map/ppermute | solution.py:175
  (3 other events, 3.0 us)
